TPU v7x, 32 devices: a whole 2x2x4 slice. The times are simulated.
32 devices in a mesh: res: 8 (over z, x), nbr: 4 (over y, core).
Axes of the slice: x: 2, y: 2, z: 4, core: 2. Of those that a mesh axis runs over, the one named last changes fastest.
Arguments:
- nodes: bfloat16 [1536, 512], P('res'), may hold values from -6 to 6
- edges: bfloat16 [1536, 60, 192], P('res', 'nbr'), may hold values from -6 to 6
- neighbours: int32 [1536, 60], P('res', 'nbr'), may hold values from 0 to 1535, as said below
- residue_mask: int32 [1536], P('res'), may hold values from 0 to 1, as said below
- msg_w1: bfloat16 [1216, 512], replicated, may hold values from -0.15625 to 0.15625
- msg_b1: bfloat16 [512], replicated, may hold values from -1.5 to 1.5
- msg_w2: bfloat16 [512, 512], replicated, may hold values from -0.25 to 0.25
- msg_b2: bfloat16 [512], replicated, may hold values from -1.5 to 1.5
- msg_w3: bfloat16 [512, 512], replicated, may hold values from -0.5 to 0.5
- msg_b3: bfloat16 [512], replicated, may hold values from -1.5 to 1.5
- norm1_gain: bfloat16 [512], replicated, may hold values from 0.25 to 1.75
- norm1_bias: bfloat16 [512], replicated, may hold values from -1.5 to 1.5
- ffn_w1: bfloat16 [512, 2048], replicated, may hold values from -0.25 to 0.25
- ffn_b1: bfloat16 [2048], replicated, may hold values from -1.5 to 1.5
- ffn_w2: bfloat16 [2048, 512], replicated, may hold values from -0.125 to 0.125
- ffn_b2: bfloat16 [512], replicated, may hold values from -1.5 to 1.5
- norm2_gain: bfloat16 [512], replicated, may hold values from 0.25 to 1.75
- norm2_bias: bfloat16 [512], replicated, may hold values from -1.5 to 1.5
- edge_w1: bfloat16 [1216, 192], replicated, may hold values from -0.15625 to 0.15625
- edge_b1: bfloat16 [192], replicated, may hold values from -1.5 to 1.5
- edge_w2: bfloat16 [192, 192], replicated, may hold values from -0.4375 to 0.4375
- edge_b2: bfloat16 [192], replicated, may hold values from -1.5 to 1.5
- edge_w3: bfloat16 [192, 192], replicated, may hold values from -0.4375 to 0.4375
- edge_b3: bfloat16 [192], replicated, may hold values from -1.5 to 1.5
- norm3_gain: bfloat16 [192], replicated, may hold values from 0.25 to 1.75
- norm3_bias: bfloat16 [192], replicated, may hold values from -1.5 to 1.5
- node_cot: bfloat16 [1536, 512], P('res'), may hold values from -6 to 6
- edge_cot: bfloat16 [1536, 60, 192], P('res', 'nbr'), may hold values from -6 to 6
Outputs:
- nodes_out: bfloat16 [1536, 512], P('res')
- edges_out: bfloat16 [1536, 60, 192], P('res', 'nbr')
- nodes_grad: float32 [1536, 512], P('res')
- edges_grad: float32 [1536, 60, 192], P('res', 'nbr')
- msg_w1_grad: float32 [1216, 512], P('nbr')
- msg_b1_grad: float32 [512], P('nbr')
- msg_w2_grad: float32 [512, 512], P('nbr')
- msg_b2_grad: float32 [512], P('nbr')
- msg_w3_grad: float32 [512, 512], P('nbr')
- msg_b3_grad: float32 [512], P('nbr')
- norm1_gain_grad: float32 [512], P('nbr')
- norm1_bias_grad: float32 [512], P('nbr')
- ffn_w1_grad: float32 [512, 2048], P('nbr')
- ffn_b1_grad: float32 [2048], P('nbr')
- ffn_w2_grad: float32 [2048, 512], P('nbr')
- ffn_b2_grad: float32 [512], P('nbr')
- norm2_gain_grad: float32 [512], P('nbr')
- norm2_bias_grad: float32 [512], P('nbr')
- edge_w1_grad: float32 [1216, 192], P('nbr')
- edge_b1_grad: float32 [192], P('nbr')
- edge_w2_grad: float32 [192, 192], P('nbr')
- edge_b2_grad: float32 [192], P('nbr')
- edge_w3_grad: float32 [192, 192], P('nbr')
- edge_b3_grad: float32 [192], P('nbr')
- norm3_gain_grad: float32 [192], P('nbr')
- norm3_bias_grad: float32 [192], P('nbr')
Inputs may be any that keep to these rules, and one draw needn't show every extreme that they name: `residue_mask`: within each block of 192 slots (one index of res) the real residues (1) come first and fill a quarter of the slots or more; some block is all real. `neighbours`: column 0 of each row names the slot itself. Every other entry names either a slot of the row's own block of 192 slots within 24 positions of it, or a real residue of any block. The rows of one block name at most 32 distinct slots of any other block, and in every draw some block names exactly 32 slots of some other block in column 1.
All inputs are finite; a program needn't handle non-finite values.
Results may differ from a plain program's by a relative error of at most 0.017.
Values may be sent and summed in bfloat16 or wider, within the bound.
No kernel may reach another device: no remote copies, remote signals or barrier semaphores. Data moves between devices by JAX's collectives and lax.ppermute only.
A program may use at most 192 MiB of HBM per device.

v0:
```python
import jax
import jax.numpy as jnp
from jax import lax
from jax.sharding import PartitionSpec as P

D = 512
E = 192


precise = lax.Precision.HIGHEST


def matmul(former, latter, accuracy=None):
    return jnp.dot(former, latter, preferred_element_type=jnp.float32, precision=accuracy)


def outer_sum(former, latter, accuracy=None):
    return lax.dot_general(
        former,
        latter,
        (((0,), (0,)), ((), ())),
        preferred_element_type=jnp.float32,
        precision=accuracy,
    )


def back_dot(former, latter, accuracy=None):
    return lax.dot_general(
        former,
        latter,
        (((1,), (1,)), ((), ())),
        preferred_element_type=jnp.float32,
        precision=accuracy,
    )


def gelu_back(before, upstream):
    return jax.vjp(jax.nn.gelu, before)[1](upstream)[0]


def norm_forward(values, scale_row, offset_row):
    centre = jnp.mean(values, axis=-1, keepdims=True)
    centred = values - centre
    inverse = lax.rsqrt(jnp.mean(centred * centred, axis=-1, keepdims=True) + 1e-05)
    normed = centred * inverse
    return (normed * scale_row + offset_row, normed, inverse)


def norm_backward(upstream, normed, inverse, scale_row):
    scaled = upstream * scale_row
    first_mean = jnp.mean(scaled, axis=-1, keepdims=True)
    second_mean = jnp.mean(scaled * normed, axis=-1, keepdims=True)
    return inverse * (scaled - first_mean - normed * second_mean)


def row_picker(index_flat):

    def collect(holder, portion, first_row):
        span_rows = portion.shape[0]
        inside = (index_flat >= 0) & (index_flat < span_rows)
        clipped = jnp.clip(index_flat, 0, span_rows - 1)
        shaped = inside.reshape((-1,) + (1,) * (portion.ndim - 1))
        return jnp.where(shaped, jnp.take(portion, clipped, axis=0), holder)

    return collect


def row_spreader(values, index_flat, span_rows):
    inside = (index_flat >= 0) & (index_flat < span_rows)
    clipped = jnp.clip(index_flat, 0, span_rows - 1)
    kept_rows = jnp.where(inside[:, None], values, 0.0)
    return jax.ops.segment_sum(kept_rows, clipped, num_segments=span_rows)


def as_float(values):
    return values.astype(jnp.float32)


def on_device(
    nodes,
    edges,
    neighbours,
    residue_mask,
    msg_w1,
    msg_b1,
    msg_w2,
    msg_b2,
    msg_w3,
    msg_b3,
    norm1_gain,
    norm1_bias,
    ffn_w1,
    ffn_b1,
    ffn_w2,
    ffn_b2,
    norm2_gain,
    norm2_bias,
    edge_w1,
    edge_b1,
    edge_w2,
    edge_b2,
    edge_w3,
    edge_b3,
    norm3_gain,
    norm3_bias,
    node_cot,
    edge_cot,
):
    node_rows, near_count = neighbours.shape
    edge_total = node_rows * near_count
    edge_flat = edges.reshape(edge_total, E)
    index_flat = neighbours.reshape(edge_total)
    present = residue_mask.astype(jnp.float32)
    picker = row_picker(index_flat)
    first_row = jnp.int32(0)
    near_nodes = picker(
        jnp.zeros((edge_total, D), jnp.bfloat16),
        lax.all_gather(nodes, "res", axis=0, tiled=True),
        first_row,
    )
    near_flag = picker(
        jnp.zeros((edge_total,), jnp.bfloat16),
        lax.all_gather(present.astype(jnp.bfloat16), "res", axis=0, tiled=True),
        first_row,
    )
    edge_mask = present[:, None] * as_float(near_flag).reshape(node_rows, near_count)
    edge_weight = edge_mask.reshape(edge_total)
    own_first = matmul(nodes, msg_w1[:D])
    edge_first = (
        matmul(near_nodes, msg_w1[D : 2 * D])
        + matmul(edge_flat, msg_w1[2 * D :])
        + as_float(msg_b1)
    )
    message_pre1 = (own_first[:, None, :] + edge_first.reshape(node_rows, near_count, D)).reshape(
        edge_total, D
    )
    message_act1 = jax.nn.gelu(message_pre1).astype(jnp.bfloat16)
    message_pre2 = matmul(message_act1, msg_w2) + as_float(msg_b2)
    message_act2 = jax.nn.gelu(message_pre2).astype(jnp.bfloat16)
    message = matmul(message_act2, msg_w3) + as_float(msg_b3)
    weighted = jnp.sum((edge_weight[:, None] * message).reshape(node_rows, near_count, D), axis=1)
    summed, totals = lax.psum((weighted, jnp.sum(edge_mask, axis=1)), "nbr")
    floored = jnp.maximum(totals, 1.0)
    mixed_sum = as_float(nodes) + summed / floored[:, None]
    first_norm, normed_one, inverse_one = norm_forward(
        mixed_sum, as_float(norm1_gain), as_float(norm1_bias)
    )
    first_low = first_norm.astype(jnp.bfloat16)
    hidden_pre = matmul(first_low, ffn_w1) + as_float(ffn_b1)
    hidden_act = jax.nn.gelu(hidden_pre).astype(jnp.bfloat16)
    branch = matmul(hidden_act, ffn_w2) + as_float(ffn_b2)
    second_norm, normed_two, inverse_two = norm_forward(
        first_norm + branch, as_float(norm2_gain), as_float(norm2_bias)
    )
    sent_low = (present[:, None] * second_norm).astype(jnp.bfloat16)
    near_sent = picker(
        jnp.zeros((edge_total, D), jnp.bfloat16),
        lax.all_gather(sent_low, "res", axis=0, tiled=True),
        jnp.int32(0),
    )
    near_term = matmul(near_sent, edge_w1[D : 2 * D])
    own_edge = matmul(sent_low, edge_w1[:D])
    edge_rest = near_term + matmul(edge_flat, edge_w1[2 * D :]) + as_float(edge_b1)
    edge_pre1 = (own_edge[:, None, :] + edge_rest.reshape(node_rows, near_count, E)).reshape(
        edge_total, E
    )
    edge_act1 = jax.nn.gelu(edge_pre1).astype(jnp.bfloat16)
    edge_pre2 = matmul(edge_act1, edge_w2) + as_float(edge_b2)
    edge_act2 = jax.nn.gelu(edge_pre2).astype(jnp.bfloat16)
    edge_branch = matmul(edge_act2, edge_w3) + as_float(edge_b3)
    edge_normout, edge_normed, edge_inverse = norm_forward(
        as_float(edge_flat) + edge_branch, as_float(norm3_gain), as_float(norm3_bias)
    )
    edges_out = (
        (edge_weight[:, None] * edge_normout).astype(jnp.bfloat16).reshape(node_rows, near_count, E)
    )
    edge_up = edge_weight[:, None] * as_float(edge_cot.reshape(edge_total, E))
    norm3_gain_grad = jnp.sum(edge_up * edge_normed, axis=0)
    norm3_bias_grad = jnp.sum(edge_up, axis=0)
    edge_sum_grad = norm_backward(edge_up, edge_normed, edge_inverse, as_float(norm3_gain))
    edge_branch_low = edge_sum_grad.astype(jnp.bfloat16)
    edge_w3_grad = outer_sum(edge_act2, edge_branch_low)
    edge_b3_grad = jnp.sum(as_float(edge_branch_low), axis=0)
    edge_low2 = gelu_back(edge_pre2, back_dot(edge_branch_low, edge_w3)).astype(jnp.bfloat16)
    edge_w2_grad = outer_sum(edge_act1, edge_low2)
    edge_b2_grad = jnp.sum(as_float(edge_low2), axis=0)
    edge_low1 = gelu_back(edge_pre1, back_dot(edge_low2, edge_w2)).astype(jnp.bfloat16)
    edge_b1_grad = jnp.sum(as_float(edge_low1), axis=0)
    edge_node_sum = jnp.sum(as_float(edge_low1).reshape(node_rows, near_count, E), axis=1)
    own_edge_grad = outer_sum(as_float(sent_low), edge_node_sum, precise)
    flat_edge_grad = outer_sum(edge_flat, edge_low1)
    node_back = back_dot(edge_node_sum, as_float(edge_w1[:D]), precise)
    edges_back = edge_sum_grad + back_dot(edge_low1, edge_w1[2 * D :])
    near_values = back_dot(edge_low1, edge_w1[D : 2 * D])
    returned = lax.psum_scatter(
        row_spreader(near_values, index_flat, lax.axis_size("res") * node_rows),
        "res",
        scatter_dimension=0,
        tiled=True,
    )
    near_edge_grad = outer_sum(near_sent, edge_low1)
    node_back = node_back + returned
    edge_w1_grad = jnp.concatenate([own_edge_grad, near_edge_grad, flat_edge_grad], axis=0)
    updated_grad = as_float(node_cot) + lax.psum(node_back, "nbr")
    upstream_two = present[:, None] * updated_grad
    sum_grad = norm_backward(upstream_two, normed_two, inverse_two, as_float(norm2_gain))
    branch_grad = sum_grad.astype(jnp.bfloat16)
    hidden_grad = gelu_back(hidden_pre, back_dot(branch_grad, ffn_w2)).astype(jnp.bfloat16)
    first_grad = sum_grad + back_dot(hidden_grad, ffn_w1)
    mixed_grad = norm_backward(first_grad, normed_one, inverse_one, as_float(norm1_gain))
    quarter = node_rows // lax.axis_size("nbr")
    first_share = lax.axis_index("nbr") * quarter

    def share(values):
        return lax.dynamic_slice_in_dim(values, first_share, quarter, 0)

    norm2_gain_grad = jnp.sum(share(upstream_two * normed_two), axis=0)
    norm2_bias_grad = jnp.sum(share(upstream_two), axis=0)
    ffn_w2_grad = outer_sum(share(hidden_act), share(branch_grad))
    ffn_b2_grad = jnp.sum(as_float(share(branch_grad)), axis=0)
    ffn_w1_grad = outer_sum(share(first_low), share(hidden_grad))
    ffn_b1_grad = jnp.sum(as_float(share(hidden_grad)), axis=0)
    norm1_gain_grad = jnp.sum(share(first_grad * normed_one), axis=0)
    norm1_bias_grad = jnp.sum(share(first_grad), axis=0)
    message_grad = (
        (edge_mask[:, :, None] * (mixed_grad / floored[:, None])[:, None, :])
        .reshape(edge_total, D)
        .astype(jnp.bfloat16)
    )
    msg_w3_grad = outer_sum(message_act2, message_grad)
    msg_b3_grad = jnp.sum(as_float(message_grad), axis=0)
    message_low2 = gelu_back(message_pre2, back_dot(message_grad, msg_w3)).astype(jnp.bfloat16)
    msg_w2_grad = outer_sum(message_act1, message_low2)
    msg_b2_grad = jnp.sum(as_float(message_low2), axis=0)
    message_low1 = gelu_back(message_pre1, back_dot(message_low2, msg_w2)).astype(jnp.bfloat16)
    msg_b1_grad = jnp.sum(as_float(message_low1), axis=0)
    message_node_sum = jnp.sum(as_float(message_low1).reshape(node_rows, near_count, D), axis=1)
    msg_w1_grad = jnp.concatenate(
        [
            outer_sum(as_float(nodes), message_node_sum, precise),
            outer_sum(near_nodes, message_low1),
            outer_sum(edge_flat, message_low1),
        ],
        axis=0,
    )
    near_message_back = back_dot(message_low1, msg_w1[D : 2 * D])
    input_back = back_dot(message_node_sum, as_float(msg_w1[:D]), precise)
    input_back = input_back + lax.psum_scatter(
        row_spreader(near_message_back, index_flat, lax.axis_size("res") * node_rows),
        "res",
        scatter_dimension=0,
        tiled=True,
    )
    nodes_grad = mixed_grad + lax.psum(input_back.astype(jnp.bfloat16), "nbr").astype(jnp.float32)
    edges_grad = (edges_back + back_dot(message_low1, msg_w1[2 * D :])).reshape(
        node_rows, near_count, E
    )
    shares = (
        lax.psum_scatter(msg_w1_grad, "nbr", scatter_dimension=0, tiled=True),
        lax.psum_scatter(msg_b1_grad, "nbr", scatter_dimension=0, tiled=True),
        lax.psum_scatter(msg_w2_grad, "nbr", scatter_dimension=0, tiled=True),
        lax.psum_scatter(msg_b2_grad, "nbr", scatter_dimension=0, tiled=True),
        lax.psum_scatter(msg_w3_grad, "nbr", scatter_dimension=0, tiled=True),
        lax.psum_scatter(msg_b3_grad, "nbr", scatter_dimension=0, tiled=True),
        lax.psum_scatter(norm1_gain_grad, "nbr", scatter_dimension=0, tiled=True),
        lax.psum_scatter(norm1_bias_grad, "nbr", scatter_dimension=0, tiled=True),
        lax.psum_scatter(ffn_w1_grad, "nbr", scatter_dimension=0, tiled=True),
        lax.psum_scatter(ffn_b1_grad, "nbr", scatter_dimension=0, tiled=True),
        lax.psum_scatter(ffn_w2_grad, "nbr", scatter_dimension=0, tiled=True),
        lax.psum_scatter(ffn_b2_grad, "nbr", scatter_dimension=0, tiled=True),
        lax.psum_scatter(norm2_gain_grad, "nbr", scatter_dimension=0, tiled=True),
        lax.psum_scatter(norm2_bias_grad, "nbr", scatter_dimension=0, tiled=True),
        lax.psum_scatter(edge_w1_grad, "nbr", scatter_dimension=0, tiled=True),
        lax.psum_scatter(edge_b1_grad, "nbr", scatter_dimension=0, tiled=True),
        lax.psum_scatter(edge_w2_grad, "nbr", scatter_dimension=0, tiled=True),
        lax.psum_scatter(edge_b2_grad, "nbr", scatter_dimension=0, tiled=True),
        lax.psum_scatter(edge_w3_grad, "nbr", scatter_dimension=0, tiled=True),
        lax.psum_scatter(edge_b3_grad, "nbr", scatter_dimension=0, tiled=True),
        lax.psum_scatter(norm3_gain_grad, "nbr", scatter_dimension=0, tiled=True),
        lax.psum_scatter(norm3_bias_grad, "nbr", scatter_dimension=0, tiled=True),
    )
    weight_sums = lax.psum(tuple(shares), "res")
    return (sent_low, edges_out, nodes_grad, edges_grad) + tuple(weight_sums)


def solution(mesh):
    in_specs = (
        P("res", None),
        P("res", "nbr", None),
        P("res", "nbr"),
        P("res"),
        P(),
        P(),
        P(),
        P(),
        P(),
        P(),
        P(),
        P(),
        P(),
        P(),
        P(),
        P(),
        P(),
        P(),
        P(),
        P(),
        P(),
        P(),
        P(),
        P(),
        P(),
        P(),
        P("res", None),
        P("res", "nbr", None),
    )
    out_specs = (
        P("res", None),
        P("res", "nbr", None),
        P("res", None),
        P("res", "nbr", None),
        P("nbr", None),
        P("nbr"),
        P("nbr", None),
        P("nbr"),
        P("nbr", None),
        P("nbr"),
        P("nbr"),
        P("nbr"),
        P("nbr", None),
        P("nbr"),
        P("nbr", None),
        P("nbr"),
        P("nbr"),
        P("nbr"),
        P("nbr", None),
        P("nbr"),
        P("nbr", None),
        P("nbr"),
        P("nbr", None),
        P("nbr"),
        P("nbr"),
        P("nbr"),
    )
    return jax.shard_map(
        on_device, mesh=mesh, in_specs=in_specs, out_specs=out_specs, check_vma=False
    )
```

profile of v0, /device:TPU:0, one launch (start us, length us, event | category | flops | bytes accessed | tf_op | source)
XLA Modules:
  0.0 1065.5 jit_solution(6921387328409336553)
XLA Ops:
  19.2 23.2 %all-reduce = bf16[1536]{0:T(1024)(128)(2,1)S(1)} all-reduce(bf16[1536]{0:T(1024)(128)(2,1)S(1)} %dynamic-update-slice), channel_id=1, replica_groups=mesh['res'=8,'nbr'=4] {'res'}, use_global_device_ids=true, to_apply=%add | all-reduce | flops 1536 | bytes 6144
  42.5 17.3 %gather_fusion = bf16[2880]{0:T(1024)(128)(2,1)S(1)} fusion(bf16[1536]{0:T(1024)(128)(2,1)S(1)} %all-reduce, s32[3072]{0:T(1024)S(1)} %pad_clamp_fusion.1), kind=kCustom, calls=%fused_computation.2 | custom fusion | bytes 23040 | tf_op jit(solution)/shard_map/jit(_take)/gather | solution.py:63
  85.3 11.3 %gather_fusion.1 = bf16[2880,512]{1,0:T(8,128)(2,1)} fusion(bf16[1536,512]{1,0:T(8,128)(2,1)} %all-gather.3.cloned.1.call-done, s32[3072]{0:T(1024)S(1)} %pad_clamp_fusion), kind=kCustom, calls=%fused_computation.clone | custom fusion | bytes 5909760 | tf_op jit(solution)/shard_map/jit(_take)/gather | solution.py:63
  127.4 30.2 %all-reduce.24.cloned.1.call-done = f32[192,512]{1,0:T(8,128)} async-done(((f32[192,512]{1,0:T(8,128)}), f32[192,512]{1,0:T(8,128)}) %all-reduce.24.cloned.1.call-update) | async-done | bytes 393232 | tf_op jit(solution)/shard_map/psum | solution.py:142
  189.2 18.4 %all-gather.5.cloned.1.call-done = bf16[1536,512]{1,0:T(8,128)(2,1)} async-done(((bf16[192,512]{1,0:T(8,128)(2,1)}), bf16[1536,512]{1,0:T(8,128)(2,1)}) %all-gather.5.cloned.1.call-update) | async-done | bytes 1572880 | tf_op jit(solution)/shard_map/all_gather | solution.py:158
  207.6 11.3 %gather_fusion.2 = bf16[2880,512]{1,0:T(8,128)(2,1)} fusion(bf16[1536,512]{1,0:T(8,128)(2,1)} %all-gather.5.cloned.1.call-done, s32[3072]{0:T(1024)S(1)} %pad_clamp_fusion), kind=kCustom, calls=%fused_computation.1.clone | custom fusion | bytes 5909760 | tf_op jit(solution)/shard_map/jit(_take)/gather | solution.py:63
  243.3 23.2 %scatter_custom_fusion = f32[1536,512]{1,0:T(8,128)} fusion(s32[2880]{0:T(1024)S(1)} %min.23, f32[2880,512]{1,0:T(8,128)} %fusion.60, f32[]{:T(128)} %constant.37.clone.1, pred[2880]{0:T(1024)(128)(4,1)} %copy-done.44), kind=kCustom, calls=%fused_computation.29 | custom fusion | flops 2949120 | bytes 9048064 | tf_op jit(solution)/shard_map/scatter-add | solution.py:72
  276.0 63.7 %reduce-scatter.13.cloned.1.call-done = f32[192,512]{1,0:T(8,128)} async-done(((f32[1536,512]{1,0:T(8,128)}), f32[192,512]{1,0:T(8,128)}) %reduce-scatter.13.cloned.1.call-update) | async-done | bytes 393232 | tf_op jit(solution)/shard_map/reduce_scatter | solution.py:195
  342.0 32.3 %all-reduce.26.cloned.1.call-done = f32[192,512]{1,0:T(8,128)} async-done(((f32[192,512]{1,0:T(8,128)}), f32[192,512]{1,0:T(8,128)}) %all-reduce.26.cloned.1.call-update) | async-done | bytes 393232 | tf_op jit(solution)/shard_map/psum | solution.py:204
  392.9 8.9 convert_reduce_fusion.1
  401.9 8.3 convert_reduce_fusion.4
  417.1 26.6 %scatter_custom_fusion.1 = f32[1536,512]{1,0:T(8,128)} fusion(s32[2880]{0:T(1024)S(1)} %min.23, f32[2880,512]{1,0:T(8,128)} %fusion.50, f32[]{:T(128)} %constant.37.clone.1, pred[2880]{0:T(1024)(128)(4,1)S(1)} %copy-done.45), kind=kCustom, calls=%fused_computation.26 | custom fusion | flops 2949120 | bytes 9048064 | tf_op jit(solution)/shard_map/scatter-add | solution.py:72
  508.5 10.0 reduce-scatter.15.cloned.1.call-done
  524.9 10.4 all-reduce.17
  543.5 18.5 %reduce-scatter.27.cloned.1.call-done = f32[48,192]{1,0:T(8,128)} async-done(((f32[192,192]{1,0:T(8,128)}), f32[48,192]{1,0:T(8,128)}) %reduce-scatter.27.cloned.1.call-update) | async-done | bytes 36880 | tf_op jit(solution)/shard_map/reduce_scatter | solution.py:275
  562.4 29.0 %reduce-scatter.31.cloned.1.call-done = f32[304,192]{1,0:T(8,128)} async-done(((f32[1216,192]{1,0:T(8,128)}), f32[304,192]{1,0:T(8,128)}) %reduce-scatter.31.cloned.1.call-update) | async-done | bytes 233488
  593.2 26.2 %reduce-scatter.21.cloned.1.call-done = f32[128,512]{1,0:T(8,128)} async-done(((f32[512,512]{1,0:T(8,128)}), f32[128,512]{1,0:T(8,128)}) %reduce-scatter.21.cloned.1.call-update) | async-done | bytes 262160 | tf_op jit(solution)/shard_map/reduce_scatter | solution.py:263
  619.4 28.0 %reduce-scatter.19.cloned.1.call-done = f32[128,512]{1,0:T(8,128)} async-done(((f32[512,512]{1,0:T(8,128)}), f32[128,512]{1,0:T(8,128)}) %reduce-scatter.19.cloned.1.call-update) | async-done | bytes 262160 | tf_op jit(solution)/shard_map/reduce_scatter | solution.py:261
  647.4 37.1 %reduce-scatter.17.cloned.1.call-done = f32[304,512]{1,0:T(8,128)} async-done(((f32[1216,512]{1,0:T(8,128)}), f32[304,512]{1,0:T(8,128)}) %reduce-scatter.17.cloned.1.call-update) | async-done | bytes 622608 | tf_op jit(solution)/shard_map/reduce_scatter | solution.py:259
  684.5 47.1 %reduce-scatter.23.cloned.1.call-done = f32[128,2048]{1,0:T(8,128)} async-done(((f32[512,2048]{1,0:T(8,128)}), f32[128,2048]{1,0:T(8,128)}) %reduce-scatter.23.cloned.1.call-update) | async-done | bytes 1048592 | tf_op jit(solution)/shard_map/reduce_scatter | solution.py:267
  731.5 47.1 %reduce-scatter.25.cloned.1.call-done = f32[512,512]{1,0:T(8,128)} async-done(((f32[2048,512]{1,0:T(8,128)}), f32[512,512]{1,0:T(8,128)}) %reduce-scatter.25.cloned.1.call-update) | async-done | bytes 1048592 | tf_op jit(solution)/shard_map/reduce_scatter | solution.py:269
  802.9 10.2 all-reduce.28.cloned.1.call-done
  814.9 79.1 %all-reduce.30.cloned.1.call-done = (f32[128]{0:T(128)}, f32[128]{0:T(128)}, f32[128]{0:T(128)}, f32[128]{0:T(128)}, f32[128]{0:T(128)}, /*index=5*/f32[512]{0:T...) async-done(((f32[128]{0:T(128)}, f32[128]{0:T(128)}, ...) | async-done | bytes 80848 | tf_op jit(solution)/shard_map/psum | solution.py:282
  894.1 146.3 %all-reduce.32.cloned.1.call-done = (f32[304,512]{1,0:T(8,128)}, f32[128,512]{1,0:T(8,128)}, f32[128,512]{1,0:T(8,128)}, f32[128,2048]{1,0:T(8,128)}, f32[512,512]{1,0:T(8,128)}, /*index=5*/f32[304,192]{0,1:T(8,128)}) async-done(((f32[304,512]{1,0:T(8,128)}, f32[128,512]{1,0:T(8,128)}, f32[128,512]{1,0:T(8,128)}, f32[128,2048]{1,0:T(8,128)}, f32[512,512]{1,0:T(8,128)}, /*index=5*/f32[304,192]{0,1:T(8,128)}), ...) | async-done | bytes 3477520 | tf_op jit(solution)/shard_map/psum | solution.py:282
  (389 shorter events, 283.6 us)
Async XLA Ops:
  7.2 152.0 %copy-start = (bf16[512,2048]{1,0:T(8,128)(2,1)S(1)}, bf16[512,2048]{1,0:T(8,128)(2,1)}, u32[]{:S(2)}) copy-start(bf16[512,2048]{1,0:T(8,128)(2,1)} %param.42) | copy-start | bytes 6291460
  7.2 78.1 %all-gather.3.cloned.1.call-start = ((), (), s32[]{:S(2)}) async-start(), calls=%async_computation.10 | async-start | bytes 1769472 | tf_op jit(solution)/shard_map/all_gather | solution.py:118
  8.0 149.6 %all-reduce.24.cloned.1.call-start = ((), (), s32[]{:S(2)}) async-start(), calls=%async_computation.11 | async-start | bytes 786432 | tf_op jit(solution)/shard_map/psum | solution.py:142
  60.5 158.4 %copy-start.44 = (pred[2880]{0:T(1024)(128)(4,1)}, pred[2880]{0:T(1024)(128)(4,1)S(1)}, u32[]{:S(2)}) copy-start(pred[2880]{0:T(1024)(128)(4,1)S(1)} %and.30) | copy-start | bytes 8644
  127.3 80.3 %all-gather.5.cloned.1.call-start = ((), (), s32[]{:S(2)}) async-start(), calls=%async_computation.12 | async-start | bytes 1769472 | tf_op jit(solution)/shard_map/all_gather | solution.py:158
  163.2 176.5 %reduce-scatter.13.cloned.1.call-start = ((), (), s32[]{:S(2)}) async-start(), calls=%async_computation.13 | async-start | bytes 3538944 | tf_op jit(solution)/shard_map/reduce_scatter | solution.py:195
  266.5 107.8 %all-reduce.26.cloned.1.call-start = ((), (), s32[]{:S(2)}) async-start(), calls=%async_computation.14 | async-start | bytes 786432 | tf_op jit(solution)/shard_map/psum | solution.py:204
  342.0 176.5 %reduce-scatter.15.cloned.1.call-start = ((), (), s32[]{:S(2)}) async-start(), calls=%async_computation.15 | async-start | bytes 3538944 | tf_op jit(solution)/shard_map/reduce_scatter | solution.py:248
  443.7 99.8 %reduce-scatter.29.cloned.1.call-start = ((), (), s32[]{:S(2)}) async-start(), calls=%async_computation.23 | async-start | bytes 245760 | tf_op jit(solution)/shard_map/reduce_scatter | solution.py:277
  455.9 106.1 %reduce-scatter.27.cloned.1.call-start = ((), (), s32[]{:S(2)}) async-start(), calls=%async_computation.22 | async-start | bytes 245760 | tf_op jit(solution)/shard_map/reduce_scatter | solution.py:275
  457.1 134.2 %reduce-scatter.31.cloned.1.call-start = ((), (), s32[]{:S(2)}) async-start(), calls=%async_computation.24 | async-start | bytes 1556480
  463.4 156.1 %reduce-scatter.21.cloned.1.call-start = ((), (), s32[]{:S(2)}) async-start(), calls=%async_computation.19 | async-start | bytes 1310720 | tf_op jit(solution)/shard_map/reduce_scatter | solution.py:263
  470.0 177.5 %reduce-scatter.19.cloned.1.call-start = ((), (), s32[]{:S(2)}) async-start(), calls=%async_computation.18 | async-start | bytes 1310720 | tf_op jit(solution)/shard_map/reduce_scatter | solution.py:261
  477.0 207.5 %reduce-scatter.17.cloned.1.call-start = ((), (), s32[]{:S(2)}) async-start(), calls=%async_computation.17 | async-start | bytes 3112960 | tf_op jit(solution)/shard_map/reduce_scatter | solution.py:259
  497.0 234.5 %reduce-scatter.23.cloned.1.call-start = ((), (), s32[]{:S(2)}) async-start(), calls=%async_computation.20 | async-start | bytes 5242880 | tf_op jit(solution)/shard_map/reduce_scatter | solution.py:267
  500.8 277.8 %reduce-scatter.25.cloned.1.call-start = ((), (), s32[]{:S(2)}) async-start(), calls=%async_computation.21 | async-start | bytes 5242880 | tf_op jit(solution)/shard_map/reduce_scatter | solution.py:269
  505.4 307.7 %all-reduce.28.cloned.1.call-start = ((), (), s32[]{:S(2)}) async-start(), calls=%async_computation.16 | async-start | bytes 393216 | tf_op jit(solution)/shard_map/psum | solution.py:254
  521.0 373.1 %all-reduce.30.cloned.1.call-start = ((), (), s32[]{:S(2)}) async-start(), calls=%async_computation.25 | async-start | bytes 214016 | tf_op jit(solution)/shard_map/psum | solution.py:282
  523.7 254.9 %copy-start.19 = (bf16[2880,192]{0,1:T(8,128)(2,1)S(1)}, bf16[2880,192]{0,1:T(8,128)(2,1)}, u32[]{:S(2)}) copy-start(bf16[2880,192]{0,1:T(8,128)(2,1)} %get-tuple-element.169) | copy-start | bytes 3317764
  562.1 478.3 %all-reduce.32.cloned.1.call-start = ((), (), s32[]{:S(2)}) async-start(), calls=%async_computation.26 | async-start | bytes 7077888 | tf_op jit(solution)/shard_map/psum | solution.py:282
  894.1 154.1 %copy-start.86 = (f32[128]{0:T(128)S(1)}, f32[128]{0:T(128)}, u32[]{:S(2)}) copy-start(f32[128]{0:T(128)} %get-tuple-element.198) | copy-start | bytes 1540
  894.1 154.7 %copy-start.85 = (f32[128]{0:T(128)S(1)}, f32[128]{0:T(128)}, u32[]{:S(2)}) copy-start(f32[128]{0:T(128)} %get-tuple-element.199) | copy-start | bytes 1540
  894.1 155.2 %copy-start.84 = (f32[128]{0:T(128)S(1)}, f32[128]{0:T(128)}, u32[]{:S(2)}) copy-start(f32[128]{0:T(128)} %get-tuple-element.200) | copy-start | bytes 1540
  894.1 156.7 %copy-start.61 = (f32[512]{0:T(512)S(1)}, f32[512]{0:T(512)}, u32[]{:S(2)}) copy-start(f32[512]{0:T(512)} %get-tuple-element.202) | copy-start | bytes 6148
  (85 other events, 883.6 us)
Sparse Core Ops, SparseCore 0:
  10.2 46.9 all-gather.2
  127.4 30.0 all-reduce.23
  163.4 44.1 all-gather.4
  266.7 72.9 reduce-scatter.12
  342.6 31.6 all-reduce.25
  443.8 74.5 reduce-scatter.14
  520.9 18.8 reduce-scatter.28
  542.3 19.7 reduce-scatter.26
  565.2 26.1 reduce-scatter.30
  594.5 24.8 reduce-scatter.20
  622.5 24.8 reduce-scatter.18
  650.6 33.8 reduce-scatter.16
  687.0 44.4 reduce-scatter.22
  734.1 44.4 reduce-scatter.24
  781.4 31.6 all-reduce.27
  821.1 72.8 all-reduce.29
  898.8 141.5 all-reduce.31
where the time goes:
time: 1070 us
  waiting for transfers between devices  624 us (58%)
  local copies, waits for them, and re-layouts  174 us (16%)
  matrix products  116 us (11%)
  other arithmetic  92.1 us (9%)
  blocking collectives  39.4 us (4%)
  between operations  18.2 us (2%)
    psum x2, waiting for transfers between devices, on_device(): weight_sums = lax.psum(tuple(shares), 'res')  225 us
    reduce_scatter x1, waiting for transfers between devices, on_device(): lax.psum_scatter(row_spreader(near_values, index_flat, lax.axis_size('res...  63.7 us
    unnamed x230, local copies, waits for them, and re-layouts  53.6 us
    scatter-add x2, other arithmetic, row_spreader(): return jax.ops.segment_sum(kept_rows, clipped, num_segments=span_rows)  49.8 us
    reduce_scatter x1, waiting for transfers between devices, on_device(): lax.psum_scatter(ffn_w2_grad, 'nbr', scatter_dimension=0, tiled=True)  47.1 us
    reduce_scatter x1, waiting for transfers between devices, on_device(): lax.psum_scatter(ffn_w1_grad, 'nbr', scatter_dimension=0, tiled=True)  47.1 us
    dot_general x12, matrix products, back_dot(): lax.dot_general(former, latter, (((1,), (1,)), ((), ())), preferred_eleme...  45.6 us
    dot_general x12, matrix products, outer_sum(): lax.dot_general(former, latter, (((0,), (0,)), ((), ())), preferred_eleme...  41.5 us
  transfers between devices with their start and end apart: 17, of which 15 were waited for; matrix products, arithmetic and copies ran while one was open for 17% of the time, Pallas kernels for 0%

commit v1 on v0

v1 whole, which is shorter than its diff:
```python
import functools

import jax
import jax.numpy as jnp
from jax import lax
from jax.experimental import pallas as pl
from jax.experimental.pallas import tpu as pltpu
from jax.sharding import PartitionSpec as P

D = 512
E = 192
FF = 2048
FAR = 32
SLOT = 16
VMEM = 56 * 1024 * 1024

bf16 = jnp.bfloat16
f32 = jnp.float32


def mm(a, b):
    return jnp.dot(a, b, preferred_element_type=f32)


def mm_tn(a, b):
    return lax.dot_general(a, b, (((0,), (0,)), ((), ())), preferred_element_type=f32)


def mm_nt(a, b):
    return lax.dot_general(a, b, (((1,), (1,)), ((), ())), preferred_element_type=f32)


def gelu_pair(v):
    c0 = 0.7978845608028654
    c1 = 0.044715 * c0
    square = v * v
    t = jnp.tanh(v * (c0 + c1 * square))
    half = 0.5 + 0.5 * t
    act = v * half
    return act, half + act * (1.0 - t) * (c0 + (3.0 * c1) * square)


def norm_forward(values):
    centred = values - jnp.mean(values, axis=-1, keepdims=True)
    inverse = lax.rsqrt(jnp.mean(centred * centred, axis=-1, keepdims=True) + 1e-05)
    return centred * inverse, inverse


def norm_backward(upstream, normed, inverse, gain):
    scaled = upstream * gain
    first = jnp.mean(scaled, axis=-1, keepdims=True)
    second = jnp.mean(scaled * normed, axis=-1, keepdims=True)
    return inverse * (scaled - first - normed * second)


def column_sum(values):
    return jnp.sum(values, axis=0, keepdims=True)


def iota(shape, dim):
    return lax.broadcasted_iota(jnp.int32, shape, dim)


def present_column(mask_ref, rows):
    real = jnp.sum(mask_ref[...].astype(f32), axis=1, keepdims=True)
    return (iota((rows, 1), 0).astype(f32) < real).astype(f32)


def pick_matrix(want_ref, rows):
    want = want_ref[...][:, :1].astype(f32)
    return (want == iota((want.shape[0], rows), 1).astype(f32)).astype(bf16)


def one_hot(column, width):
    return (column == iota((column.shape[0], width), 1)).astype(bf16)


def padded(ref, pad):
    rows, kn, c = ref.shape
    pad[:, kn:, :] = jnp.zeros((rows, SLOT - kn, c), pad.dtype)
    pad[:, :kn, :] = ref[...]
    return pad[...].reshape(rows * SLOT, c)


def spread(rows, values):
    n, c = rows.shape
    return (values.reshape(n, SLOT, c) + rows[:, None, :]).reshape(n * SLOT, c)


def gathered(values):
    n, c = values.shape
    return jnp.sum(values.reshape(n // SLOT, SLOT, c), axis=1)


def index_kernel(blocks, me_ref, near_ref, mask_ref, col_ref, want_ref, count_ref):
    rows, kn = near_ref.shape
    total = rows * SLOT
    me = me_ref[0].astype(f32)
    lanes = max(128, blocks)
    wide = jnp.broadcast_to(near_ref[...].astype(f32)[:, None, :], (rows, SLOT, kn)).reshape(total, kn)
    place = iota((total, 1), 0) & (SLOT - 1)
    index = jnp.sum(jnp.where(iota((total, kn), 1) == place, wide, 0.0), axis=1, keepdims=True)
    valid = place < kn
    block = jnp.floor((index + 0.5) * (1.0 / rows))
    slot = index - block * rows
    local = block == me
    far = jnp.logical_and(valid, jnp.logical_not(local))
    hot_slot = (slot == iota((total, rows), 1).astype(f32)).astype(bf16)
    block_key = jnp.where(far, block, -1.0)
    hot_block = (block_key == iota((total, lanes), 1).astype(f32)).astype(bf16)
    flags = (mm_tn(hot_block, hot_slot) > 0.0).astype(f32)
    before = (iota((rows, rows), 0) < iota((rows, rows), 1)).astype(bf16)
    rank = mm(flags.astype(bf16), before)
    edge_rank = jnp.sum(mm(hot_block, rank.astype(bf16)) * hot_slot.astype(f32), axis=1, keepdims=True)
    real = jnp.sum(mask_ref[...].astype(f32), axis=1, keepdims=True)
    own_place = (iota((total, 1), 0) // SLOT).astype(f32)
    named = jnp.logical_or(jnp.logical_not(local), slot < real)
    kept = jnp.logical_and(jnp.logical_and(valid, named), own_place < real)
    column = jnp.where(local, blocks * FAR + slot, block * FAR + edge_rank)
    column = jnp.where(kept, column, -1.0)
    col_ref[...] = column.astype(jnp.int32)
    key = jnp.where(flags > 0.0, rank, -1.0)[:blocks]
    key = jnp.broadcast_to(key[:, None, :], (blocks, FAR, rows)).reshape(blocks * FAR, rows)
    level = (iota((blocks * FAR, 1), 0) & (FAR - 1)).astype(f32)
    hit = (key == level).astype(f32)
    place_row = iota((blocks * FAR, rows), 1).astype(f32)
    want = jnp.sum(hit * place_row, axis=1, keepdims=True)
    found = jnp.sum(hit, axis=1, keepdims=True)
    want = jnp.where(found > 0.0, want, 255.0)
    want_ref[...] = jnp.broadcast_to(want, want_ref.shape).astype(bf16)
    counts = jnp.sum(kept.astype(f32).reshape(rows, SLOT, 1), axis=1)
    count_ref[...] = jnp.broadcast_to(counts, count_ref.shape).astype(bf16)


def message_forward_kernel(
    col_ref, edges_ref, nodes_ref, far_ref, w1_ref, w2_ref, small_ref,
    act1_ref, d1_ref, d2_ref, sum_ref, table, own, pad,
):
    step = pl.program_id(0)
    rows = edges_ref.shape[0]
    n_far = far_ref.shape[0]
    width = table.shape[0]

    @pl.when(step == 0)
    def _():
        weight = w1_ref[D : 2 * D, :]
        table[:n_far] = mm(far_ref[...], weight).astype(bf16)
        table[n_far:] = mm(nodes_ref[...], weight).astype(bf16)
        own[...] = mm(nodes_ref[...], w1_ref[:D, :]) + small_ref[0:1, :]

    edge = padded(edges_ref, pad)
    column = col_ref[...]
    pre1 = mm(one_hot(column, width), table[...]) + mm(edge, w1_ref[2 * D :, :])
    pre1 = spread(own[pl.ds(step * rows, rows), :], pre1)
    act, slope = gelu_pair(pre1)
    act1 = act.astype(bf16)
    act1_ref[...] = act1
    d1_ref[...] = slope.astype(bf16)
    act, slope = gelu_pair(mm(act1, w2_ref[...]) + small_ref[1:2, :])
    weight = (column >= 0).astype(f32)
    d2_ref[...] = (slope * weight).astype(bf16)
    sum_ref[...] = gathered(act.astype(bf16).astype(f32) * weight).astype(bf16)


def node_forward_kernel(
    sum_a, sum_b, count_a, count_b, nodes_ref, mask_ref, want_ref, w3_ref, f1_ref, f2_ref, small_ref, small_ff_ref,
    total_ref, low_ref, normed1_ref, inv1_ref, hid_ref, slope_ref, normed2_ref, inv2_ref, sent_ref, send_ref,
):
    rows = nodes_ref.shape[0]
    present = present_column(mask_ref, rows)
    count = count_a[...].astype(f32) + count_b[...].astype(f32)
    count = count[:, :1]
    total = sum_a[...].astype(f32) + sum_b[...].astype(f32)
    high = total.astype(bf16)
    total_ref[...] = high
    rest = (total - high.astype(f32)).astype(bf16)
    summed = mm(high, w3_ref[...]) + mm(rest, w3_ref[...]) + count * small_ref[2:3, :]
    mixed = nodes_ref[...].astype(f32) + summed / jnp.maximum(count, 1.0)
    normed, inverse = norm_forward(mixed)
    normed1_ref[...] = normed
    inv1_ref[...] = inverse
    first = normed * small_ref[3:4, :] + small_ref[4:5, :]
    low = first.astype(bf16)
    low_ref[...] = low
    act, slope = gelu_pair(mm(low, f1_ref[...]) + small_ff_ref[...])
    act = act.astype(bf16)
    hid_ref[...] = act
    slope_ref[...] = slope.astype(bf16)
    branch = mm(act, f2_ref[...]) + small_ref[5:6, :]
    normed, inverse = norm_forward(first + branch)
    normed2_ref[...] = normed
    inv2_ref[...] = inverse
    sent = (present * (normed * small_ref[6:7, :] + small_ref[7:8, :])).astype(bf16)
    sent_ref[...] = sent
    send_ref[...] = mm(pick_matrix(want_ref, rows), sent).astype(bf16)


def edge_kernel(
    order, col_ref, edges_ref, cot_ref, sent_ref, far_ref, w1_ref, w2_ref, w3_ref, small_ref,
    out_ref, base_ref, own_ref, far_grad_ref, local_grad_ref, packed_ref,
    table, own, pad, pad2, sums, w1_acc, w2_acc, w3_acc, bias_acc, own_acc,
):
    step = pl.program_id(0)
    last = pl.num_programs(0) - 1
    rows, kn, _ = edges_ref.shape
    n_far = far_ref.shape[0]
    width = table.shape[0]

    @pl.when(step == 0)
    def _():
        weight = w1_ref[D : 2 * D, :]
        table[:n_far] = mm(far_ref[...], weight).astype(bf16)
        table[n_far:] = mm(sent_ref[...], weight).astype(bf16)
        own[...] = mm(sent_ref[...], w1_ref[:D, :]) + small_ref[0:1, :]
        for acc in (sums, w1_acc, w2_acc, w3_acc, bias_acc):
            acc[...] = jnp.zeros_like(acc)

    edge = padded(edges_ref, pad)
    cot = padded(cot_ref, pad2)
    column = col_ref[...]
    hot = one_hot(column, width)
    pre1 = mm(hot, table[...]) + mm(edge, w1_ref[2 * D :, :])
    pre1 = spread(own[pl.ds(step * rows, rows), :], pre1)
    act, slope1 = gelu_pair(pre1)
    act1 = act.astype(bf16)
    act, slope2 = gelu_pair(mm(act1, w2_ref[...]) + small_ref[1:2, :])
    act2 = act.astype(bf16)
    branch = mm(act2, w3_ref[...]) + small_ref[2:3, :]
    weight = (column >= 0).astype(f32)
    normed, inverse = norm_forward(edge.astype(f32) + branch)
    gain = small_ref[3:4, :]
    out = weight * (normed * gain + small_ref[4:5, :])
    out_ref[...] = out.astype(bf16).reshape(rows, SLOT, E)[:, :kn, :]
    up = weight * cot.astype(f32)
    grad = norm_backward(up, normed, inverse, gain)
    low3 = grad.astype(bf16)
    w3_acc[...] += mm_tn(act2, low3)
    low2 = (slope2 * mm_nt(low3, w3_ref[...])).astype(bf16)
    w2_acc[...] += mm_tn(act1, low2)
    low1 = (slope1 * mm_nt(low2, w2_ref[...])).astype(bf16)
    w1_acc[...] += mm_tn(edge, low1)
    sums[...] += mm_tn(hot, low1)
    base_ref[...] = grad + mm_nt(low1, w1_ref[2 * D :, :])
    own_sum = gathered(low1.astype(f32))
    own_ref[...] = own_sum.astype(bf16)
    own_acc[pl.ds(step * rows, rows), :] = own_sum
    row = iota((16, 1), 0)
    bias_acc[...] += (
        jnp.where(row == 0, column_sum(own_sum), 0.0)
        + jnp.where(row == 1, column_sum(low2.astype(f32)), 0.0)
        + jnp.where(row == 2, column_sum(low3.astype(f32)), 0.0)
        + jnp.where(row == 3, column_sum(up * normed), 0.0)
        + jnp.where(row == 4, column_sum(up), 0.0)
    )

    @pl.when(step == last)
    def _():
        total = sums[...]
        far_grad_ref[...] = total[:n_far].astype(bf16)
        local_grad_ref[...] = total[n_far:].astype(bf16)
        sent = sent_ref[...]
        parts = len(order)
        first = (2 * D + E) // parts
        second = E // parts
        whole = jnp.concatenate(
            [
                mm_tn(sent, own_acc[...].astype(bf16)),
                mm_tn(far_ref[...], total[:n_far].astype(bf16)) + mm_tn(sent, total[n_far:].astype(bf16)),
                w1_acc[...],
            ],
            axis=0,
        ).astype(bf16)
        second_w = w2_acc[...].astype(bf16)
        third_w = w3_acc[...].astype(bf16)
        bias = bias_acc[...].astype(bf16)
        for q, n in enumerate(order):
            packed_ref[q, :first, :] = whole[n * first : (n + 1) * first]
            packed_ref[q, first : first + second, :] = second_w[n * second : (n + 1) * second]
            packed_ref[q, first + second : first + 2 * second, :] = third_w[n * second : (n + 1) * second]
            packed_ref[q, first + 2 * second :, :] = bias


def returned_kernel(own_ref, local_ref, back_ref, want_ref, out_ref):
    rows = local_ref.shape[0]
    near = local_ref[...].astype(f32) + mm_tn(pick_matrix(want_ref, rows), back_ref[...])
    out_ref[...] = jnp.concatenate([own_ref[...], near.astype(bf16)], axis=1)


def returned_last_kernel(own_ref, local_ref, back_ref, want_ref, w1_ref, out_ref):
    rows = local_ref.shape[0]
    near = local_ref[...].astype(f32) + mm_tn(pick_matrix(want_ref, rows), back_ref[...])
    grad = mm_nt(own_ref[...], w1_ref[:D, :]) + mm_nt(near.astype(bf16), w1_ref[D : 2 * D, :])
    out_ref[...] = grad.astype(bf16)


def node_backward_kernel(
    parts, place_ref, back_a, back_b, count_a, count_b, cot_ref, mask_ref, total_ref, low_ref, normed1_ref, inv1_ref,
    hid_ref, slope_ref, normed2_ref, inv2_ref, ew1_ref, w3_ref, f1_ref, f2_ref, small_ref, edge_part_ref,
    mixed_ref, up_ref, bias_ref, packed_ref, hid_grad,
):
    rows = cot_ref.shape[0]
    place = place_ref[0]
    present = present_column(mask_ref, rows)
    count = (count_a[...].astype(f32) + count_b[...].astype(f32))[:, :1]
    back = (back_a[...].astype(f32) + back_b[...].astype(f32)).astype(bf16)
    node_back = mm_nt(back[:, :E], ew1_ref[:D, :]) + mm_nt(back[:, E:], ew1_ref[D : 2 * D, :])
    up = present * (cot_ref[...].astype(f32) + node_back)
    normed2 = normed2_ref[...]
    sum_grad = norm_backward(up, normed2, inv2_ref[...], small_ref[6:7, :])
    branch_grad = sum_grad.astype(bf16)
    hidden_grad = (slope_ref[...].astype(f32) * mm_nt(branch_grad, f2_ref[...])).astype(bf16)
    first_grad = sum_grad + mm_nt(hidden_grad, f1_ref[...])
    normed1 = normed1_ref[...]
    mixed_grad = norm_backward(first_grad, normed1, inv1_ref[...], small_ref[3:4, :])
    mixed_ref[...] = mixed_grad
    message_grad = (mixed_grad / jnp.maximum(count, 1.0)).astype(bf16)
    up_ref[...] = mm_nt(message_grad, w3_ref[...])
    row = iota((16, 1), 0)
    hidden_sum = column_sum(hidden_grad.astype(f32))
    bias = (
        jnp.where(row == 2, column_sum(count * message_grad.astype(f32)), 0.0)
        + jnp.where(row == 3, column_sum(first_grad * normed1), 0.0)
        + jnp.where(row == 4, column_sum(first_grad), 0.0)
        + jnp.where(row == 5, column_sum(branch_grad.astype(f32)), 0.0)
        + jnp.where(row == 6, column_sum(up * normed2), 0.0)
        + jnp.where(row == 7, column_sum(up), 0.0)
    )
    for j in range(FF // D):
        bias = bias + jnp.where(row == 8 + j, hidden_sum[:, j * D : (j + 1) * D], 0.0)
    bias_ref[...] = bias * (1.0 / parts)
    wide, narrow = FF // parts, D // parts
    low = low_ref[:, pl.ds(pl.multiple_of(place * narrow, narrow), narrow)]
    for j in range(FF // D):
        packed_ref[j * narrow : (j + 1) * narrow, :] = mm_tn(low, hidden_grad[:, j * D : (j + 1) * D]).astype(bf16)
    hid = hid_ref[:, pl.ds(pl.multiple_of(place * wide, wide), wide)]
    packed_ref[D : D + wide, :] = mm_tn(hid, branch_grad).astype(bf16)
    total = total_ref[:, pl.ds(pl.multiple_of(place * narrow, narrow), narrow)]
    packed_ref[D + wide : D + wide + narrow, :] = mm_tn(total, message_grad).astype(bf16)
    at = D + wide + narrow
    half = edge_part_ref.shape[0] // 2
    packed_ref[at:, :] = jnp.zeros((packed_ref.shape[0] - at, D), bf16)
    packed_ref[at : at + half, :E] = edge_part_ref[:half, :]
    packed_ref[at : at + half, 256 : 256 + E] = edge_part_ref[half:, :]


def message_backward_kernel(
    order, col_ref, edges_ref, act1_ref, d1_ref, d2_ref, up_ref, base_ref, nodes_ref, far_ref, w1_ref, w2_ref, node_bias_ref,
    out_ref, own_ref, far_grad_ref, local_grad_ref, packed_ref,
    pad, sums, w1_acc, w2_acc, bias_acc, own_acc,
):
    step = pl.program_id(0)
    last = pl.num_programs(0) - 1
    rows, kn, _ = edges_ref.shape
    n_far = far_ref.shape[0]
    width = sums.shape[0]

    @pl.when(step == 0)
    def _():
        for acc in (sums, w1_acc, w2_acc):
            acc[...] = jnp.zeros_like(acc)
        bias_acc[...] = node_bias_ref[...]

    edge = padded(edges_ref, pad)
    hot = one_hot(col_ref[...], width)
    up = jnp.broadcast_to(up_ref[...][:, None, :], (rows, SLOT, D)).reshape(rows * SLOT, D)
    low2 = (d2_ref[...].astype(f32) * up).astype(bf16)
    w2_acc[...] += mm_tn(act1_ref[...], low2)
    low1 = (d1_ref[...].astype(f32) * mm_nt(low2, w2_ref[...])).astype(bf16)
    w1_acc[...] += mm_tn(edge, low1)
    sums[...] += mm_tn(hot, low1)
    grad = base_ref[...] + mm_nt(low1, w1_ref[2 * D :, :])
    out_ref[...] = grad.reshape(rows, SLOT, E)[:, :kn, :]
    own_sum = gathered(low1.astype(f32))
    own_ref[...] = own_sum.astype(bf16)
    own_acc[pl.ds(step * rows, rows), :] = own_sum
    row = iota((16, 1), 0)
    bias_acc[...] += jnp.where(row == 0, column_sum(own_sum), 0.0) + jnp.where(
        row == 1, column_sum(low2.astype(f32)), 0.0
    )

    @pl.when(step == last)
    def _():
        total = sums[...]
        far_grad_ref[...] = total[:n_far].astype(bf16)
        local_grad_ref[...] = total[n_far:].astype(bf16)
        nodes = nodes_ref[...]
        parts = len(order)
        first = (2 * D + E) // parts
        second = D // parts
        whole = jnp.concatenate(
            [
                mm_tn(nodes, own_acc[...].astype(bf16)),
                mm_tn(far_ref[...], total[:n_far].astype(bf16)) + mm_tn(nodes, total[n_far:].astype(bf16)),
                w1_acc[...],
            ],
            axis=0,
        ).astype(bf16)
        second_w = w2_acc[...].astype(bf16)
        bias = bias_acc[...].astype(bf16)
        for q, n in enumerate(order):
            packed_ref[q, :first, :] = whole[n * first : (n + 1) * first]
            packed_ref[q, first : first + second, :] = second_w[n * second : (n + 1) * second]
            packed_ref[q, first + second : first + second + 16, :] = bias
            if packed_ref.shape[1] > first + second + 16:
                packed_ref[q, first + second + 16 :, :] = jnp.zeros(
                    (packed_ref.shape[1] - first - second - 16, D), bf16
                )


def swap(values, axis, bit):
    return lax.ppermute(values, axis, [(i, i ^ bit) for i in range(lax.axis_size(axis))])


def bits_of(axis):
    size, bit, out = lax.axis_size(axis), 1, []
    while bit < size:
        out.append(bit)
        bit *= 2
    return out


def add_low(a, b):
    return (a.astype(f32) + b.astype(f32)).astype(bf16)


def shared_sum(values, axis):
    bits = bits_of(axis)
    for bit in bits[:-1]:
        values = add_low(values, swap(values, axis, bit))
    return values, swap(values, axis, bits[-1])


def halves(values, axis, bit):
    half = values.shape[0] // 2
    side = (lax.axis_index(axis) // bit) & 1
    kept = lax.dynamic_slice_in_dim(values, side * half, half, 0)
    given = lax.dynamic_slice_in_dim(values, (1 - side) * half, half, 0)
    return kept, given


def scattered_sum(values, axis):
    for bit in bits_of(axis):
        kept, given = halves(values, axis, bit)
        values = add_low(kept, swap(given, axis, bit))
    return values


def assembled(values, axis):
    for bit in reversed(bits_of(axis)):
        other = swap(values, axis, bit)
        side = (lax.axis_index(axis) // bit) & 1
        rows = values.shape[0]
        whole = jnp.zeros((2 * rows,) + values.shape[1:], values.dtype)
        whole = lax.dynamic_update_slice_in_dim(whole, values, side * rows, 0)
        values = lax.dynamic_update_slice_in_dim(whole, other, (1 - side) * rows, 0)
    return values


def exchange(values, blocks):
    shaped = values.reshape((blocks, values.shape[0] // blocks) + values.shape[1:])
    return lax.all_to_all(shaped, "res", 0, 0, tiled=True).reshape(values.shape)


def call(kernel, outs, scratch=(), grid=None, in_specs=None, out_specs=None, cost=None):
    extra = {}
    if grid is not None:
        extra = dict(grid=grid, in_specs=in_specs, out_specs=out_specs)
    elif in_specs is not None:
        extra = dict(in_specs=in_specs)
    return pl.pallas_call(
        kernel,
        out_shape=outs,
        scratch_shapes=list(scratch),
        compiler_params=pltpu.CompilerParams(vmem_limit_bytes=VMEM),
        cost_estimate=cost,
        **extra,
    )


def shape(dims, dtype):
    return jax.ShapeDtypeStruct(dims, dtype)


def up_to(value, unit):
    return -(-value // unit) * unit


def on_device(
    nodes,
    edges,
    neighbours,
    residue_mask,
    msg_w1,
    msg_b1,
    msg_w2,
    msg_b2,
    msg_w3,
    msg_b3,
    norm1_gain,
    norm1_bias,
    ffn_w1,
    ffn_b1,
    ffn_w2,
    ffn_b2,
    norm2_gain,
    norm2_bias,
    edge_w1,
    edge_b1,
    edge_w2,
    edge_b2,
    edge_w3,
    edge_b3,
    norm3_gain,
    norm3_bias,
    node_cot,
    edge_cot,
):
    rows, kn = neighbours.shape
    blocks, parts = lax.axis_size("res"), lax.axis_size("nbr")
    total = rows * SLOT
    n_far = blocks * FAR
    width = n_far + rows
    tile = rows // 4
    grid = (rows // tile,)
    nbr_bits = bits_of("nbr")
    order = tuple(
        sum(bit for i, bit in enumerate(nbr_bits) if (q >> (len(nbr_bits) - 1 - i)) & 1) for q in range(parts)
    )
    mask_row = residue_mask.reshape(1, rows)
    small = jnp.stack([msg_b1, msg_b2, msg_b3, norm1_gain, norm1_bias, ffn_b2, norm2_gain, norm2_bias]).astype(f32)
    small_ff = ffn_b1.reshape(1, FF).astype(f32)
    small_edge = jnp.stack(
        [edge_b1, edge_b2, edge_b3, norm3_gain, norm3_bias, norm3_bias, norm3_bias, norm3_bias]
    ).astype(f32)
    res_place = lax.axis_index("res").astype(jnp.int32).reshape(1)
    nbr_place = lax.axis_index("nbr").astype(jnp.int32).reshape(1)

    smem = pl.BlockSpec(memory_space=pltpu.SMEM)
    vmem = pl.BlockSpec(memory_space=pltpu.VMEM)

    def fixed(*dims):
        return pl.BlockSpec(dims, lambda i: (0,) * len(dims))

    def tiled(*dims):
        return pl.BlockSpec(dims, lambda i: (i,) + (0,) * (len(dims) - 1))

    column, want, counts = call(
        functools.partial(index_kernel, blocks),
        (shape((total, 1), jnp.int32), shape((n_far, 128), bf16), shape((rows, 128), bf16)),
        in_specs=[smem, vmem, vmem],
    )(res_place, neighbours, mask_row)
    wanted = exchange(want, blocks)
    count_a, count_b = shared_sum(counts, "nbr")

    picks = (wanted[:, :1].astype(jnp.int32) == iota((n_far, rows), 1)).astype(bf16)
    far_nodes = exchange(mm(picks, nodes).astype(bf16), blocks)

    edge_tile = tiled(tile, kn, E)
    flat = tiled(tile * SLOT, D)
    act1, d1, d2, act_sum = call(
        message_forward_kernel,
        (shape((total, D), bf16), shape((total, D), bf16), shape((total, D), bf16), shape((rows, D), bf16)),
        scratch=[pltpu.VMEM((width, D), bf16), pltpu.VMEM((rows, D), f32), pltpu.VMEM((tile, SLOT, E), bf16)],
        grid=grid,
        in_specs=[
            tiled(tile * SLOT, 1),
            edge_tile,
            fixed(rows, D),
            fixed(n_far, D),
            fixed(2 * D + E, D),
            fixed(D, D),
            fixed(8, D),
        ],
        out_specs=(flat, flat, flat, tiled(tile, D)),
    )(column, edges, nodes, far_nodes, msg_w1, msg_w2, small)
    sum_a, sum_b = shared_sum(act_sum, "nbr")

    total_act, first_low, normed1, inv1, hidden, hidden_slope, normed2, inv2, sent, send = call(
        node_forward_kernel,
        (
            shape((rows, D), bf16),
            shape((rows, D), bf16),
            shape((rows, D), f32),
            shape((rows, 1), f32),
            shape((rows, FF), bf16),
            shape((rows, FF), bf16),
            shape((rows, D), f32),
            shape((rows, 1), f32),
            shape((rows, D), bf16),
            shape((n_far, D), bf16),
        ),
    )(sum_a, sum_b, count_a, count_b, nodes, mask_row, wanted, msg_w3, ffn_w1, ffn_w2, small, small_ff)
    far_sent = exchange(send, blocks)

    first_rows, second_rows = (2 * D + E) // parts, E // parts
    edge_rows = up_to(first_rows + 2 * second_rows + 16, 32)
    edges_out, base, own_sum, far_sum, local_sum, edge_packed = call(
        functools.partial(edge_kernel, order),
        (
            shape((rows, kn, E), bf16),
            shape((total, E), f32),
            shape((rows, E), bf16),
            shape((n_far, E), bf16),
            shape((rows, E), bf16),
            shape((parts, edge_rows, E), bf16),
        ),
        scratch=[
            pltpu.VMEM((width, E), bf16),
            pltpu.VMEM((rows, E), f32),
            pltpu.VMEM((tile, SLOT, E), bf16),
            pltpu.VMEM((tile, SLOT, E), bf16),
            pltpu.VMEM((width, E), f32),
            pltpu.VMEM((E, E), f32),
            pltpu.VMEM((E, E), f32),
            pltpu.VMEM((E, E), f32),
            pltpu.VMEM((16, E), f32),
            pltpu.VMEM((rows, E), f32),
        ],
        grid=grid,
        in_specs=[
            tiled(tile * SLOT, 1),
            edge_tile,
            edge_tile,
            fixed(rows, D),
            fixed(n_far, D),
            fixed(2 * D + E, E),
            fixed(E, E),
            fixed(E, E),
            fixed(8, E),
        ],
        out_specs=(
            edge_tile,
            tiled(tile * SLOT, E),
            tiled(tile, E),
            fixed(n_far, E),
            fixed(rows, E),
            fixed(parts, edge_rows, E),
        ),
    )(column, edges, edge_cot, sent, far_sent, edge_w1, edge_w2, edge_w3, small_edge)

    back = call(returned_kernel, shape((rows, 2 * E), bf16))(own_sum, local_sum, exchange(far_sum, blocks), wanted)
    back_a, back_b = shared_sum(back, "nbr")
    edge_part = scattered_sum(edge_packed, "nbr").reshape(edge_rows, E)

    wide, narrow = FF // parts, D // parts
    node_rows = up_to(D + wide + narrow + edge_rows // 2, 16 * blocks)
    mixed_grad, up, node_bias, node_packed = call(
        functools.partial(node_backward_kernel, parts),
        (
            shape((rows, D), f32),
            shape((rows, D), f32),
            shape((16, D), f32),
            shape((node_rows, D), bf16),
        ),
        scratch=[pltpu.VMEM((rows, FF), bf16)],
        in_specs=[smem] + [vmem] * 20,
    )(
        nbr_place, back_a, back_b, count_a, count_b, node_cot, mask_row, total_act, first_low, normed1, inv1,
        hidden, hidden_slope, normed2, inv2, edge_w1, msg_w3, ffn_w1, ffn_w2, small, edge_part,
    )
    node_share = assembled(scattered_sum(node_packed, "res"), "res")

    msg_rows = up_to(first_rows + narrow + 16, 8 * blocks)
    edges_grad, own_sum, far_sum, local_sum, msg_packed = call(
        functools.partial(message_backward_kernel, order),
        (
            shape((rows, kn, E), f32),
            shape((rows, D), bf16),
            shape((n_far, D), bf16),
            shape((rows, D), bf16),
            shape((parts, msg_rows, D), bf16),
        ),
        scratch=[
            pltpu.VMEM((tile, SLOT, E), bf16),
            pltpu.VMEM((width, D), f32),
            pltpu.VMEM((E, D), f32),
            pltpu.VMEM((D, D), f32),
            pltpu.VMEM((16, D), f32),
            pltpu.VMEM((rows, D), f32),
        ],
        grid=grid,
        in_specs=[
            tiled(tile * SLOT, 1),
            edge_tile,
            flat,
            flat,
            flat,
            tiled(tile, D),
            tiled(tile * SLOT, E),
            fixed(rows, D),
            fixed(n_far, D),
            fixed(2 * D + E, D),
            fixed(D, D),
            fixed(16, D),
        ],
        out_specs=(edge_tile, tiled(tile, D), fixed(n_far, D), fixed(rows, D), fixed(parts, msg_rows, D)),
    )(column, edges, act1, d1, d2, up, base, nodes, far_nodes, msg_w1, msg_w2, node_bias)

    back = call(returned_last_kernel, shape((rows, D), bf16))(
        own_sum, local_sum, exchange(far_sum, blocks), wanted, msg_w1
    )
    back_a, back_b = shared_sum(back, "nbr")
    nodes_grad = mixed_grad + (back_a.astype(f32) + back_b.astype(f32))
    msg_part = scattered_sum(msg_packed, "nbr").reshape(msg_rows, D)
    msg_share = assembled(scattered_sum(msg_part, "res"), "res").astype(f32)

    node_share = node_share.astype(f32)
    ffn_w1_grad = jnp.concatenate([node_share[j * narrow : (j + 1) * narrow] for j in range(FF // D)], axis=1)
    ffn_w2_grad = node_share[D : D + wide]
    at = D + wide + narrow
    msg_w3_grad = node_share[D + wide : at]
    half = edge_rows // 2
    edge_share = jnp.concatenate([node_share[at : at + half, :E], node_share[at : at + half, 256 : 256 + E]], axis=0)
    edge_w1_grad = edge_share[:first_rows]
    edge_w2_grad = edge_share[first_rows : first_rows + second_rows]
    edge_w3_grad = edge_share[first_rows + second_rows : first_rows + 2 * second_rows]
    place = lax.axis_index("nbr")
    edge_bias = edge_share[first_rows + 2 * second_rows : first_rows + 2 * second_rows + 8]
    edge_bias = lax.dynamic_slice_in_dim(edge_bias, place * second_rows, second_rows, 1)
    msg_w1_grad = msg_share[:first_rows]
    msg_w2_grad = msg_share[first_rows : first_rows + narrow]
    bias_all = msg_share[first_rows + narrow : first_rows + narrow + 16]
    bias = lax.dynamic_slice_in_dim(bias_all[:8], place * narrow, narrow, 1)
    ffn_b1_grad = lax.dynamic_index_in_dim(bias_all[8 : 8 + FF // D], place, 0, keepdims=False)
    return (
        sent,
        edges_out,
        nodes_grad,
        edges_grad,
        msg_w1_grad,
        bias[0],
        msg_w2_grad,
        bias[1],
        msg_w3_grad,
        bias[2],
        bias[3],
        bias[4],
        ffn_w1_grad,
        ffn_b1_grad,
        ffn_w2_grad,
        bias[5],
        bias[6],
        bias[7],
        edge_w1_grad,
        edge_bias[0],
        edge_w2_grad,
        edge_bias[1],
        edge_w3_grad,
        edge_bias[2],
        edge_bias[3],
        edge_bias[4],
    )


def solution(mesh):
    every = P()
    in_specs = (
        (P("res", None), P("res", "nbr", None), P("res", "nbr"), P("res"))
        + (every,) * 22
        + (P("res", None), P("res", "nbr", None))
    )
    matrix, vector = P("nbr", None), P("nbr")
    out_specs = (
        (P("res", None), P("res", "nbr", None), P("res", None), P("res", "nbr", None))
        + (matrix, vector) * 3
        + (vector, vector, matrix, vector, matrix, vector, vector, vector)
        + (matrix, vector) * 3
        + (vector, vector)
    )
    return jax.shard_map(on_device, mesh=mesh, in_specs=in_specs, out_specs=out_specs, check_vma=False)
```

time: 1070 us -> 249 us (0.23)
  waiting for transfers between devices: 624 us -> 82.6 us
  local copies, waits for them, and re-layouts: 174 us -> 29.3 us
  matrix products: 116 us -> 1.91 us
  other arithmetic: 92.1 us -> 8.88 us
  Pallas kernels: 0 us -> 70.9 us
  starting transfers between devices: 1.67 us -> 38.6 us
  blocking collectives: 39.4 us -> 14.2 us
  between operations: 18.2 us -> 1.41 us
    psum x5 -> x0, waiting for transfers between devices: 298 us -> none  [the longest x2 225 us: on_device(): weight_sums = lax.psum(tuple(shares), 'res')]
    reduce_scatter x9 -> x0, waiting for transfers between devices: 278 us -> none  [the longest x1 63.7 us: on_device(): lax.psum_scatter(row_spreader(near_values, index_flat, lax.axis_size('res...]
    dot_general x36 -> x1, matrix products: 116 us -> 1.91 us  [mm(): return jnp.dot(a, b, preferred_element_type=f32)]
    pallas_call x0 -> x8, Pallas kernels: none -> 70.9 us  [the longest x1 17.5 us: on_device(): call(functools.partial(edge_kernel, order), (shape((rows, kn, E), bf16),...]
    ppermute x0 -> x24, waiting for transfers between devices: none -> 61.2 us  [swap(): lax.ppermute(values, axis, [(i, i ^ bit) for i in range(lax.axis_size(axi...]
    scatter-add x2 -> x0, other arithmetic: 49.8 us -> none  [row_spreader(): return jax.ops.segment_sum(kept_rows, clipped, num_segments=span_rows)]
    gather x4 -> x0, local copies, waits for them, and re-layouts: 40.1 us -> none  [collect(): return jnp.where(shaped, jnp.take(portion, clipped, axis=0), holder)]
    unnamed x230 -> x81, local copies, waits for them, and re-layouts: 53.6 us -> 19.5 us
  transfers between devices with their start and end apart: 17 -> 28, of which waited for: 15 -> 18; matrix products, arithmetic and copies ran while one was open for 17% -> 11% of each run, Pallas kernels for 0% -> 2%
where the time goes in v1:
time: 249 us; the launch traced here: 248 us
  waiting for transfers between devices  82.6 us (33%)
  Pallas kernels  70.9 us (28%)
  starting transfers between devices  38.6 us (16%)
  local copies, waits for them, and re-layouts  29.3 us (12%)
  blocking collectives  14.2 us (6%)
  other arithmetic  8.88 us (4%)
    ppermute x24, waiting for transfers between devices, swap(): lax.ppermute(values, axis, [(i, i ^ bit) for i in range(lax.axis_size(axi...  61.2 us
    ppermute x24, starting transfers between devices, swap(): lax.ppermute(values, axis, [(i, i ^ bit) for i in range(lax.axis_size(axi...  24.3 us
    all_to_all x4, waiting for transfers between devices, exchange(): return lax.all_to_all(shaped, 'res', 0, 0, tiled=True).reshape(values.shape)  21.4 us
    unnamed x81, local copies, waits for them, and re-layouts  19.5 us
    pallas_call x1, Pallas kernels, on_device(): call(functools.partial(edge_kernel, order), (shape((rows, kn, E), bf16),...  17.5 us
    pallas_call x1, Pallas kernels, on_device(): call(message_forward_kernel, (shape((total, D), bf16), shape((total, D),...  14.8 us
    all_to_all x4, starting transfers between devices, exchange(): return lax.all_to_all(shaped, 'res', 0, 0, tiled=True).reshape(values.shape)  14.4 us
    all_to_all x1, blocking collectives, exchange(): return lax.all_to_all(shaped, 'res', 0, 0, tiled=True).reshape(values.shape)  14.2 us
  transfers between devices with their start and end apart: 28, of which 18 were waited for; matrix products, arithmetic and copies ran while one was open for 11% of the time, Pallas kernels for 2%

profile of v1, /device:TPU:0, one launch (start us, length us, event | category | flops | bytes accessed | tf_op | source)
XLA Modules:
  0.0 247.8 jit_solution(17461530411378362430)
XLA Ops:
  2.1 5.8 %shard_map.467 = (s32[3072,1]{1,0:T(8,128)}, bf16[256,128]{1,0:T(8,128)(2,1)}, bf16[192,128]{1,0:T(8,128)(2,1)}) custom-call(s32[1]{0:T(128)} %bitcast.me_ref, s32[192,15]{1,0:T(8,128)} %copy.64.near_ref, s32[1,192]{1,0:T(1,128)} %bitcast.63), custom_call_target="tpu_custom_call" | custom-call | tf_op jit(solution)/shard_map/pallas_call | solution.py:547
  7.9 14.2 %all_to_all.25 = bf16[8,32,128]{2,1,0:T(8,128)(2,1)S(1)} all-to-all(bf16[8,32,128]{2,1,0:T(8,128)(2,1)} %bitcast.61), channel_id=1, replica_groups=mesh['res'=8,'nbr'=4] {'res'}, dimensions={0} | all-to-all | bytes 131072 | tf_op jit(solution)/shard_map/all_to_all | solution.py:461
  24.1 3.4 %all-to-all-start.1 = ((bf16[8,32,512]{2,1,0:T(8,128)(2,1)}), bf16[8,32,512]{2,1,0:T(8,128)(2,1)S(1)}, u32[]{:S(2)}, u32[]{:S(2)}) async-start(bf16[8,32,512]{2,1,0:T(8,128)(2,1)} %bitcast.4), calls=%async_computation.1 | async-start | bytes 524288 | tf_op jit(solution)/shard_map/all_to_all | solution.py:461
  27.6 3.4 %copy.65.edges_ref = bf16[192,15,192]{2,1,0:T(8,128)(2,1)} copy(bf16[192,15,192]{2,0,1:T(8,128)(2,1)} %param.29) | data formatting | bytes 2211840 | tf_op args[1]
  31.8 3.9 %all-to-all-done.1 = bf16[8,32,512]{2,1,0:T(8,128)(2,1)S(1)} async-done(((bf16[8,32,512]{2,1,0:T(8,128)(2,1)}), bf16[8,32,512]{2,1,0:T(8,128)(2,1)S(1)}, u32[]{:S(2)}, u32[]{:S(2)}) %all-to-all-start.1) | async-done | bytes 262176 | tf_op jit(solution)/shard_map/all_to_all | solution.py:461
  36.4 14.8 %shard_map.468 = (bf16[3072,512]{1,0:T(8,128)(2,1)}, bf16[3072,512]{1,0:T(8,128)(2,1)}, bf16[3072,512]{1,0:T(8,128)(2,1)}, bf16[192,512]{1,0:T(8,128)(2,1)}) custom-call(s32[3072,1]{1,0:T(8,128)} %get-tuple-element.58.col_ref, bf16[192,15,192]{2,1,0:T(8,128)(2,1)} %copy.65.edges_ref, bf16[192,512]{1,0:T(8,128)(2,1)} %nodes_ref.5, bf16[256,512]{1,0:T(8,128)(2,1)} %bitcast.49, ...), custom_call_target="tpu_custom_call" | custom-call | tf_op jit(solution)/shard_map/pallas_call | solution.py:560
  56.6 5.3 %collective-permute-done.3.count_b = bf16[192,128]{1,0:T(8,128)(2,1)S(1)} collective-permute-done((bf16[192,128]{1,0:T(8,128)(2,1)S(1)}, bf16[192,128]{1,0:T(8,128)(2,1)S(1)}, u32[]{:S(2)}, u32[]{:S(2)}) %collective-permute-start.3) | collective-permute-done | bytes 49184 | tf_op jit(solution)/shard_map/ppermute | solution.py:411
  62.6 6.1 %shard_map.469 = (bf16[192,512]{1,0:T(8,128)(2,1)}, bf16[192,512]{1,0:T(8,128)(2,1)}, f32[192,512]{1,0:T(8,128)}, f32[192,1]{1,0:T(8,128)}, bf16[192,2048]{1,0:T...) custom-call(bf16[192,512]{1,0:T(8,128)(2,1)} %copy-done.11, ...), custom_call_target="tpu_custom_call" | custom-call | tf_op jit(solution)/shard_map/pallas_call | solution.py:578
  68.7 3.6 %all-to-all-start.2 = ((bf16[8,32,512]{2,1,0:T(8,128)(2,1)}), bf16[8,32,512]{2,1,0:T(8,128)(2,1)S(1)}, u32[]{:S(2)}, u32[]{:S(2)}) async-start(bf16[8,32,512]{2,1,0:T(8,128)(2,1)} %bitcast.58), calls=%async_computation.2 | async-start | bytes 524288 | tf_op jit(solution)/shard_map/all_to_all | solution.py:461
  76.1 4.6 %all-to-all-done.2 = bf16[8,32,512]{2,1,0:T(8,128)(2,1)S(1)} async-done(((bf16[8,32,512]{2,1,0:T(8,128)(2,1)}), bf16[8,32,512]{2,1,0:T(8,128)(2,1)S(1)}, u32[]{:S(2)}, u32[]{:S(2)}) %all-to-all-start.2) | async-done | bytes 262176 | tf_op jit(solution)/shard_map/all_to_all | solution.py:461
  81.4 17.5 %shard_map.470 = (bf16[192,15,192]{2,1,0:T(8,128)(2,1)}, f32[3072,192]{1,0:T(8,128)}, bf16[192,192]{1,0:T(8,128)(2,1)}, bf16[256,192]{1,0:T(8,128)(2,1)}, bf16[1...) custom-call(s32[3072,1]{1,0:T(8,128)} %get-tuple-element.58.col_ref, bf16[192,15,192]{2,1,0:T(8,128)(2,1)} %copy.65.edges_ref, ...), custom_call_target="tpu_custom_call" | custom-call | tf_op jit(solution)/shard_map/pallas_call | solution.py:597
  100.2 3.6 %all-to-all-start.3 = ((bf16[8,32,192]{2,1,0:T(8,128)(2,1)}), bf16[8,32,192]{2,1,0:T(8,128)(2,1)S(1)}, u32[]{:S(2)}, u32[]{:S(2)}) async-start(bf16[8,32,192]{2,1,0:T(8,128)(2,1)} %bitcast.60), calls=%async_computation.3 | async-start | bytes 262144 | tf_op jit(solution)/shard_map/all_to_all | solution.py:461
  103.8 7.7 %all-to-all-done.3 = bf16[8,32,192]{2,1,0:T(8,128)(2,1)S(1)} async-done(((bf16[8,32,192]{2,1,0:T(8,128)(2,1)}), bf16[8,32,192]{2,1,0:T(8,128)(2,1)S(1)}, u32[]{:S(2)}, u32[]{:S(2)}) %all-to-all-start.3) | async-done | bytes 98336 | tf_op jit(solution)/shard_map/all_to_all | solution.py:461
  117.3 5.1 %collective-permute-done.7 = bf16[1,416,192]{2,1,0:T(8,128)(2,1)S(1)} collective-permute-done((bf16[1,416,192]{2,1,0:T(8,128)(2,1)S(1)}, bf16[1,416,192]{2,1,0:T(8,128)(2,1)S(1)}, u32[]{:S(2)}, u32[]{:S(2)}) %collective-permute-start.7) | collective-permute-done | bytes 159776 | tf_op jit(solution)/shard_map/ppermute | solution.py:411
  125.8 7.6 %shard_map.472 = (f32[192,512]{1,0:T(8,128)}, f32[192,512]{1,0:T(8,128)}, f32[16,512]{1,0:T(8,128)}, bf16[1408,512]{1,0:T(8,128)(2,1)}) custom-call(s32[1]{0:T(128)} %bitcast.9.place_ref, bf16[192,384]{1,0:T(8,128)(2,1)} %copy-done.14, bf16[192,384]{1,0:T(8,128)(2,1)} %copy-done.21, bf16[192,128]{1,0:T(8,128)(2,1)} %copy-done.17, ...), custom_call_target="tpu_custom_call" | custom-call | tf_op jit(solution)/shard_map/pallas_call | solution.py:647
  133.4 14.1 %shard_map.473 = (f32[192,15,192]{2,1,0:T(8,128)}, bf16[192,512]{1,0:T(8,128)(2,1)}, bf16[256,512]{1,0:T(8,128)(2,1)}, bf16[192,512]{1,0:T(8,128)(2,1)}, bf16[4,448,512]{2,1,0:T(8,128)(2,1)}) custom-call(s32[3072,1]{1,0:T(8,128)} %get-tuple-element.58.col_ref, bf16[192,15,192]{2,1,0:T(8,128)(2,1)} %copy.65.edges_ref, ...), custom_call_target="tpu_custom_call" | custom-call | tf_op jit(solution)/shard_map/pallas_call | solution.py:664
  147.5 3.8 %all-to-all-start.4 = ((bf16[8,32,512]{2,1,0:T(8,128)(2,1)}), bf16[8,32,512]{2,1,0:T(8,128)(2,1)S(1)}, u32[]{:S(2)}, u32[]{:S(2)}) async-start(bf16[8,32,512]{2,1,0:T(8,128)(2,1)} %bitcast.59), calls=%async_computation.4 | async-start | bytes 524288 | tf_op jit(solution)/shard_map/all_to_all | solution.py:461
  154.9 5.3 %all-to-all-done.4 = bf16[8,32,512]{2,1,0:T(8,128)(2,1)S(1)} async-done(((bf16[8,32,512]{2,1,0:T(8,128)(2,1)}), bf16[8,32,512]{2,1,0:T(8,128)(2,1)S(1)}, u32[]{:S(2)}, u32[]{:S(2)}) %all-to-all-start.4) | async-done | bytes 262176 | tf_op jit(solution)/shard_map/all_to_all | solution.py:461
  179.5 4.8 %collective-permute-done.19 = bf16[352,512]{1,0:T(8,128)(2,1)S(1)} collective-permute-done((bf16[352,512]{1,0:T(8,128)(2,1)S(1)}, bf16[352,512]{1,0:T(8,128)(2,1)S(1)}, u32[]{:S(2)}, u32[]{:S(2)}) %collective-permute-start.19) | collective-permute-done | bytes 360480 | tf_op jit(solution)/shard_map/ppermute | solution.py:411
  189.3 5.3 %collective-permute-done.20 = bf16[176,512]{1,0:T(8,128)(2,1)S(1)} collective-permute-done((bf16[176,512]{1,0:T(8,128)(2,1)S(1)}, bf16[176,512]{1,0:T(8,128)(2,1)S(1)}, u32[]{:S(2)}, u32[]{:S(2)}) %collective-permute-start.20) | collective-permute-done | bytes 180256 | tf_op jit(solution)/shard_map/ppermute | solution.py:411
  197.9 7.3 %collective-permute-done.21 = bf16[176,512]{1,0:T(8,128)(2,1)S(1)} collective-permute-done((bf16[176,512]{1,0:T(8,128)(2,1)S(1)}, bf16[176,512]{1,0:T(8,128)(2,1)S(1)}, u32[]{:S(2)}, u32[]{:S(2)}) %collective-permute-start.21) | collective-permute-done | bytes 180256 | tf_op jit(solution)/shard_map/ppermute | solution.py:411
  207.3 7.2 %collective-permute-done.14 = bf16[56,512]{1,0:T(8,128)(2,1)S(1)} collective-permute-done((bf16[56,512]{1,0:T(8,128)(2,1)S(1)}, bf16[56,512]{1,0:T(8,128)(2,1)S(1)}, u32[]{:S(2)}, u32[]{:S(2)}) %collective-permute-start.14) | collective-permute-done | bytes 57376 | tf_op jit(solution)/shard_map/ppermute | solution.py:411
  214.5 3.4 %collective-permute-start.15 = (bf16[56,512]{1,0:T(8,128)(2,1)S(1)}, bf16[56,512]{1,0:T(8,128)(2,1)S(1)}, u32[]{:S(2)}, u32[]{:S(2)}) collective-permute-start(bf16[56,512]{1,0:T(8,128)(2,1)S(1)} %get-tuple-element.145), channel_id=1, source_target_pairs={{0,16},{4,20},{8,24},{12,28},{16,0},{20,4},{24,8},{28,12},{1,17},{... | collective-permute-start | bytes 172040 | tf_op jit(solution)/shard_map/ppermute | solution.py:411
  225.9 13.9 %collective-permute-done.17 = bf16[224,512]{1,0:T(8,128)(2,1)S(1)} collective-permute-done((bf16[224,512]{1,0:T(8,128)(2,1)S(1)}, bf16[224,512]{1,0:T(8,128)(2,1)S(1)}, u32[]{:S(2)}, u32[]{:S(2)}) %collective-permute-start.17) | collective-permute-done | bytes 229408 | tf_op jit(solution)/shard_map/ppermute | solution.py:411
  (199 shorter events, 74.9 us)
Async XLA Ops:
  24.1 11.6 %all-to-all-start.1 = ((bf16[8,32,512]{2,1,0:T(8,128)(2,1)}), bf16[8,32,512]{2,1,0:T(8,128)(2,1)S(1)}, u32[]{:S(2)}, u32[]{:S(2)}) async-start(bf16[8,32,512]{2,1,0:T(8,128)(2,1)} %bitcast.4), calls=%async_computation.1 | async-start | bytes 524288 | tf_op jit(solution)/shard_map/all_to_all | solution.py:461
  53.8 8.1 %collective-permute-start.1 = (bf16[192,512]{1,0:T(8,128)(2,1)S(1)}, bf16[192,512]{1,0:T(8,128)(2,1)S(1)}, u32[]{:S(2)}, u32[]{:S(2)}) collective-permute-start(bf16[192,512]{1,0:T(8,128)(2,1)S(1)} %add_convert_fusion.7.sum_a), channel_id=1, source_target_pairs={{0,2},{1,3},{2,0},{3,1},{4,6},{5,7},{6,4},{7,5},{8,10},{9,11},{10,... | collective-permute-start | bytes 589832 | tf_op jit(solution)/shard_map/ppermute | solution.py:411
  55.5 6.4 %collective-permute-start.3 = (bf16[192,128]{1,0:T(8,128)(2,1)S(1)}, bf16[192,128]{1,0:T(8,128)(2,1)S(1)}, u32[]{:S(2)}, u32[]{:S(2)}) collective-permute-start(bf16[192,128]{1,0:T(8,128)(2,1)S(1)} %add_convert_fusion.12.count_a), channel_id=1, source_target_pairs={{0,2},{1,3},{2,0},{3,1},{4,6},{5,7},{6,4},{7,5},{8,10},{9,11},{10,... | collective-permute-start | bytes 147464 | tf_op jit(solution)/shard_map/ppermute | solution.py:411
  68.7 12.0 %all-to-all-start.2 = ((bf16[8,32,512]{2,1,0:T(8,128)(2,1)}), bf16[8,32,512]{2,1,0:T(8,128)(2,1)S(1)}, u32[]{:S(2)}, u32[]{:S(2)}) async-start(bf16[8,32,512]{2,1,0:T(8,128)(2,1)} %bitcast.58), calls=%async_computation.2 | async-start | bytes 524288 | tf_op jit(solution)/shard_map/all_to_all | solution.py:461
  100.1 14.0 %collective-permute-start.6 = (bf16[2,416,192]{2,1,0:T(8,128)(2,1)S(1)}, bf16[2,416,192]{2,1,0:T(8,128)(2,1)S(1)}, u32[]{:S(2)}, u32[]{:S(2)}) collective-permute-start(bf16[2,416,192]{2,1,0:T(8,128)(2,1)S(1)} %constant_dynamic-slice_fusion.11), channel_id=1, source_target_pairs={{0,1},{1,0},{2,3},{3,2},{4,5},{5,4},{6,7},{7,6},{8,9},{9,8},{10,11... | collective-permute-start | bytes 958472 | tf_op jit(solution)/shard_map/ppermute | solution.py:411
  100.2 11.2 %all-to-all-start.3 = ((bf16[8,32,192]{2,1,0:T(8,128)(2,1)}), bf16[8,32,192]{2,1,0:T(8,128)(2,1)S(1)}, u32[]{:S(2)}, u32[]{:S(2)}) async-start(bf16[8,32,192]{2,1,0:T(8,128)(2,1)} %bitcast.60), calls=%async_computation.3 | async-start | bytes 262144 | tf_op jit(solution)/shard_map/all_to_all | solution.py:461
  114.3 8.1 %collective-permute-start.7 = (bf16[1,416,192]{2,1,0:T(8,128)(2,1)S(1)}, bf16[1,416,192]{2,1,0:T(8,128)(2,1)S(1)}, u32[]{:S(2)}, u32[]{:S(2)}) collective-permute-start(bf16[1,416,192]{2,1,0:T(8,128)(2,1)S(1)} %constant_dynamic-slice_fusion.10), channel_id=1, source_target_pairs={{0,2},{1,3},{2,0},{3,1},{4,6},{5,7},{6,4},{7,5},{8,10},{9,11},{10,... | collective-permute-start | bytes 479240 | tf_op jit(solution)/shard_map/ppermute | solution.py:411
  115.9 9.2 %collective-permute-start.5 = (bf16[192,384]{1,0:T(8,128)(2,1)S(1)}, bf16[192,384]{1,0:T(8,128)(2,1)S(1)}, u32[]{:S(2)}, u32[]{:S(2)}) collective-permute-start(bf16[192,384]{1,0:T(8,128)(2,1)S(1)} %add_convert_fusion.9.back_a), channel_id=1, source_target_pairs={{0,2},{1,3},{2,0},{3,1},{4,6},{5,7},{6,4},{7,5},{8,10},{9,11},{10,... | collective-permute-start | bytes 442376 | tf_op jit(solution)/shard_map/ppermute | solution.py:411
  147.5 12.7 %all-to-all-start.4 = ((bf16[8,32,512]{2,1,0:T(8,128)(2,1)}), bf16[8,32,512]{2,1,0:T(8,128)(2,1)S(1)}, u32[]{:S(2)}, u32[]{:S(2)}) async-start(bf16[8,32,512]{2,1,0:T(8,128)(2,1)} %bitcast.59), calls=%async_computation.4 | async-start | bytes 524288 | tf_op jit(solution)/shard_map/all_to_all | solution.py:461
  152.2 20.5 %collective-permute-start.18 = (bf16[704,512]{1,0:T(8,128)(2,1)}, bf16[704,512]{1,0:T(8,128)(2,1)}, u32[]{:S(2)}, u32[]{:S(2)}) collective-permute-start(bf16[704,512]{1,0:T(8,128)(2,1)} %constant_dynamic-slice_fusion.4), channel_id=1, source_target_pairs={{0,4},{4,0},{8,12},{12,8},{16,20},{20,16},{24,28},{28,24},{1,5},{5... | collective-permute-start | bytes 2162696 | tf_op jit(solution)/shard_map/ppermute | solution.py:411
  154.9 20.7 %collective-permute-start.10 = (bf16[2,448,512]{2,1,0:T(8,128)(2,1)}, bf16[2,448,512]{2,1,0:T(8,128)(2,1)}, u32[]{:S(2)}, u32[]{:S(2)}) collective-permute-start(bf16[2,448,512]{2,1,0:T(8,128)(2,1)} %constant_dynamic-slice_fusion.9), channel_id=1, source_target_pairs={{0,1},{1,0},{2,3},{3,2},{4,5},{5,4},{6,7},{7,6},{8,9},{9,8},{10,11... | collective-permute-start | bytes 2752520 | tf_op jit(solution)/shard_map/ppermute | solution.py:411
  163.9 6.5 %collective-permute-start.8 = (bf16[192,512]{1,0:T(8,128)(2,1)}, bf16[192,512]{1,0:T(8,128)(2,1)S(1)}, u32[]{:S(2)}, u32[]{:S(2)}) collective-permute-start(bf16[192,512]{1,0:T(8,128)(2,1)} %shard_map.474), channel_id=1, source_target_pairs={{0,1},{1,0},{2,3},{3,2},{4,5},{5,4},{6,7},{7,6},{8,9},{9,8},{10,11... | collective-permute-start | bytes 589832 | tf_op jit(solution)/shard_map/ppermute | solution.py:411
  170.5 8.2 %collective-permute-start.9 = (bf16[192,512]{1,0:T(8,128)(2,1)S(1)}, bf16[192,512]{1,0:T(8,128)(2,1)S(1)}, u32[]{:S(2)}, u32[]{:S(2)}) collective-permute-start(bf16[192,512]{1,0:T(8,128)(2,1)S(1)} %add_convert_fusion.6), channel_id=1, source_target_pairs={{0,2},{1,3},{2,0},{3,1},{4,6},{5,7},{6,4},{7,5},{8,10},{9,11},{10,... | collective-permute-start | bytes 589832 | tf_op jit(solution)/shard_map/ppermute | solution.py:411
  174.1 10.1 %collective-permute-start.19 = (bf16[352,512]{1,0:T(8,128)(2,1)S(1)}, bf16[352,512]{1,0:T(8,128)(2,1)S(1)}, u32[]{:S(2)}, u32[]{:S(2)}) collective-permute-start(bf16[352,512]{1,0:T(8,128)(2,1)S(1)} %constant_dynamic-slice_fusion.3), channel_id=1, source_target_pairs={{0,8},{4,12},{8,0},{12,4},{16,24},{20,28},{24,16},{28,20},{1,9},{5... | collective-permute-start | bytes 1081352 | tf_op jit(solution)/shard_map/ppermute | solution.py:411
  177.1 11.9 %collective-permute-start.11 = (bf16[1,448,512]{2,1,0:T(8,128)(2,1)S(1)}, bf16[1,448,512]{2,1,0:T(8,128)(2,1)S(1)}, u32[]{:S(2)}, u32[]{:S(2)}) collective-permute-start(bf16[1,448,512]{2,1,0:T(8,128)(2,1)S(1)} %constant_dynamic-slice_fusion.8), channel_id=1, source_target_pairs={{0,2},{1,3},{2,0},{3,1},{4,6},{5,7},{6,4},{7,5},{8,10},{9,11},{10,... | collective-permute-start | bytes 1376264 | tf_op jit(solution)/shard_map/ppermute | solution.py:411
  184.4 10.2 %collective-permute-start.20 = (bf16[176,512]{1,0:T(8,128)(2,1)S(1)}, bf16[176,512]{1,0:T(8,128)(2,1)S(1)}, u32[]{:S(2)}, u32[]{:S(2)}) collective-permute-start(bf16[176,512]{1,0:T(8,128)(2,1)S(1)} %constant_dynamic-slice_fusion.2), channel_id=1, source_target_pairs={{0,16},{4,20},{8,24},{12,28},{16,0},{20,4},{24,8},{28,12},{1,17},{... | collective-permute-start | bytes 540680 | tf_op jit(solution)/shard_map/ppermute | solution.py:411
  189.1 6.1 %collective-permute-start.12 = (bf16[224,512]{1,0:T(8,128)(2,1)S(1)}, bf16[224,512]{1,0:T(8,128)(2,1)S(1)}, u32[]{:S(2)}, u32[]{:S(2)}) collective-permute-start(bf16[224,512]{1,0:T(8,128)(2,1)S(1)} %dynamic-slice_bitcast_fusion), channel_id=1, source_target_pairs={{0,4},{4,0},{8,12},{12,8},{16,20},{20,16},{24,28},{28,24},{1,5},{5... | collective-permute-start | bytes 688136 | tf_op jit(solution)/shard_map/ppermute | solution.py:411
  194.6 10.6 %collective-permute-start.21 = (bf16[176,512]{1,0:T(8,128)(2,1)S(1)}, bf16[176,512]{1,0:T(8,128)(2,1)S(1)}, u32[]{:S(2)}, u32[]{:S(2)}) collective-permute-start(bf16[176,512]{1,0:T(8,128)(2,1)S(1)} %get-tuple-element.143), channel_id=1, source_target_pairs={{0,16},{4,20},{8,24},{12,28},{16,0},{20,4},{24,8},{28,12},{1,17},{... | collective-permute-start | bytes 540680 | tf_op jit(solution)/shard_map/ppermute | solution.py:411
  195.3 10.0 %collective-permute-start.13 = (bf16[112,512]{1,0:T(8,128)(2,1)S(1)}, bf16[112,512]{1,0:T(8,128)(2,1)S(1)}, u32[]{:S(2)}, u32[]{:S(2)}) collective-permute-start(bf16[112,512]{1,0:T(8,128)(2,1)S(1)} %constant_dynamic-slice_fusion.7), channel_id=1, source_target_pairs={{0,8},{4,12},{8,0},{12,4},{16,24},{20,28},{24,16},{28,20},{1,9},{5... | collective-permute-start | bytes 344072 | tf_op jit(solution)/shard_map/ppermute | solution.py:411
  205.2 12.8 %collective-permute-start.22 = (bf16[352,512]{1,0:T(8,128)(2,1)S(1)}, bf16[352,512]{1,0:T(8,128)(2,1)S(1)}, u32[]{:S(2)}, u32[]{:S(2)}) collective-permute-start(bf16[352,512]{1,0:T(8,128)(2,1)S(1)} %constant_dynamic-update-slice_fusion.4), channel_id=1, source_target_pairs={{0,8},{4,12},{8,0},{12,4},{16,24},{20,28},{24,16},{28,20},{1,9},{5... | collective-permute-start | bytes 1081352 | tf_op jit(solution)/shard_map/ppermute | solution.py:411
  205.4 9.1 %collective-permute-start.14 = (bf16[56,512]{1,0:T(8,128)(2,1)S(1)}, bf16[56,512]{1,0:T(8,128)(2,1)S(1)}, u32[]{:S(2)}, u32[]{:S(2)}) collective-permute-start(bf16[56,512]{1,0:T(8,128)(2,1)S(1)} %constant_dynamic-slice_fusion.6), channel_id=1, source_target_pairs={{0,16},{4,20},{8,24},{12,28},{16,0},{20,4},{24,8},{28,12},{1,17},{... | collective-permute-start | bytes 172040 | tf_op jit(solution)/shard_map/ppermute | solution.py:411
  214.5 5.8 %collective-permute-start.15 = (bf16[56,512]{1,0:T(8,128)(2,1)S(1)}, bf16[56,512]{1,0:T(8,128)(2,1)S(1)}, u32[]{:S(2)}, u32[]{:S(2)}) collective-permute-start(bf16[56,512]{1,0:T(8,128)(2,1)S(1)} %get-tuple-element.145), channel_id=1, source_target_pairs={{0,16},{4,20},{8,24},{12,28},{16,0},{20,4},{24,8},{28,12},{1,17},{... | collective-permute-start | bytes 172040 | tf_op jit(solution)/shard_map/ppermute | solution.py:411
  218.0 24.5 %collective-permute-start.23 = (bf16[704,512]{1,0:T(8,128)(2,1)S(1)}, bf16[704,512]{1,0:T(8,128)(2,1)S(1)}, u32[]{:S(2)}, u32[]{:S(2)}) collective-permute-start(bf16[704,512]{1,0:T(8,128)(2,1)S(1)} %constant_dynamic-update-slice_fusion.2), channel_id=1, source_target_pairs={{0,4},{4,0},{8,12},{12,8},{16,20},{20,16},{24,28},{28,24},{1,5},{5... | collective-permute-start | bytes 2162696 | tf_op jit(solution)/shard_map/ppermute | solution.py:411
  225.2 14.6 %collective-permute-start.17 = (bf16[224,512]{1,0:T(8,128)(2,1)S(1)}, bf16[224,512]{1,0:T(8,128)(2,1)S(1)}, u32[]{:S(2)}, u32[]{:S(2)}) collective-permute-start(bf16[224,512]{1,0:T(8,128)(2,1)S(1)} %constant_dynamic-update-slice_fusion.8), channel_id=1, source_target_pairs={{0,4},{4,0},{8,12},{12,8},{16,20},{20,16},{24,28},{28,24},{1,5},{5... | collective-permute-start | bytes 688136 | tf_op jit(solution)/shard_map/ppermute | solution.py:411
  (41 other events, 203.0 us)

commit v2 on v1

v2 whole, which is shorter than its diff:
```python
import functools

import jax
import jax.numpy as jnp
from jax import lax
from jax.experimental import pallas as pl
from jax.experimental.pallas import tpu as pltpu
from jax.sharding import PartitionSpec as P

D = 512
E = 192
FF = 2048
FAR = 32
SLOT = 16
KT = 5
VMEM = 32 * 1024 * 1024

bf16 = jnp.bfloat16
f32 = jnp.float32


def mm(a, b):
    return jnp.dot(a, b, preferred_element_type=f32)


def mm_tn(a, b):
    return lax.dot_general(a, b, (((0,), (0,)), ((), ())), preferred_element_type=f32)


def mm_nt(a, b):
    return lax.dot_general(a, b, (((1,), (1,)), ((), ())), preferred_element_type=f32)


def gelu_pair(v):
    c0 = 0.7978845608028654
    c1 = 0.044715 * c0
    square = v * v
    t = jnp.tanh(v * (c0 + c1 * square))
    half = 0.5 + 0.5 * t
    act = v * half
    return act, half + act * (1.0 - t) * (c0 + (3.0 * c1) * square)


def norm_forward(values):
    centred = values - jnp.mean(values, axis=-1, keepdims=True)
    inverse = lax.rsqrt(jnp.mean(centred * centred, axis=-1, keepdims=True) + 1e-05)
    return centred * inverse, inverse


def norm_backward(upstream, normed, inverse, gain):
    scaled = upstream * gain
    first = jnp.mean(scaled, axis=-1, keepdims=True)
    second = jnp.mean(scaled * normed, axis=-1, keepdims=True)
    return inverse * (scaled - first - normed * second)


def row_of(ref):
    return ref[...].astype(f32).reshape(1, ref.shape[0])


def column_sum(values):
    return jnp.sum(values, axis=0, keepdims=True)


def iota(shape, dim):
    return lax.broadcasted_iota(jnp.int32, shape, dim)


def present_column(mask_ref, rows):
    real = jnp.sum(mask_ref[...].astype(f32), axis=1, keepdims=True)
    return (iota((rows, 1), 0).astype(f32) < real).astype(f32)


def pick_matrix(want_ref, rows):
    want = want_ref[...][:, :1].astype(f32)
    return (want == iota((want.shape[0], rows), 1).astype(f32)).astype(bf16)


def one_hot(column, width):
    return (column == iota((column.shape[0], width), 1)).astype(bf16)


def columns_of(col_ref, first, count):
    values = col_ref[...]
    lane = iota(values.shape, 1)
    return [
        jnp.sum(jnp.where(lane == first + j, values, 0.0), axis=1, keepdims=True).astype(jnp.int32)
        for j in range(count)
    ]


def kept_weight(columns):
    return jnp.concatenate([(column >= 0).astype(f32) for column in columns], axis=0)


def spread(rows, values):
    n, c = rows.shape
    return (values.reshape(-1, n, c) + rows[None]).reshape(values.shape)


def gathered(values, n):
    return jnp.sum(values.reshape(-1, n, values.shape[1]), axis=0)


def slot_sums(row_ref, first, count, width, values, acc):
    n = row_ref.shape[1]
    for j in range(count):
        row = row_ref[pl.ds(first + j, 1), :]
        hot = (row == iota((width, n), 0)).astype(bf16)
        acc[...] += mm(hot, values[j * n : (j + 1) * n])


def index_kernel(blocks, me_ref, near_ref, mask_ref, row_ref, col_ref, want_ref, count_ref):
    kn, rows = near_ref.shape
    me = me_ref[0].astype(f32)
    lanes = max(16, blocks)
    index = near_ref[...].astype(f32)
    block = jnp.floor((index + 0.5) * (1.0 / rows))
    slot = index - block * rows
    local = block == me
    far_block = jnp.where(local, -1.0, block)
    real = jnp.sum(mask_ref[...].astype(f32), axis=1, keepdims=True)
    own_place = iota((kn, rows), 1).astype(f32)
    kept = jnp.logical_and(jnp.logical_or(jnp.logical_not(local), slot < real), own_place < real)
    slot_line = iota((rows, rows), 0).astype(f32)
    block_line = iota((lanes, rows), 0).astype(f32)
    hot_slot = [(slot[k : k + 1] == slot_line).astype(bf16) for k in range(kn)]
    hot_block = [(far_block[k : k + 1] == block_line).astype(bf16) for k in range(kn)]
    named = mm_nt(hot_block[0], hot_slot[0])
    for k in range(1, kn):
        named = named + mm_nt(hot_block[k], hot_slot[k])
    flags = (named > 0.0).astype(f32)
    before = (iota((rows, rows), 0) < iota((rows, rows), 1)).astype(bf16)
    rank = mm(flags.astype(bf16), before)
    key = jnp.where(flags > 0.0, rank, -1.0)[:blocks]
    key = jnp.broadcast_to(key[:, None, :], (blocks, FAR, rows)).reshape(blocks * FAR, rows)
    level = (iota((blocks * FAR, 1), 0) & (FAR - 1)).astype(f32)
    hit = (key == level).astype(f32)
    place_row = iota((blocks * FAR, rows), 1).astype(f32)
    want = jnp.sum(hit * place_row, axis=1, keepdims=True)
    found = jnp.sum(hit, axis=1, keepdims=True)
    want = jnp.where(found > 0.0, want, 255.0)
    want_ref[...] = jnp.broadcast_to(want, want_ref.shape).astype(bf16)
    after = (iota((rows, rows), 0) > iota((rows, rows), 1)).astype(bf16)
    rank_down = mm_nt(after, flags.astype(bf16)).astype(bf16)
    edge_rank = jnp.concatenate(
        [
            jnp.sum(mm(rank_down, hot_block[k]) * hot_slot[k].astype(f32), axis=0, keepdims=True)
            for k in range(kn)
        ],
        axis=0,
    )
    place = jnp.where(local, blocks * FAR + slot, block * FAR + edge_rank)
    place = jnp.where(kept, place, -1.0)
    place = jnp.concatenate([place, jnp.full((SLOT - kn, rows), -1.0, f32)], axis=0)
    row_ref[...] = place.astype(jnp.int32)
    col_ref[...] = place.T
    counts = jnp.sum((col_ref[...] >= 0.0).astype(f32), axis=1, keepdims=True)
    count_ref[...] = jnp.broadcast_to(counts, count_ref.shape).astype(bf16)


def message_forward_kernel(
    col_ref, edges_ref, nodes_ref, far_ref, w1_ref, w2_ref, b1_ref, b2_ref,
    act1_ref, d1_ref, d2_ref, sum_ref, table, own, acc,
):
    step = pl.program_id(0)
    last = pl.num_programs(0) - 1
    kt, rows, _ = edges_ref.shape
    n_far = far_ref.shape[0]
    width = table.shape[0]

    @pl.when(step == 0)
    def _():
        weight = w1_ref[D : 2 * D, :]
        table[:n_far] = mm(far_ref[...], weight).astype(bf16)
        table[n_far:] = mm(nodes_ref[...], weight).astype(bf16)
        own[...] = mm(nodes_ref[...], w1_ref[:D, :]) + row_of(b1_ref)
        acc[...] = jnp.zeros_like(acc)

    edge = edges_ref[...].reshape(kt * rows, E)
    columns = columns_of(col_ref, step * kt, kt)
    hot = jnp.concatenate([one_hot(column, width) for column in columns], axis=0)
    pre1 = spread(own[...], mm(hot, table[...]) + mm(edge, w1_ref[2 * D :, :]))
    act, slope = gelu_pair(pre1)
    act1 = act.astype(bf16)
    act1_ref[...] = act1
    d1_ref[...] = slope.astype(bf16)
    act, slope = gelu_pair(mm(act1, w2_ref[...]) + row_of(b2_ref))
    weight = kept_weight(columns)
    d2_ref[...] = (slope * weight).astype(bf16)
    acc[...] += gathered(act.astype(bf16).astype(f32) * weight, rows)

    @pl.when(step == last)
    def _():
        sum_ref[...] = acc[...].astype(bf16)


def node_forward_kernel(
    sum_a, sum_b, count_a, count_b, nodes_ref, mask_ref, want_ref, w3_ref, f1_ref, f2_ref,
    b3_ref, gain1_ref, bias1_ref, fb1_ref, fb2_ref, gain2_ref, bias2_ref,
    total_ref, low_ref, normed1_ref, inv1_ref, hid_ref, slope_ref, normed2_ref, inv2_ref, sent_ref, send_ref,
):
    rows = nodes_ref.shape[0]
    present = present_column(mask_ref, rows)
    count = count_a[...].astype(f32) + count_b[...].astype(f32)
    count = count[:, :1]
    total = sum_a[...].astype(f32) + sum_b[...].astype(f32)
    high = total.astype(bf16)
    total_ref[...] = high
    rest = (total - high.astype(f32)).astype(bf16)
    summed = mm(high, w3_ref[...]) + mm(rest, w3_ref[...]) + count * row_of(b3_ref)
    mixed = nodes_ref[...].astype(f32) + summed / jnp.maximum(count, 1.0)
    normed, inverse = norm_forward(mixed)
    normed1_ref[...] = normed
    inv1_ref[...] = inverse
    first = normed * row_of(gain1_ref) + row_of(bias1_ref)
    low = first.astype(bf16)
    low_ref[...] = low
    act, slope = gelu_pair(mm(low, f1_ref[...]) + row_of(fb1_ref))
    act = act.astype(bf16)
    hid_ref[...] = act
    slope_ref[...] = slope.astype(bf16)
    branch = mm(act, f2_ref[...]) + row_of(fb2_ref)
    normed, inverse = norm_forward(first + branch)
    normed2_ref[...] = normed
    inv2_ref[...] = inverse
    sent = (present * (normed * row_of(gain2_ref) + row_of(bias2_ref))).astype(bf16)
    sent_ref[...] = sent
    send_ref[...] = mm(pick_matrix(want_ref, rows), sent).astype(bf16)


def edge_kernel(
    order, row_ref, col_ref, edges_ref, cot_ref, sent_ref, far_ref, w1_ref, w2_ref, w3_ref, b1_ref, b2_ref, b3_ref, gain_ref, shift_ref,
    out_ref, base_ref, own_ref, far_grad_ref, local_grad_ref, packed_ref,
    table, own, sums, w1_acc, w2_acc, w3_acc, bias_acc, own_acc,
):
    step = pl.program_id(0)
    last = pl.num_programs(0) - 1
    kt, rows, _ = edges_ref.shape
    n_far = far_ref.shape[0]
    width = table.shape[0]

    @pl.when(step == 0)
    def _():
        weight = w1_ref[:, D : 2 * D]
        table[:n_far] = mm_nt(far_ref[...], weight).astype(bf16)
        table[n_far:] = mm_nt(sent_ref[...], weight).astype(bf16)
        own[...] = mm_nt(sent_ref[...], w1_ref[:, :D]) + row_of(b1_ref)
        for acc in (sums, w1_acc, w2_acc, w3_acc, bias_acc, own_acc):
            acc[...] = jnp.zeros_like(acc)

    edge = edges_ref[...].reshape(kt * rows, E)
    cot = cot_ref[...].reshape(kt * rows, E)
    columns = columns_of(col_ref, step * kt, kt)
    hot = jnp.concatenate([one_hot(column, width) for column in columns], axis=0)
    edge_weight = w1_ref[:, 2 * D :]
    pre1 = spread(own[...], mm(hot, table[...]) + mm_nt(edge, edge_weight))
    act, slope1 = gelu_pair(pre1)
    act1 = act.astype(bf16)
    act, slope2 = gelu_pair(mm(act1, w2_ref[...]) + row_of(b2_ref))
    act2 = act.astype(bf16)
    branch = mm(act2, w3_ref[...]) + row_of(b3_ref)
    weight = kept_weight(columns)
    normed, inverse = norm_forward(edge.astype(f32) + branch)
    gain = row_of(gain_ref)
    out = weight * (normed * gain + row_of(shift_ref))
    out_ref[...] = out.astype(bf16).reshape(kt, rows, E)
    up = weight * cot.astype(f32)
    grad = norm_backward(up, normed, inverse, gain)
    low3 = grad.astype(bf16)
    w3_acc[...] += mm_tn(act2, low3)
    low2 = (slope2 * mm_nt(low3, w3_ref[...])).astype(bf16)
    w2_acc[...] += mm_tn(act1, low2)
    low1 = (slope1 * mm_nt(low2, w2_ref[...])).astype(bf16)
    w1_acc[...] += mm_tn(edge, low1)
    slot_sums(row_ref, step * kt, kt, width, low1, sums)
    base_ref[...] = grad + mm(low1, edge_weight)
    own_sum = gathered(low1.astype(f32), rows)
    own_acc[...] += own_sum
    row = iota((16, 1), 0)
    bias_acc[...] += (
        jnp.where(row == 0, column_sum(own_sum), 0.0)
        + jnp.where(row == 1, column_sum(low2.astype(f32)), 0.0)
        + jnp.where(row == 2, column_sum(low3.astype(f32)), 0.0)
        + jnp.where(row == 3, column_sum(up * normed), 0.0)
        + jnp.where(row == 4, column_sum(up), 0.0)
    )

    @pl.when(step == last)
    def _():
        total = sums[...]
        own_low = own_acc[...].astype(bf16)
        own_ref[...] = own_low
        far_grad_ref[...] = total[:n_far].astype(bf16)
        local_grad_ref[...] = total[n_far:].astype(bf16)
        sent = sent_ref[...]
        parts = len(order)
        first = (2 * D + E) // parts
        second = E // parts
        whole = jnp.concatenate(
            [
                mm_tn(sent, own_low),
                mm_tn(far_ref[...], total[:n_far].astype(bf16)) + mm_tn(sent, total[n_far:].astype(bf16)),
                w1_acc[...],
            ],
            axis=0,
        ).astype(bf16)
        second_w = w2_acc[...].astype(bf16)
        third_w = w3_acc[...].astype(bf16)
        bias = bias_acc[...].astype(bf16)
        for q, n in enumerate(order):
            packed_ref[q, :first, :] = whole[n * first : (n + 1) * first]
            packed_ref[q, first : first + second, :] = second_w[n * second : (n + 1) * second]
            packed_ref[q, first + second : first + 2 * second, :] = third_w[n * second : (n + 1) * second]
            packed_ref[q, first + 2 * second :, :] = bias


def returned_kernel(own_ref, local_ref, back_ref, want_ref, out_ref):
    rows = local_ref.shape[0]
    near = local_ref[...].astype(f32) + mm_tn(pick_matrix(want_ref, rows), back_ref[...])
    out_ref[...] = jnp.concatenate([own_ref[...], near.astype(bf16)], axis=1)


def returned_last_kernel(own_ref, local_ref, back_ref, want_ref, w1_ref, out_ref):
    rows = local_ref.shape[0]
    near = local_ref[...].astype(f32) + mm_tn(pick_matrix(want_ref, rows), back_ref[...])
    grad = mm_nt(own_ref[...], w1_ref[:D, :]) + mm_nt(near.astype(bf16), w1_ref[D : 2 * D, :])
    out_ref[...] = grad.astype(bf16)


def node_backward_kernel(
    parts, place_ref, back_a, back_b, count_a, count_b, cot_ref, mask_ref, total_ref, low_ref, normed1_ref, inv1_ref,
    hid_ref, slope_ref, normed2_ref, inv2_ref, ew1_ref, w3_ref, f1_ref, f2_ref, gain1_ref, gain2_ref, edge_part_ref,
    mixed_ref, up_ref, bias_ref, packed_ref, hid_grad,
):
    rows = cot_ref.shape[0]
    place = place_ref[0]
    present = present_column(mask_ref, rows)
    count = (count_a[...].astype(f32) + count_b[...].astype(f32))[:, :1]
    back = (back_a[...].astype(f32) + back_b[...].astype(f32)).astype(bf16)
    node_back = mm(back[:, :E], ew1_ref[:, :D]) + mm(back[:, E:], ew1_ref[:, D : 2 * D])
    up = present * (cot_ref[...].astype(f32) + node_back)
    normed2 = normed2_ref[...]
    sum_grad = norm_backward(up, normed2, inv2_ref[...], row_of(gain2_ref))
    branch_grad = sum_grad.astype(bf16)
    hidden_grad = (slope_ref[...].astype(f32) * mm_nt(branch_grad, f2_ref[...])).astype(bf16)
    first_grad = sum_grad + mm_nt(hidden_grad, f1_ref[...])
    normed1 = normed1_ref[...]
    mixed_grad = norm_backward(first_grad, normed1, inv1_ref[...], row_of(gain1_ref))
    mixed_ref[...] = mixed_grad
    message_grad = (mixed_grad / jnp.maximum(count, 1.0)).astype(bf16)
    up_ref[...] = mm_nt(message_grad, w3_ref[...])
    row = iota((16, 1), 0)
    hidden_sum = column_sum(hidden_grad.astype(f32))
    bias = (
        jnp.where(row == 2, column_sum(count * message_grad.astype(f32)), 0.0)
        + jnp.where(row == 3, column_sum(first_grad * normed1), 0.0)
        + jnp.where(row == 4, column_sum(first_grad), 0.0)
        + jnp.where(row == 5, column_sum(branch_grad.astype(f32)), 0.0)
        + jnp.where(row == 6, column_sum(up * normed2), 0.0)
        + jnp.where(row == 7, column_sum(up), 0.0)
    )
    for j in range(FF // D):
        bias = bias + jnp.where(row == 8 + j, hidden_sum[:, j * D : (j + 1) * D], 0.0)
    bias_ref[...] = bias * (1.0 / parts)
    wide, narrow = FF // parts, D // parts
    low = low_ref[:, pl.ds(pl.multiple_of(place * narrow, narrow), narrow)]
    for j in range(FF // D):
        packed_ref[j * narrow : (j + 1) * narrow, :] = mm_tn(low, hidden_grad[:, j * D : (j + 1) * D]).astype(bf16)
    hid = hid_ref[:, pl.ds(pl.multiple_of(place * wide, wide), wide)]
    packed_ref[D : D + wide, :] = mm_tn(hid, branch_grad).astype(bf16)
    total = total_ref[:, pl.ds(pl.multiple_of(place * narrow, narrow), narrow)]
    packed_ref[D + wide : D + wide + narrow, :] = mm_tn(total, message_grad).astype(bf16)
    at = D + wide + narrow
    half = edge_part_ref.shape[0] // 2
    packed_ref[at:, :] = jnp.zeros((packed_ref.shape[0] - at, D), bf16)
    packed_ref[at : at + half, :E] = edge_part_ref[:half, :]
    packed_ref[at : at + half, 256 : 256 + E] = edge_part_ref[half:, :]


def message_backward_kernel(
    order, row_ref, edges_ref, act1_ref, d1_ref, d2_ref, up_ref, base_ref, nodes_ref, far_ref, w1_ref, w2_ref, node_bias_ref,
    out_ref, own_ref, far_grad_ref, local_grad_ref, packed_ref,
    sums, w1_acc, w2_acc, bias_acc, own_acc,
):
    step = pl.program_id(0)
    last = pl.num_programs(0) - 1
    kt, rows, _ = edges_ref.shape
    n_far = far_ref.shape[0]
    width = sums.shape[0]

    @pl.when(step == 0)
    def _():
        for acc in (sums, w1_acc, w2_acc, own_acc):
            acc[...] = jnp.zeros_like(acc)
        bias_acc[...] = node_bias_ref[...]

    edge = edges_ref[...].reshape(kt * rows, E)
    slope2 = d2_ref[...].astype(f32).reshape(kt, rows, D)
    low2 = (slope2 * up_ref[...][None]).astype(bf16).reshape(kt * rows, D)
    w2_acc[...] += mm_tn(act1_ref[...], low2)
    low1 = (d1_ref[...].astype(f32) * mm_nt(low2, w2_ref[...])).astype(bf16)
    w1_acc[...] += mm_tn(edge, low1)
    slot_sums(row_ref, step * kt, kt, width, low1, sums)
    grad = base_ref[...] + mm_nt(low1, w1_ref[2 * D :, :])
    out_ref[...] = grad.reshape(kt, rows, E)
    own_sum = gathered(low1.astype(f32), rows)
    own_acc[...] += own_sum
    row = iota((16, 1), 0)
    bias_acc[...] += jnp.where(row == 0, column_sum(own_sum), 0.0) + jnp.where(
        row == 1, column_sum(low2.astype(f32)), 0.0
    )

    @pl.when(step == last)
    def _():
        total = sums[...]
        own_low = own_acc[...].astype(bf16)
        own_ref[...] = own_low
        far_grad_ref[...] = total[:n_far].astype(bf16)
        local_grad_ref[...] = total[n_far:].astype(bf16)
        nodes = nodes_ref[...]
        parts = len(order)
        first = (2 * D + E) // parts
        second = D // parts
        whole = jnp.concatenate(
            [
                mm_tn(nodes, own_low),
                mm_tn(far_ref[...], total[:n_far].astype(bf16)) + mm_tn(nodes, total[n_far:].astype(bf16)),
                w1_acc[...],
            ],
            axis=0,
        ).astype(bf16)
        second_w = w2_acc[...].astype(bf16)
        bias = bias_acc[...].astype(bf16)
        for q, n in enumerate(order):
            packed_ref[q, :first, :] = whole[n * first : (n + 1) * first]
            packed_ref[q, first : first + second, :] = second_w[n * second : (n + 1) * second]
            packed_ref[q, first + second : first + second + 16, :] = bias
            if packed_ref.shape[1] > first + second + 16:
                packed_ref[q, first + second + 16 :, :] = jnp.zeros(
                    (packed_ref.shape[1] - first - second - 16, D), bf16
                )


def swap(values, axis, bit):
    return lax.ppermute(values, axis, [(i, i ^ bit) for i in range(lax.axis_size(axis))])


def bits_of(axis):
    size, bit, out = lax.axis_size(axis), 1, []
    while bit < size:
        out.append(bit)
        bit *= 2
    return out


def add_low(a, b):
    return (a.astype(f32) + b.astype(f32)).astype(bf16)


def shared_sum(values, axis):
    bits = bits_of(axis)
    for bit in bits[:-1]:
        values = add_low(values, swap(values, axis, bit))
    return values, swap(values, axis, bits[-1])


def halved_sum(values, axis, bit):
    half = values.shape[0] // 2
    side = (lax.axis_index(axis) // bit) & 1
    kept = lax.dynamic_slice_in_dim(values, side * half, half, 0)
    given = lax.dynamic_slice_in_dim(values, (1 - side) * half, half, 0)
    return add_low(kept, swap(given, axis, bit))


def rejoined(values, axis, bit):
    other = swap(values, axis, bit)
    side = (lax.axis_index(axis) // bit) & 1
    return jnp.where(
        side == 0, jnp.concatenate([values, other], axis=0), jnp.concatenate([other, values], axis=0)
    )


def scattered_sum(values, axis, bits):
    for bit in bits:
        values = halved_sum(values, axis, bit)
    return values


def gathered_rows(values, axis, bits):
    for bit in bits:
        values = rejoined(values, axis, bit)
    return values


def exchange(values, blocks):
    shaped = values.reshape((blocks, values.shape[0] // blocks) + values.shape[1:])
    return lax.all_to_all(shaped, "res", 0, 0, tiled=True).reshape(values.shape)


def call(kernel, outs, scratch=(), grid=None, in_specs=None, out_specs=None, cost=None):
    extra = {}
    if grid is not None:
        extra = dict(grid=grid, in_specs=in_specs, out_specs=out_specs)
    elif in_specs is not None:
        extra = dict(in_specs=in_specs)
    return pl.pallas_call(
        kernel,
        out_shape=outs,
        scratch_shapes=list(scratch),
        compiler_params=pltpu.CompilerParams(vmem_limit_bytes=VMEM),
        cost_estimate=cost,
        **extra,
    )


def shape(dims, dtype):
    return jax.ShapeDtypeStruct(dims, dtype)


def stored(dims, dtype):
    return pltpu.HBM(dims, dtype)


def read(*values):
    return tuple(pltpu.with_memory_space_constraint(value, pltpu.HBM) for value in values)


def up_to(value, unit):
    return -(-value // unit) * unit


def on_device(
    nodes,
    edges,
    neighbours,
    residue_mask,
    msg_w1,
    msg_b1,
    msg_w2,
    msg_b2,
    msg_w3,
    msg_b3,
    norm1_gain,
    norm1_bias,
    ffn_w1,
    ffn_b1,
    ffn_w2,
    ffn_b2,
    norm2_gain,
    norm2_bias,
    edge_w1,
    edge_b1,
    edge_w2,
    edge_b2,
    edge_w3,
    edge_b3,
    norm3_gain,
    norm3_bias,
    node_cot,
    edge_cot,
):
    rows, kn = neighbours.shape
    blocks, parts = lax.axis_size("res"), lax.axis_size("nbr")
    total = rows * kn
    n_far = blocks * FAR
    width = n_far + rows
    kt = next(t for t in (KT, 3, 1) if kn % t == 0)
    grid = (kn // kt,)
    nbr_bits = bits_of("nbr")
    order = tuple(
        sum(bit for i, bit in enumerate(nbr_bits) if (q >> (len(nbr_bits) - 1 - i)) & 1) for q in range(parts)
    )
    mask_row = residue_mask.reshape(1, rows)
    edges = edges.transpose(1, 0, 2)
    edge_cot = edge_cot.transpose(1, 0, 2)
    edge_w1 = edge_w1.T
    res_place = lax.axis_index("res").astype(jnp.int32).reshape(1)
    nbr_place = lax.axis_index("nbr").astype(jnp.int32).reshape(1)

    smem = pl.BlockSpec(memory_space=pltpu.SMEM)
    vmem = pl.BlockSpec(memory_space=pltpu.VMEM)

    def fixed(*dims):
        return pl.BlockSpec(dims, lambda i: (0,) * len(dims))

    def tiled(*dims):
        return pl.BlockSpec(dims, lambda i: (i,) + (0,) * (len(dims) - 1))

    place_row, place_col, want, counts = call(
        functools.partial(index_kernel, blocks),
        (
            shape((SLOT, rows), jnp.int32),
            shape((rows, SLOT), f32),
            shape((n_far, 128), bf16),
            shape((rows, 128), bf16),
        ),
        in_specs=[smem, vmem, vmem],
    )(res_place, neighbours.T, mask_row)
    together = lax.optimization_barrier
    wanted = exchange(want, blocks)

    picks = (wanted[:, :1].astype(jnp.int32) == iota((n_far, rows), 1)).astype(bf16)
    far_nodes = exchange(mm(picks, nodes).astype(bf16), blocks)
    far_nodes, counts = together((far_nodes, counts))
    count_a, count_b = shared_sum(counts, "nbr")

    edge_tile = tiled(kt, rows, E)
    flat = tiled(kt * rows, D)
    flat_edge = tiled(kt * rows, E)
    act1, d1, d2, act_sum = call(
        message_forward_kernel,
        (stored((total, D), bf16), stored((total, D), bf16), stored((total, D), bf16), shape((rows, D), bf16)),
        scratch=[pltpu.VMEM((width, D), bf16), pltpu.VMEM((rows, D), f32), pltpu.VMEM((rows, D), f32)],
        grid=grid,
        in_specs=[
            fixed(rows, SLOT),
            edge_tile,
            fixed(rows, D),
            fixed(n_far, D),
            fixed(2 * D + E, D),
            fixed(D, D),
            fixed(D),
            fixed(D),
        ],
        out_specs=(flat, flat, flat, fixed(rows, D)),
        cost=pl.CostEstimate(flops=16 * total * D * D, bytes_accessed=total * D * 8, transcendentals=2 * total * D),
    )(*read(place_col, edges, nodes), far_nodes, *read(msg_w1, msg_w2), msg_b1, msg_b2)
    sum_a, sum_b = shared_sum(act_sum, "nbr")

    total_act, first_low, normed1, inv1, hidden, hidden_slope, normed2, inv2, sent, send = call(
        node_forward_kernel,
        (
            stored((rows, D), bf16),
            stored((rows, D), bf16),
            stored((rows, D), f32),
            stored((rows, 1), f32),
            stored((rows, FF), bf16),
            stored((rows, FF), bf16),
            stored((rows, D), f32),
            stored((rows, 1), f32),
            stored((rows, D), bf16),
            shape((n_far, D), bf16),
        ),
    )(sum_a, sum_b, count_a, count_b, nodes, mask_row, wanted, msg_w3, ffn_w1, ffn_w2,
      msg_b3, norm1_gain, norm1_bias, ffn_b1, ffn_b2, norm2_gain, norm2_bias)
    far_sent = exchange(send, blocks)

    first_rows, second_rows = (2 * D + E) // parts, E // parts
    edge_rows = up_to(first_rows + 2 * second_rows + 16, 32)
    edges_out, base, own_sum, far_sum, local_sum, edge_packed = call(
        functools.partial(edge_kernel, order),
        (
            shape((kn, rows, E), bf16),
            stored((total, E), f32),
            stored((rows, E), bf16),
            shape((n_far, E), bf16),
            stored((rows, E), bf16),
            shape((parts, edge_rows, E), bf16),
        ),
        scratch=[
            pltpu.VMEM((width, E), bf16),
            pltpu.VMEM((rows, E), f32),
            pltpu.VMEM((width, E), f32),
            pltpu.VMEM((E, E), f32),
            pltpu.VMEM((E, E), f32),
            pltpu.VMEM((E, E), f32),
            pltpu.VMEM((16, E), f32),
            pltpu.VMEM((rows, E), f32),
        ],
        grid=grid,
        in_specs=[
            fixed(SLOT, rows),
            fixed(rows, SLOT),
            edge_tile,
            edge_tile,
            fixed(rows, D),
            fixed(n_far, D),
            fixed(E, 2 * D + E),
            fixed(E, E),
            fixed(E, E),
        ]
        + [fixed(E)] * 5,
        out_specs=(
            edge_tile,
            flat_edge,
            fixed(rows, E),
            fixed(n_far, E),
            fixed(rows, E),
            fixed(parts, edge_rows, E),
        ),
        cost=pl.CostEstimate(flops=16 * total * D * D, bytes_accessed=total * E * 12, transcendentals=2 * total * E),
    )(*read(place_row, place_col, edges, edge_cot, sent), far_sent, *read(edge_w1, edge_w2, edge_w3),
      edge_b1, edge_b2, edge_b3, norm3_gain, norm3_bias)

    far_back, edge_packed = together((exchange(far_sum, blocks), edge_packed))
    back = call(returned_kernel, shape((rows, 2 * E), bf16))(own_sum, local_sum, far_back, wanted)
    back_a, back_b = shared_sum(back, "nbr")
    edge_part = scattered_sum(edge_packed, "nbr", nbr_bits).reshape(edge_rows, E)

    wide, narrow = FF // parts, D // parts
    node_rows = up_to(D + wide + narrow + edge_rows // 2, 16 * blocks)
    mixed_grad, up, node_bias, node_packed = call(
        functools.partial(node_backward_kernel, parts),
        (
            shape((rows, D), f32),
            shape((rows, D), f32),
            shape((16, D), f32),
            shape((node_rows, D), bf16),
        ),
        scratch=[pltpu.VMEM((rows, FF), bf16)],
        in_specs=[smem] + [vmem] * 21,
    )(
        nbr_place, back_a, back_b, count_a, count_b, *read(node_cot), mask_row, *read(total_act, first_low, normed1, inv1),
        *read(hidden, hidden_slope, normed2, inv2, edge_w1), msg_w3, ffn_w1, ffn_w2, norm1_gain, norm2_gain, edge_part,
    )
    bits = bits_of("res")
    order_a, order_b = bits, bits[1:2] + bits[:1] + bits[2:]
    part_a = halved_sum(node_packed[: node_rows // 2], "res", order_a[0])
    part_b = halved_sum(node_packed[node_rows // 2 :], "res", order_b[0])

    msg_rows = up_to(first_rows + narrow + 16, 8 * blocks)
    edges_grad, own_sum, far_sum, local_sum, msg_packed = call(
        functools.partial(message_backward_kernel, order),
        (
            shape((kn, rows, E), f32),
            shape((rows, D), bf16),
            shape((n_far, D), bf16),
            shape((rows, D), bf16),
            shape((parts, msg_rows, D), bf16),
        ),
        scratch=[
            pltpu.VMEM((width, D), f32),
            pltpu.VMEM((E, D), f32),
            pltpu.VMEM((D, D), f32),
            pltpu.VMEM((16, D), f32),
            pltpu.VMEM((rows, D), f32),
        ],
        grid=grid,
        in_specs=[
            fixed(SLOT, rows),
            edge_tile,
            flat,
            flat,
            flat,
            fixed(rows, D),
            flat_edge,
            fixed(rows, D),
            fixed(n_far, D),
            fixed(2 * D + E, D),
            fixed(D, D),
            fixed(16, D),
        ],
        out_specs=(edge_tile, fixed(rows, D), fixed(n_far, D), fixed(rows, D), fixed(parts, msg_rows, D)),
        cost=pl.CostEstimate(flops=16 * total * D * D, bytes_accessed=total * D * 10, transcendentals=0),
    )(*read(place_row, edges, act1, d1, d2), up, *read(base, nodes), far_nodes, *read(msg_w1, msg_w2), node_bias)

    far_sum, msg_part, part_a, part_b = together((far_sum, msg_packed, part_a, part_b))
    msg_part = halved_sum(msg_part, "nbr", nbr_bits[0])
    part_a = halved_sum(part_a, "res", order_a[1])
    part_b = halved_sum(part_b, "res", order_b[1])
    far_sum, msg_part, part_a, part_b = together((far_sum, msg_part, part_a, part_b))
    msg_part = scattered_sum(msg_part, "nbr", nbr_bits[1:]).reshape(msg_rows, D)
    far_back = exchange(far_sum, blocks)
    part_a = scattered_sum(part_a, "res", order_a[2:])
    part_b = scattered_sum(part_b, "res", order_b[2:])
    far_back, msg_part, part_a, part_b = together((far_back, msg_part, part_a, part_b))
    msg_part = halved_sum(msg_part, "res", bits[0])
    back = call(returned_last_kernel, shape((rows, D), bf16))(own_sum, local_sum, far_back, wanted, msg_w1)
    for bit in nbr_bits[:-1]:
        back = add_low(back, swap(back, "nbr", bit))
    part_a = gathered_rows(part_a, "res", order_a[:1:-1])
    part_b = gathered_rows(part_b, "res", order_b[:1:-1])
    back, msg_part, part_a, part_b = together((back, msg_part, part_a, part_b))
    msg_part = scattered_sum(msg_part, "res", bits[1:-1])
    back_b = swap(back, "nbr", nbr_bits[-1])
    part_a = rejoined(part_a, "res", order_a[1])
    part_b = rejoined(part_b, "res", order_b[1])
    back, back_b, msg_part, part_a, part_b = together((back, back_b, msg_part, part_a, part_b))
    nodes_grad = mixed_grad + (back.astype(f32) + back_b.astype(f32))
    msg_part = add_low(msg_part, swap(msg_part, "res", bits[-1]))
    part_a = rejoined(part_a, "res", order_a[0])
    part_b = rejoined(part_b, "res", order_b[0])
    msg_part, part_a, part_b = together((msg_part, part_a, part_b))
    msg_share = gathered_rows(msg_part, "res", bits[-2::-1]).astype(f32)
    node_share = jnp.concatenate([part_a, part_b], axis=0).astype(f32)

    ffn_w1_grad = jnp.concatenate([node_share[j * narrow : (j + 1) * narrow] for j in range(FF // D)], axis=1)
    ffn_w2_grad = node_share[D : D + wide]
    at = D + wide + narrow
    msg_w3_grad = node_share[D + wide : at]
    half = edge_rows // 2
    edge_share = jnp.concatenate([node_share[at : at + half, :E], node_share[at : at + half, 256 : 256 + E]], axis=0)
    edge_w1_grad = edge_share[:first_rows]
    edge_w2_grad = edge_share[first_rows : first_rows + second_rows]
    edge_w3_grad = edge_share[first_rows + second_rows : first_rows + 2 * second_rows]
    place = lax.axis_index("nbr")
    edge_bias = edge_share[first_rows + 2 * second_rows : first_rows + 2 * second_rows + 8]
    edge_bias = lax.dynamic_slice_in_dim(edge_bias, place * second_rows, second_rows, 1)
    msg_w1_grad = msg_share[:first_rows]
    msg_w2_grad = msg_share[first_rows : first_rows + narrow]
    bias_all = msg_share[first_rows + narrow : first_rows + narrow + 16]
    bias = lax.dynamic_slice_in_dim(bias_all[:8], place * narrow, narrow, 1)
    ffn_b1_grad = lax.dynamic_index_in_dim(bias_all[8 : 8 + FF // D], place, 0, keepdims=False)
    return (
        sent,
        edges_out.transpose(1, 0, 2),
        nodes_grad,
        edges_grad.transpose(1, 0, 2),
        msg_w1_grad,
        bias[0],
        msg_w2_grad,
        bias[1],
        msg_w3_grad,
        bias[2],
        bias[3],
        bias[4],
        ffn_w1_grad,
        ffn_b1_grad,
        ffn_w2_grad,
        bias[5],
        bias[6],
        bias[7],
        edge_w1_grad,
        edge_bias[0],
        edge_w2_grad,
        edge_bias[1],
        edge_w3_grad,
        edge_bias[2],
        edge_bias[3],
        edge_bias[4],
    )


def solution(mesh):
    every = P()
    in_specs = (
        (P("res", None), P("res", "nbr", None), P("res", "nbr"), P("res"))
        + (every,) * 22
        + (P("res", None), P("res", "nbr", None))
    )
    matrix, vector = P("nbr", None), P("nbr")
    out_specs = (
        (P("res", None), P("res", "nbr", None), P("res", None), P("res", "nbr", None))
        + (matrix, vector) * 3
        + (vector, vector, matrix, vector, matrix, vector, vector, vector)
        + (matrix, vector) * 3
        + (vector, vector)
    )
    return jax.shard_map(on_device, mesh=mesh, in_specs=in_specs, out_specs=out_specs, check_vma=False)
```

time: 249 us -> 207 us (0.83)
  waiting for transfers between devices: 82.6 us -> 49.7 us
  blocking collectives: 14.2 us -> 36 us
  Pallas kernels: 70.9 us -> 53.8 us
  local copies, waits for them, and re-layouts: 29.3 us -> 14.7 us
    all_to_all x1 -> x3, blocking collectives: 14.2 us -> 36 us  [exchange(): return lax.all_to_all(shaped, 'res', 0, 0, tiled=True).reshape(values.shape)]
    ppermute x24 -> x29, waiting for transfers between devices: 61.2 us -> 39.7 us  [swap(): lax.ppermute(values, axis, [(i, i ^ bit) for i in range(lax.axis_size(axi...]
    unnamed x81 -> x75, local copies, waits for them, and re-layouts: 19.5 us -> 6.21 us
    all_to_all x4 -> x2, waiting for transfers between devices: 21.4 us -> 10.1 us  [exchange(): return lax.all_to_all(shaped, 'res', 0, 0, tiled=True).reshape(values.shape)]
    pallas_call x5, Pallas kernels: 58.3 us -> 47.2 us  [the longest x1 14.7 us: on_device(): call(functools.partial(edge_kernel, order), (shape((kn, rows, E), bf16),...]
    ppermute x24 -> x29, starting transfers between devices: 24.3 us -> 31.3 us  [swap(): lax.ppermute(values, axis, [(i, i ^ bit) for i in range(lax.axis_size(axi...]
    all_to_all x4 -> x2, starting transfers between devices: 14.4 us -> 7.44 us  [exchange(): return lax.all_to_all(shaped, 'res', 0, 0, tiled=True).reshape(values.shape)]
    pallas_call x1, Pallas kernels: 7.57 us -> 4.67 us  [on_device(): call(functools.partial(node_backward_kernel, parts), (shape((rows, D), f3...]
  transfers between devices with their start and end apart: 28 -> 31, of which waited for: 18 -> 21; matrix products, arithmetic and copies ran while one was open for 11% -> 6% of each run, Pallas kernels for 2% -> 7%
where the time goes in v2:
time: 207 us; the launch traced here: 206 us
  Pallas kernels  53.8 us (26%)
  waiting for transfers between devices  49.7 us (24%)
  starting transfers between devices  38.8 us (19%)
  blocking collectives  36 us (17%)
  local copies, waits for them, and re-layouts  14.7 us (7%)
  other arithmetic  10.6 us (5%)
    ppermute x29, waiting for transfers between devices, swap(): lax.ppermute(values, axis, [(i, i ^ bit) for i in range(lax.axis_size(axi...  39.7 us
    all_to_all x3, blocking collectives, exchange(): return lax.all_to_all(shaped, 'res', 0, 0, tiled=True).reshape(values.shape)  36 us
    ppermute x29, starting transfers between devices, swap(): lax.ppermute(values, axis, [(i, i ^ bit) for i in range(lax.axis_size(axi...  31.3 us
    pallas_call x1, Pallas kernels, on_device(): call(functools.partial(edge_kernel, order), (shape((kn, rows, E), bf16),...  14.7 us
    pallas_call x1, Pallas kernels, on_device(): call(message_forward_kernel, (stored((total, D), bf16), stored((total, D)...  13.8 us
    pallas_call x1, Pallas kernels, on_device(): call(functools.partial(message_backward_kernel, order), (shape((kn, rows,...  12.6 us
    all_to_all x2, waiting for transfers between devices, exchange(): return lax.all_to_all(shaped, 'res', 0, 0, tiled=True).reshape(values.shape)  10.1 us
    all_to_all x2, starting transfers between devices, exchange(): return lax.all_to_all(shaped, 'res', 0, 0, tiled=True).reshape(values.shape)  7.44 us
  transfers between devices with their start and end apart: 31, of which 21 were waited for; matrix products, arithmetic and copies ran while one was open for 6% of the time, Pallas kernels for 7%

profile of v2, /device:TPU:0, one launch (start us, length us, event | category | flops | bytes accessed | tf_op | source)
XLA Modules:
  0.0 206.1 jit_solution(16254769114474278086)
XLA Ops:
  2.1 2.1 shard_map.467
  4.2 14.0 %all_to_all.25 = bf16[8,32,128]{2,1,0:T(8,128)(2,1)S(1)} all-to-all(bf16[8,32,128]{2,1,0:T(8,128)(2,1)S(1)} %bitcast.61), channel_id=1, replica_groups=mesh['res'=8,'nbr'=4] {'res'}, dimensions={0} | all-to-all | bytes 131072 | tf_op jit(solution)/shard_map/all_to_all | solution.py:498
  19.5 10.6 %all_to_all.26 = bf16[8,32,512]{2,1,0:T(8,128)(2,1)S(1)} all-to-all(bf16[8,32,512]{2,1,0:T(8,128)(2,1)S(1)} %bitcast.66), channel_id=1, replica_groups=mesh['res'=8,'nbr'=4] {'res'}, dimensions={0} | all-to-all | bytes 524288 | tf_op jit(solution)/shard_map/all_to_all | solution.py:498
  31.6 13.8 %shard_map.468 = (bf16[2880,512]{1,0:T(8,128)(2,1)}, bf16[2880,512]{1,0:T(8,128)(2,1)}, bf16[2880,512]{1,0:T(8,128)(2,1)}, bf16[192,512]{1,0:T(8,128)(2,1)S(1)}) custom-call(f32[192,16]{1,0:T(8,128)} %copy-done.25, bf16[15,192,192]{2,1,0:T(8,128)(2,1)} %bitcast.71, bf16[192,512]{1,0:T(8,128)(2,1)} %nodes_ref.5, bf16[256,512]{1,0:T(8,128)(2,1)S(1)} %bitcast.56, ...), custom_call_target="tpu_custom_call" | custom-call | flops 12079595520 | bytes 11796480 | tf_op jit(solution)/shard_map/pallas_call | solution.py:611
  49.1 5.8 %collective-permute-done.3.count_b = bf16[192,128]{1,0:T(8,128)(2,1)S(1)} collective-permute-done((bf16[192,128]{1,0:T(8,128)(2,1)S(1)}, bf16[192,128]{1,0:T(8,128)(2,1)S(1)}, u32[]{:S(2)}, u32[]{:S(2)}) %collective-permute-start.3) | collective-permute-done | bytes 49184 | tf_op jit(solution)/shard_map/ppermute | solution.py:446
  55.1 3.9 %shard_map.469 = (bf16[192,512]{1,0:T(8,128)(2,1)}, bf16[192,512]{1,0:T(8,128)(2,1)}, f32[192,512]{1,0:T(8,128)}, f32[192,1]{1,0:T(8,128)}, bf16[192,2048]{1,0:T...) custom-call(bf16[192,512]{1,0:T(8,128)(2,1)S(1)} %add_convert_fusion, ...), custom_call_target="tpu_custom_call" | custom-call | tf_op jit(solution)/shard_map/pallas_call | solution.py:631
  59.0 11.4 %all_to_all.27 = bf16[8,32,512]{2,1,0:T(8,128)(2,1)S(1)} all-to-all(bf16[8,32,512]{2,1,0:T(8,128)(2,1)S(1)} %bitcast.58), channel_id=1, replica_groups=mesh['res'=8,'nbr'=4] {'res'}, dimensions={0} | all-to-all | bytes 524288 | tf_op jit(solution)/shard_map/all_to_all | solution.py:498
  70.4 14.7 %shard_map.470 = (bf16[15,192,192]{2,1,0:T(8,128)(2,1)}, f32[2880,192]{1,0:T(8,128)}, bf16[192,192]{1,0:T(8,128)(2,1)}, bf16[256,192]{1,0:T(8,128)(2,1)S(1)}, bf...) custom-call(s32[16,192]{1,0:T(8,128)} %copy-done.26, f32[192,16]{1,0:T(8,128)} %copy-done.25, ...), custom_call_target="tpu_custom_call" | custom-call | flops 12079595520 | bytes 6635520 | tf_op jit(solution)/shard_map/pallas_call | solution.py:651
  85.8 4.0 %all-to-all-start.3 = ((bf16[8,32,192]{2,1,0:T(8,128)(2,1)}), bf16[8,32,192]{2,1,0:T(8,128)(2,1)}, u32[]{:S(2)}, u32[]{:S(2)}) async-start(bf16[8,32,192]{2,1,0:T(8,128)(2,1)} %bitcast.60), calls=%async_computation.3 | async-start | bytes 262144 | tf_op jit(solution)/shard_map/all_to_all | solution.py:498
  89.9 7.4 %all-to-all-done.3 = bf16[8,32,192]{2,1,0:T(8,128)(2,1)} async-done(((bf16[8,32,192]{2,1,0:T(8,128)(2,1)}), bf16[8,32,192]{2,1,0:T(8,128)(2,1)}, u32[]{:S(2)}, u32[]{:S(2)}) %all-to-all-start.3) | async-done | bytes 98336 | tf_op jit(solution)/shard_map/all_to_all | solution.py:498
  105.1 6.0 %collective-permute-done.7 = bf16[1,416,192]{2,1,0:T(8,128)(2,1)S(1)} collective-permute-done((bf16[1,416,192]{2,1,0:T(8,128)(2,1)S(1)}, bf16[1,416,192]{2,1,0:T(8,128)(2,1)S(1)}, u32[]{:S(2)}, u32[]{:S(2)}) %collective-permute-start.7) | collective-permute-done | bytes 159776 | tf_op jit(solution)/shard_map/ppermute | solution.py:446
  111.1 2.3 %collective-permute-done.5.back_b = bf16[192,384]{1,0:T(8,128)(2,1)S(1)} collective-permute-done((bf16[192,384]{1,0:T(8,128)(2,1)S(1)}, bf16[192,384]{1,0:T(8,128)(2,1)S(1)}, u32[]{:S(2)}, u32[]{:S(2)}) %collective-permute-start.5) | collective-permute-done | bytes 147488 | tf_op jit(solution)/shard_map/ppermute | solution.py:446
  113.4 4.7 %shard_map.472 = (f32[192,512]{1,0:T(8,128)S(1)}, f32[192,512]{1,0:T(8,128)S(1)}, f32[16,512]{1,0:T(8,128)S(1)}, bf16[1408,512]{1,0:T(8,128)(2,1)S(1)}) custom-call(s32[1]{0:T(128)} %bitcast.13.place_ref, bf16[192,384]{1,0:T(8,128)(2,1)S(1)} %add_convert_fusion.11.back_a, bf16[192,384]{1,0:T(8,128)(2,1)S(1)} %collective-permute-done.5.back_b, ...), custom_call_target="tpu_custom_call" | custom-call | tf_op jit(solution)/shard_map/pallas_call | solution.py:703
  119.6 12.6 %shard_map.473 = (f32[15,192,192]{2,1,0:T(8,128)}, bf16[192,512]{1,0:T(8,128)(2,1)S(1)}, bf16[256,512]{1,0:T(8,128)(2,1)}, bf16[192,512]{1,0:T(8,128)(2,1)S(1)}, bf16[4,448,512]{2,1,0:T(8,128)(2,1)S(1)}) custom-call(s32[16,192]{1,0:T(8,128)} %copy-done.26, bf16[15,192,192]{2,1,0:T(8,128)(2,1)} %bitcast.73, bf16[2880,512]{1,0:T(8,128)(2,1)} %get-tuple-element.112.act1_ref, ...), custom_call_target="tpu_custom_call" | custom-call | flops 12079595520 | bytes 14745600 | tf_op jit(solution)/shard_map/pallas_call | solution.py:723
  135.0 2.1 %collective-permute-start.11 = (bf16[176,512]{1,0:T(8,128)(2,1)S(1)}, bf16[176,512]{1,0:T(8,128)(2,1)S(1)}, u32[]{:S(2)}, u32[]{:S(2)}) collective-permute-start(bf16[176,512]{1,0:T(8,128)(2,1)S(1)} %constant_dynamic-slice_fusion.10), channel_id=1, source_target_pairs={{0,8},{4,12},{8,0},{12,4},{16,24},{20,28},{24,16},{28,20},{1,9},{5... | collective-permute-start | bytes 540680 | tf_op jit(solution)/shard_map/ppermute | solution.py:446
  137.0 4.5 %collective-permute-done.12 = bf16[176,512]{1,0:T(8,128)(2,1)} collective-permute-done((bf16[176,512]{1,0:T(8,128)(2,1)}, bf16[176,512]{1,0:T(8,128)(2,1)}, u32[]{:S(2)}, u32[]{:S(2)}) %collective-permute-start.12) | collective-permute-done | bytes 180256 | tf_op jit(solution)/shard_map/ppermute | solution.py:446
  147.2 2.1 collective-permute-start.14
  149.3 3.4 %all-to-all-start.4 = ((bf16[8,32,512]{2,1,0:T(8,128)(2,1)}), bf16[8,32,512]{2,1,0:T(8,128)(2,1)S(1)}, u32[]{:S(2)}, u32[]{:S(2)}) async-start(bf16[8,32,512]{2,1,0:T(8,128)(2,1)} %bitcast.17), calls=%async_computation.4 | async-start | bytes 524288 | tf_op jit(solution)/shard_map/all_to_all | solution.py:498
  158.3 2.7 %all-to-all-done.4 = bf16[8,32,512]{2,1,0:T(8,128)(2,1)S(1)} async-done(((bf16[8,32,512]{2,1,0:T(8,128)(2,1)}), bf16[8,32,512]{2,1,0:T(8,128)(2,1)S(1)}, u32[]{:S(2)}, u32[]{:S(2)}) %all-to-all-start.4) | async-done | bytes 262176 | tf_op jit(solution)/shard_map/all_to_all | solution.py:498
  166.2 2.8 %collective-permute-done.19 = bf16[88,512]{1,0:T(8,128)(2,1)S(1)} collective-permute-done((bf16[88,512]{1,0:T(8,128)(2,1)S(1)}, bf16[88,512]{1,0:T(8,128)(2,1)S(1)}, u32[]{:S(2)}, u32[]{:S(2)}) %collective-permute-start.19) | collective-permute-done | bytes 90144 | tf_op jit(solution)/shard_map/ppermute | solution.py:446
  180.9 2.2 %collective-permute-start.24 = (bf16[112,512]{1,0:T(8,128)(2,1)S(1)}, bf16[112,512]{1,0:T(8,128)(2,1)S(1)}, u32[]{:S(2)}, u32[]{:S(2)}) collective-permute-start(bf16[112,512]{1,0:T(8,128)(2,1)S(1)} %add_convert_fusion.13), channel_id=1, source_target_pairs={{0,16},{4,20},{8,24},{12,28},{16,0},{20,4},{24,8},{28,12},{1,17},{... | collective-permute-start | bytes 344072 | tf_op jit(solution)/shard_map/ppermute | solution.py:446
  183.9 2.9 %collective-permute-done.24 = bf16[112,512]{1,0:T(8,128)(2,1)S(1)} collective-permute-done((bf16[112,512]{1,0:T(8,128)(2,1)S(1)}, bf16[112,512]{1,0:T(8,128)(2,1)S(1)}, u32[]{:S(2)}, u32[]{:S(2)}) %collective-permute-start.24) | collective-permute-done | bytes 114720 | tf_op jit(solution)/shard_map/ppermute | solution.py:446
  190.2 4.1 %collective-permute-start.27 = (bf16[112,512]{1,0:T(8,128)(2,1)S(1)}, bf16[112,512]{1,0:T(8,128)(2,1)S(1)}, u32[]{:S(2)}, u32[]{:S(2)}) collective-permute-start(bf16[112,512]{1,0:T(8,128)(2,1)S(1)} %add_convert_fusion.12), channel_id=1, source_target_pairs={{0,8},{4,12},{8,0},{12,4},{16,24},{20,28},{24,16},{28,20},{1,9},{5... | collective-permute-start | bytes 344072 | tf_op jit(solution)/shard_map/ppermute | solution.py:446
  200.0 3.2 %collective-permute-done.28 = bf16[224,512]{1,0:T(8,128)(2,1)S(1)} collective-permute-done((bf16[224,512]{1,0:T(8,128)(2,1)S(1)}, bf16[224,512]{1,0:T(8,128)(2,1)S(1)}, u32[]{:S(2)}, u32[]{:S(2)}) %collective-permute-start.28) | collective-permute-done | bytes 229408 | tf_op jit(solution)/shard_map/ppermute | solution.py:446
  (181 shorter events, 61.7 us)
Async XLA Ops:
  46.9 8.1 %collective-permute-start.1 = (bf16[192,512]{1,0:T(8,128)(2,1)S(1)}, bf16[192,512]{1,0:T(8,128)(2,1)S(1)}, u32[]{:S(2)}, u32[]{:S(2)}) collective-permute-start(bf16[192,512]{1,0:T(8,128)(2,1)S(1)} %add_convert_fusion.8.sum_a), channel_id=1, source_target_pairs={{0,2},{1,3},{2,0},{3,1},{4,6},{5,7},{6,4},{7,5},{8,10},{9,11},{10,... | collective-permute-start | bytes 589832 | tf_op jit(solution)/shard_map/ppermute | solution.py:446
  48.5 6.4 %collective-permute-start.3 = (bf16[192,128]{1,0:T(8,128)(2,1)S(1)}, bf16[192,128]{1,0:T(8,128)(2,1)S(1)}, u32[]{:S(2)}, u32[]{:S(2)}) collective-permute-start(bf16[192,128]{1,0:T(8,128)(2,1)S(1)} %add_convert_fusion.16.count_a), channel_id=1, source_target_pairs={{0,2},{1,3},{2,0},{3,1},{4,6},{5,7},{6,4},{7,5},{8,10},{9,11},{10,... | collective-permute-start | bytes 147464 | tf_op jit(solution)/shard_map/ppermute | solution.py:446
  85.8 11.4 %all-to-all-start.3 = ((bf16[8,32,192]{2,1,0:T(8,128)(2,1)}), bf16[8,32,192]{2,1,0:T(8,128)(2,1)}, u32[]{:S(2)}, u32[]{:S(2)}) async-start(bf16[8,32,192]{2,1,0:T(8,128)(2,1)} %bitcast.60), calls=%async_computation.3 | async-start | bytes 262144 | tf_op jit(solution)/shard_map/all_to_all | solution.py:498
  102.9 8.2 %collective-permute-start.7 = (bf16[1,416,192]{2,1,0:T(8,128)(2,1)S(1)}, bf16[1,416,192]{2,1,0:T(8,128)(2,1)S(1)}, u32[]{:S(2)}, u32[]{:S(2)}) collective-permute-start(bf16[1,416,192]{2,1,0:T(8,128)(2,1)S(1)} %constant_dynamic-slice_fusion.14), channel_id=1, source_target_pairs={{0,2},{1,3},{2,0},{3,1},{4,6},{5,7},{6,4},{7,5},{8,10},{9,11},{10,... | collective-permute-start | bytes 479240 | tf_op jit(solution)/shard_map/ppermute | solution.py:446
  104.5 8.9 %collective-permute-start.5 = (bf16[192,384]{1,0:T(8,128)(2,1)S(1)}, bf16[192,384]{1,0:T(8,128)(2,1)S(1)}, u32[]{:S(2)}, u32[]{:S(2)}) collective-permute-start(bf16[192,384]{1,0:T(8,128)(2,1)S(1)} %add_convert_fusion.11.back_a), channel_id=1, source_target_pairs={{0,2},{1,3},{2,0},{3,1},{4,6},{5,7},{6,4},{7,5},{8,10},{9,11},{10,... | collective-permute-start | bytes 442376 | tf_op jit(solution)/shard_map/ppermute | solution.py:446
  118.2 14.1 %collective-permute-start.9 = (bf16[352,512]{1,0:T(8,128)(2,1)S(1)}, bf16[352,512]{1,0:T(8,128)(2,1)S(1)}, u32[]{:S(2)}, u32[]{:S(2)}) collective-permute-start(bf16[352,512]{1,0:T(8,128)(2,1)S(1)} %constant_dynamic-slice_fusion.12), channel_id=1, source_target_pairs={{0,8},{4,12},{8,0},{12,4},{16,24},{20,28},{24,16},{28,20},{1,9},{5... | collective-permute-start | bytes 1081352 | tf_op jit(solution)/shard_map/ppermute | solution.py:446
  118.3 14.1 %collective-permute-start.8 = (bf16[352,512]{1,0:T(8,128)(2,1)S(1)}, bf16[352,512]{1,0:T(8,128)(2,1)S(1)}, u32[]{:S(2)}, u32[]{:S(2)}) collective-permute-start(bf16[352,512]{1,0:T(8,128)(2,1)S(1)} %constant_dynamic-slice_fusion.13), channel_id=1, source_target_pairs={{0,4},{4,0},{8,12},{12,8},{16,20},{20,16},{24,28},{28,24},{1,5},{5... | collective-permute-start | bytes 1081352 | tf_op jit(solution)/shard_map/ppermute | solution.py:446
  133.5 9.0 %collective-permute-start.10 = (bf16[2,448,512]{2,1,0:T(8,128)(2,1)}, bf16[2,448,512]{2,1,0:T(8,128)(2,1)}, u32[]{:S(2)}, u32[]{:S(2)}) collective-permute-start(bf16[2,448,512]{2,1,0:T(8,128)(2,1)} %constant_dynamic-slice_fusion.11), channel_id=1, source_target_pairs={{0,1},{1,0},{2,3},{3,2},{4,5},{5,4},{6,7},{7,6},{8,9},{9,8},{10,11... | collective-permute-start | bytes 2752520 | tf_op jit(solution)/shard_map/ppermute | solution.py:446
  134.2 7.3 %collective-permute-start.12 = (bf16[176,512]{1,0:T(8,128)(2,1)}, bf16[176,512]{1,0:T(8,128)(2,1)}, u32[]{:S(2)}, u32[]{:S(2)}) collective-permute-start(bf16[176,512]{1,0:T(8,128)(2,1)} %constant_dynamic-slice_fusion.9), channel_id=1, source_target_pairs={{0,4},{4,0},{8,12},{12,8},{16,20},{20,16},{24,28},{28,24},{1,5},{5... | collective-permute-start | bytes 540680 | tf_op jit(solution)/shard_map/ppermute | solution.py:446
  135.0 7.5 %collective-permute-start.11 = (bf16[176,512]{1,0:T(8,128)(2,1)S(1)}, bf16[176,512]{1,0:T(8,128)(2,1)S(1)}, u32[]{:S(2)}, u32[]{:S(2)}) collective-permute-start(bf16[176,512]{1,0:T(8,128)(2,1)S(1)} %constant_dynamic-slice_fusion.10), channel_id=1, source_target_pairs={{0,8},{4,12},{8,0},{12,4},{16,24},{20,28},{24,16},{28,20},{1,9},{5... | collective-permute-start | bytes 540680 | tf_op jit(solution)/shard_map/ppermute | solution.py:446
  144.1 9.7 %collective-permute-start.15 = (bf16[88,512]{1,0:T(8,128)(2,1)S(1)}, bf16[88,512]{1,0:T(8,128)(2,1)S(1)}, u32[]{:S(2)}, u32[]{:S(2)}) collective-permute-start(bf16[88,512]{1,0:T(8,128)(2,1)S(1)} %constant_dynamic-slice_fusion.6), channel_id=1, source_target_pairs={{0,16},{4,20},{8,24},{12,28},{16,0},{20,4},{24,8},{28,12},{1,17},{... | collective-permute-start | bytes 270344 | tf_op jit(solution)/shard_map/ppermute | solution.py:446
  145.0 12.0 %collective-permute-start.13 = (bf16[1,448,512]{2,1,0:T(8,128)(2,1)S(1)}, bf16[1,448,512]{2,1,0:T(8,128)(2,1)}, u32[]{:S(2)}, u32[]{:S(2)}) collective-permute-start(bf16[1,448,512]{2,1,0:T(8,128)(2,1)S(1)} %constant_dynamic-slice_fusion.8), channel_id=1, source_target_pairs={{0,2},{1,3},{2,0},{3,1},{4,6},{5,7},{6,4},{7,5},{8,10},{9,11},{10,... | collective-permute-start | bytes 1376264 | tf_op jit(solution)/shard_map/ppermute | solution.py:446
  147.2 8.0 %collective-permute-start.14 = (bf16[88,512]{1,0:T(8,128)(2,1)}, bf16[88,512]{1,0:T(8,128)(2,1)}, u32[]{:S(2)}, u32[]{:S(2)}) collective-permute-start(bf16[88,512]{1,0:T(8,128)(2,1)} %constant_dynamic-slice_fusion.7), channel_id=1, source_target_pairs={{0,16},{4,20},{8,24},{12,28},{16,0},{20,4},{24,8},{28,12},{1,17},{... | collective-permute-start | bytes 270344 | tf_op jit(solution)/shard_map/ppermute | solution.py:446
  149.3 11.7 %all-to-all-start.4 = ((bf16[8,32,512]{2,1,0:T(8,128)(2,1)}), bf16[8,32,512]{2,1,0:T(8,128)(2,1)S(1)}, u32[]{:S(2)}, u32[]{:S(2)}) async-start(bf16[8,32,512]{2,1,0:T(8,128)(2,1)} %bitcast.17), calls=%async_computation.4 | async-start | bytes 524288 | tf_op jit(solution)/shard_map/all_to_all | solution.py:498
  161.1 7.9 %collective-permute-start.19 = (bf16[88,512]{1,0:T(8,128)(2,1)S(1)}, bf16[88,512]{1,0:T(8,128)(2,1)S(1)}, u32[]{:S(2)}, u32[]{:S(2)}) collective-permute-start(bf16[88,512]{1,0:T(8,128)(2,1)S(1)} %add_convert_fusion.14), channel_id=1, source_target_pairs={{0,16},{4,20},{8,24},{12,28},{16,0},{20,4},{24,8},{28,12},{1,17},{... | collective-permute-start | bytes 270344 | tf_op jit(solution)/shard_map/ppermute | solution.py:446
  161.9 8.0 %collective-permute-start.18 = (bf16[88,512]{1,0:T(8,128)(2,1)S(1)}, bf16[88,512]{1,0:T(8,128)(2,1)S(1)}, u32[]{:S(2)}, u32[]{:S(2)}) collective-permute-start(bf16[88,512]{1,0:T(8,128)(2,1)S(1)} %add_convert_fusion.15), channel_id=1, source_target_pairs={{0,16},{4,20},{8,24},{12,28},{16,0},{20,4},{24,8},{28,12},{1,17},{... | collective-permute-start | bytes 270344 | tf_op jit(solution)/shard_map/ppermute | solution.py:446
  164.0 6.1 %collective-permute-start.17 = (bf16[224,512]{1,0:T(8,128)(2,1)S(1)}, bf16[224,512]{1,0:T(8,128)(2,1)S(1)}, u32[]{:S(2)}, u32[]{:S(2)}) collective-permute-start(bf16[224,512]{1,0:T(8,128)(2,1)S(1)} %constant_dynamic-slice_fusion.5), channel_id=1, source_target_pairs={{0,4},{4,0},{8,12},{12,8},{16,20},{20,16},{24,28},{28,24},{1,5},{5... | collective-permute-start | bytes 688136 | tf_op jit(solution)/shard_map/ppermute | solution.py:446
  171.7 5.7 %collective-permute-start.22 = (bf16[176,512]{1,0:T(8,128)(2,1)S(1)}, bf16[176,512]{1,0:T(8,128)(2,1)S(1)}, u32[]{:S(2)}, u32[]{:S(2)}) collective-permute-start(bf16[176,512]{1,0:T(8,128)(2,1)S(1)} %maximum_select_fusion.6), channel_id=1, source_target_pairs={{0,8},{4,12},{8,0},{12,4},{16,24},{20,28},{24,16},{28,20},{1,9},{5... | collective-permute-start | bytes 540680 | tf_op jit(solution)/shard_map/ppermute | solution.py:446
  173.6 5.7 %collective-permute-start.20 = (bf16[192,512]{1,0:T(8,128)(2,1)S(1)}, bf16[192,512]{1,0:T(8,128)(2,1)S(1)}, u32[]{:S(2)}, u32[]{:S(2)}) collective-permute-start(bf16[192,512]{1,0:T(8,128)(2,1)S(1)} %add_convert_fusion.7), channel_id=1, source_target_pairs={{0,2},{1,3},{2,0},{3,1},{4,6},{5,7},{6,4},{7,5},{8,10},{9,11},{10,... | collective-permute-start | bytes 589832 | tf_op jit(solution)/shard_map/ppermute | solution.py:446
  179.3 9.1 %collective-permute-start.26 = (bf16[352,512]{1,0:T(8,128)(2,1)S(1)}, bf16[352,512]{1,0:T(8,128)(2,1)S(1)}, u32[]{:S(2)}, u32[]{:S(2)}) collective-permute-start(bf16[352,512]{1,0:T(8,128)(2,1)S(1)} %maximum_select_fusion.4), channel_id=1, source_target_pairs={{0,8},{4,12},{8,0},{12,4},{16,24},{20,28},{24,16},{28,20},{1,9},{5... | collective-permute-start | bytes 1081352 | tf_op jit(solution)/shard_map/ppermute | solution.py:446
  179.4 9.3 %collective-permute-start.25 = (bf16[352,512]{1,0:T(8,128)(2,1)S(1)}, bf16[352,512]{1,0:T(8,128)(2,1)S(1)}, u32[]{:S(2)}, u32[]{:S(2)}) collective-permute-start(bf16[352,512]{1,0:T(8,128)(2,1)S(1)} %maximum_select_fusion.3), channel_id=1, source_target_pairs={{0,4},{4,0},{8,12},{12,8},{16,20},{20,16},{24,28},{28,24},{1,5},{5... | collective-permute-start | bytes 1081352 | tf_op jit(solution)/shard_map/ppermute | solution.py:446
  180.9 5.8 %collective-permute-start.24 = (bf16[112,512]{1,0:T(8,128)(2,1)S(1)}, bf16[112,512]{1,0:T(8,128)(2,1)S(1)}, u32[]{:S(2)}, u32[]{:S(2)}) collective-permute-start(bf16[112,512]{1,0:T(8,128)(2,1)S(1)} %add_convert_fusion.13), channel_id=1, source_target_pairs={{0,16},{4,20},{8,24},{12,28},{16,0},{20,4},{24,8},{28,12},{1,17},{... | collective-permute-start | bytes 344072 | tf_op jit(solution)/shard_map/ppermute | solution.py:446
  190.2 6.8 %collective-permute-start.27 = (bf16[112,512]{1,0:T(8,128)(2,1)S(1)}, bf16[112,512]{1,0:T(8,128)(2,1)S(1)}, u32[]{:S(2)}, u32[]{:S(2)}) collective-permute-start(bf16[112,512]{1,0:T(8,128)(2,1)S(1)} %add_convert_fusion.12), channel_id=1, source_target_pairs={{0,8},{4,12},{8,0},{12,4},{16,24},{20,28},{24,16},{28,20},{1,9},{5... | collective-permute-start | bytes 344072 | tf_op jit(solution)/shard_map/ppermute | solution.py:446
  197.1 6.1 %collective-permute-start.28 = (bf16[224,512]{1,0:T(8,128)(2,1)S(1)}, bf16[224,512]{1,0:T(8,128)(2,1)S(1)}, u32[]{:S(2)}, u32[]{:S(2)}) collective-permute-start(bf16[224,512]{1,0:T(8,128)(2,1)S(1)} %maximum_select_fusion.5), channel_id=1, source_target_pairs={{0,4},{4,0},{8,12},{12,8},{16,20},{20,16},{24,28},{28,24},{1,5},{5... | collective-permute-start | bytes 688136 | tf_op jit(solution)/shard_map/ppermute | solution.py:446
  (44 other events, 553.7 us)

commit v3 on v2

--- a/solution.py
+++ b/solution.py
@@ -329,11 +329,29 @@
 
 
 def node_backward_kernel(
-    parts, place_ref, back_a, back_b, count_a, count_b, cot_ref, mask_ref, total_ref, low_ref, normed1_ref, inv1_ref,
-    hid_ref, slope_ref, normed2_ref, inv2_ref, ew1_ref, w3_ref, f1_ref, f2_ref, gain1_ref, gain2_ref, edge_part_ref,
-    mixed_ref, up_ref, bias_ref, packed_ref, hid_grad,
+    parts, place_ref, back_a, back_b, count_a, count_b, cot_ref, mask_ref, inv1_ref, normed2_ref, inv2_ref, ew1_ref,
+    gain1_ref, gain2_ref, f2_far, slope_far, f1_far, normed1_far, w3_far, low_far, hid_far, total_far,
+    mixed_ref, up_ref, bias_ref, packed_ref, w3_grad_ref,
+    f2_ref, slope_ref, f1_ref, normed1_ref, w3_ref, low_ref, hid_ref, total_ref, arrivals,
 ):
     rows = cot_ref.shape[0]
+    fetches = [
+        pltpu.make_async_copy(source, target, arrivals.at[i])
+        for i, (source, target) in enumerate(
+            (
+                (f2_far, f2_ref),
+                (slope_far, slope_ref),
+                (f1_far, f1_ref),
+                (normed1_far, normed1_ref),
+                (w3_far, w3_ref),
+                (low_far, low_ref),
+                (hid_far, hid_ref),
+                (total_far, total_ref),
+            )
+        )
+    ]
+    for fetch in fetches:
+        fetch.start()
     place = place_ref[0]
     present = present_column(mask_ref, rows)
     count = (count_a[...].astype(f32) + count_b[...].astype(f32))[:, :1]
@@ -343,12 +361,17 @@
     normed2 = normed2_ref[...]
     sum_grad = norm_backward(up, normed2, inv2_ref[...], row_of(gain2_ref))
     branch_grad = sum_grad.astype(bf16)
+    fetches[0].wait()
+    fetches[1].wait()
     hidden_grad = (slope_ref[...].astype(f32) * mm_nt(branch_grad, f2_ref[...])).astype(bf16)
+    fetches[2].wait()
     first_grad = sum_grad + mm_nt(hidden_grad, f1_ref[...])
+    fetches[3].wait()
     normed1 = normed1_ref[...]
     mixed_grad = norm_backward(first_grad, normed1, inv1_ref[...], row_of(gain1_ref))
     mixed_ref[...] = mixed_grad
     message_grad = (mixed_grad / jnp.maximum(count, 1.0)).astype(bf16)
+    fetches[4].wait()
     up_ref[...] = mm_nt(message_grad, w3_ref[...])
     row = iota((16, 1), 0)
     hidden_sum = column_sum(hidden_grad.astype(f32))
@@ -364,24 +387,23 @@
         bias = bias + jnp.where(row == 8 + j, hidden_sum[:, j * D : (j + 1) * D], 0.0)
     bias_ref[...] = bias * (1.0 / parts)
     wide, narrow = FF // parts, D // parts
+    for fetch in fetches[5:]:
+        fetch.wait()
     low = low_ref[:, pl.ds(pl.multiple_of(place * narrow, narrow), narrow)]
     for j in range(FF // D):
         packed_ref[j * narrow : (j + 1) * narrow, :] = mm_tn(low, hidden_grad[:, j * D : (j + 1) * D]).astype(bf16)
     hid = hid_ref[:, pl.ds(pl.multiple_of(place * wide, wide), wide)]
     packed_ref[D : D + wide, :] = mm_tn(hid, branch_grad).astype(bf16)
     total = total_ref[:, pl.ds(pl.multiple_of(place * narrow, narrow), narrow)]
-    packed_ref[D + wide : D + wide + narrow, :] = mm_tn(total, message_grad).astype(bf16)
-    at = D + wide + narrow
-    half = edge_part_ref.shape[0] // 2
+    w3_grad_ref[...] = mm_tn(total, message_grad).astype(bf16)
+    at = D + wide
     packed_ref[at:, :] = jnp.zeros((packed_ref.shape[0] - at, D), bf16)
-    packed_ref[at : at + half, :E] = edge_part_ref[:half, :]
-    packed_ref[at : at + half, 256 : 256 + E] = edge_part_ref[half:, :]
 
 
 def message_backward_kernel(
-    order, row_ref, edges_ref, act1_ref, d1_ref, d2_ref, up_ref, base_ref, nodes_ref, far_ref, w1_ref, w2_ref, node_bias_ref,
-    out_ref, own_ref, far_grad_ref, local_grad_ref, packed_ref,
-    sums, w1_acc, w2_acc, bias_acc, own_acc,
+    parts, core_ref, row_ref, edges_ref, act1_ref, d1_ref, d2_ref, up_ref, base_ref, nodes_ref, far_ref, w1_ref, w2_ref, node_bias_ref,
+    out_ref, own_ref, far_grad_ref, local_grad_ref, kept_ref, given_ref,
+    sums, w1_acc, w2_acc, bias_acc, own_acc, whole,
 ):
     step = pl.program_id(0)
     last = pl.num_programs(0) - 1
@@ -419,27 +441,83 @@
         far_grad_ref[...] = total[:n_far].astype(bf16)
         local_grad_ref[...] = total[n_far:].astype(bf16)
         nodes = nodes_ref[...]
-        parts = len(order)
         first = (2 * D + E) // parts
         second = D // parts
-        whole = jnp.concatenate(
-            [
-                mm_tn(nodes, own_low),
-                mm_tn(far_ref[...], total[:n_far].astype(bf16)) + mm_tn(nodes, total[n_far:].astype(bf16)),
-                w1_acc[...],
-            ],
-            axis=0,
+        whole[:D, :] = mm_tn(nodes, own_low).astype(bf16)
+        whole[D : 2 * D, :] = (
+            mm_tn(far_ref[...], total[:n_far].astype(bf16)) + mm_tn(nodes, total[n_far:].astype(bf16))
         ).astype(bf16)
-        second_w = w2_acc[...].astype(bf16)
+        whole[2 * D : 2 * D + E, :] = w1_acc[...].astype(bf16)
+        whole[2 * D + E :, :] = w2_acc[...].astype(bf16)
         bias = bias_acc[...].astype(bf16)
-        for q, n in enumerate(order):
-            packed_ref[q, :first, :] = whole[n * first : (n + 1) * first]
-            packed_ref[q, first : first + second, :] = second_w[n * second : (n + 1) * second]
-            packed_ref[q, first + second : first + second + 16, :] = bias
-            if packed_ref.shape[1] > first + second + 16:
-                packed_ref[q, first + second + 16 :, :] = jnp.zeros(
-                    (packed_ref.shape[1] - first - second - 16, D), bf16
-                )
+        half = kept_ref.shape[0]
+        for ref, side in ((kept_ref, core_ref[0]), (given_ref, 1 - core_ref[0])):
+            for q in range(half):
+                n = q * 2 + side
+                ref[q, :first, :] = whole[pl.ds(pl.multiple_of(n * first, 16), first), :]
+                ref[q, first : first + second, :] = whole[
+                    pl.ds(pl.multiple_of(2 * D + E + n * second, 16), second), :
+                ]
+                ref[q, first + second : first + second + 16, :] = bias
+
+
+def picked_lanes(rows, place, parts):
+    wide = rows.shape[1] // parts
+    out = jnp.zeros((rows.shape[0], wide), f32)
+    for n in range(parts):
+        out = out + jnp.where(place == n, rows[:, n * wide : (n + 1) * wide], 0.0)
+    return out
+
+
+def joined(whole, index, piece):
+    rows = piece.shape[0]
+    whole[pl.ds(pl.multiple_of(index * rows, 16), rows), :] = piece[...]
+
+
+def node_weights_kernel(
+    parts, half, at_ref, a0, a1, b0, b1, mixed_ref, back_a, back_b, nodes_ref,
+    f1_ref, f2_ref, ew1_ref, ew2_ref, ew3_ref, eb1_ref, eb2_ref, eb3_ref, eg_ref, es_ref, whole,
+):
+    nodes_ref[...] = mixed_ref[...] + (back_a[...].astype(f32) + back_b[...].astype(f32))
+    top = whole.shape[0] // 2
+    low, high = whole.at[:top], whole.at[top:]
+    joined(low, at_ref[1], a0)
+    joined(low, 1 - at_ref[1], a1)
+    joined(high, at_ref[2], b0)
+    joined(high, 1 - at_ref[2], b1)
+    place = at_ref[0]
+    wide, narrow = FF // parts, D // parts
+    for j in range(FF // D):
+        f1_ref[:, j * D : (j + 1) * D] = whole[j * narrow : (j + 1) * narrow, :].astype(f32)
+    at = D + wide
+    f2_ref[...] = whole[D:at, :].astype(f32)
+    edge = jnp.concatenate([whole[at : at + half, :E], whole[at : at + half, 256 : 256 + E]], axis=0).astype(f32)
+    first, second = (2 * D + E) // parts, E // parts
+    ew1_ref[...] = edge[:first].T
+    ew2_ref[...] = edge[first : first + second]
+    ew3_ref[...] = edge[first + second : first + 2 * second]
+    rows = picked_lanes(edge[first + 2 * second : first + 2 * second + 8], place, parts)
+    for j, ref in enumerate((eb1_ref, eb2_ref, eb3_ref, eg_ref, es_ref)):
+        ref[...] = rows[j : j + 1].reshape(second)
+
+
+def message_weights_kernel(parts, at_ref, p0, p1, p2, p3, w1_ref, w2_ref, w3_ref, *refs):
+    *vectors, fb1_ref, whole = refs
+    for mask, piece in enumerate((p0, p1, p2, p3)):
+        joined(whole, at_ref[1] ^ mask, piece)
+    place = at_ref[0]
+    first, narrow = (2 * D + E) // parts, D // parts
+    w1_ref[...] = whole[:first, :].astype(f32)
+    w2_ref[...] = whole[first : first + narrow, :].astype(f32)
+    w3_ref[...] = whole[first + narrow + 16 : first + 2 * narrow + 16, :].astype(f32)
+    bias = whole[first + narrow : first + narrow + 16, :].astype(f32)
+    rows = picked_lanes(bias[:8], place, parts)
+    for j, ref in enumerate(vectors):
+        ref[...] = rows[j : j + 1].reshape(narrow)
+    hidden = jnp.zeros((1, D), f32)
+    for n in range(FF // D):
+        hidden = hidden + jnp.where(place == n, bias[8 + n : 9 + n], 0.0)
+    fb1_ref[...] = hidden.reshape(FF // parts)
 
 
 def swap(values, axis, bit):
@@ -465,19 +543,23 @@
     return values, swap(values, axis, bits[-1])
 
 
-def halved_sum(values, axis, bit):
-    half = values.shape[0] // 2
+def after(values, *earlier):
+    return lax.optimization_barrier((values, *earlier))[0]
+
+
+def halved_sum(values, axis, bit, dim=0):
+    half = values.shape[dim] // 2
     side = (lax.axis_index(axis) // bit) & 1
-    kept = lax.dynamic_slice_in_dim(values, side * half, half, 0)
-    given = lax.dynamic_slice_in_dim(values, (1 - side) * half, half, 0)
+    kept = lax.dynamic_slice_in_dim(values, side * half, half, dim)
+    given = lax.dynamic_slice_in_dim(values, (1 - side) * half, half, dim)
     return add_low(kept, swap(given, axis, bit))
 
 
-def rejoined(values, axis, bit):
+def rejoined(values, axis, bit, dim=0):
     other = swap(values, axis, bit)
     side = (lax.axis_index(axis) // bit) & 1
     return jnp.where(
-        side == 0, jnp.concatenate([values, other], axis=0), jnp.concatenate([other, values], axis=0)
+        side == 0, jnp.concatenate([values, other], axis=dim), jnp.concatenate([other, values], axis=dim)
     )
 
 
@@ -491,6 +573,45 @@
     for bit in bits:
         values = rejoined(values, axis, bit)
     return values
+
+
+def total_of(addends, rows):
+    total = 0.0
+    for values, start in addends:
+        total = total + lax.dynamic_slice_in_dim(values, start, rows, 0).astype(f32)
+    return total.astype(bf16)
+
+
+def halve(addends, rows, axis, bit):
+    half = rows // 2
+    side = (lax.axis_index(axis) // bit) & 1
+    given = total_of([(values, start + (1 - side) * half) for values, start in addends], half)
+    return [(values, start + side * half) for values, start in addends] + [(swap(given, axis, bit), 0)]
+
+
+def quarter_sum(values, axis, bits):
+    rows = values.shape[0] // 4
+    low, high = ((lax.axis_index(axis) // bit) & 1 for bit in bits)
+    mine = 2 * low + high
+    total = lax.dynamic_slice_in_dim(values, mine * rows, rows, 0).astype(f32)
+    for mask in (1, 2, 3):
+        given = lax.dynamic_slice_in_dim(values, (mine ^ mask) * rows, rows, 0)
+        total = total + swap(given, axis, (mask >> 1) * bits[0] + (mask & 1) * bits[1]).astype(f32)
+    return total.astype(bf16)
+
+
+def held_together(*lists):
+    flat = []
+    for item in lists:
+        flat += [values for values, _ in item] if isinstance(item, list) else [item]
+    flat = iter(lax.optimization_barrier(tuple(flat)))
+    return tuple(
+        [(next(flat), start) for _, start in item] if isinstance(item, list) else next(flat) for item in lists
+    )
+
+
+def quarters(values, axis, bits):
+    return [values] + [swap(values, axis, (mask >> 1) * bits[0] + (mask & 1) * bits[1]) for mask in (1, 2, 3)]
 
 
 def exchange(values, blocks):
@@ -596,7 +717,7 @@
             shape((rows, 128), bf16),
         ),
         in_specs=[smem, vmem, vmem],
-    )(res_place, neighbours.T, mask_row)
+    )(res_place, *read(neighbours.T, mask_row))
     together = lax.optimization_barrier
     wanted = exchange(want, blocks)
 
@@ -625,7 +746,7 @@
         ],
         out_specs=(flat, flat, flat, fixed(rows, D)),
         cost=pl.CostEstimate(flops=16 * total * D * D, bytes_accessed=total * D * 8, transcendentals=2 * total * D),
-    )(*read(place_col, edges, nodes), far_nodes, *read(msg_w1, msg_w2), msg_b1, msg_b2)
+    )(*read(place_col, edges, nodes), far_nodes, *read(msg_w1, msg_w2, msg_b1, msg_b2))
     sum_a, sum_b = shared_sum(act_sum, "nbr")
 
     total_act, first_low, normed1, inv1, hidden, hidden_slope, normed2, inv2, sent, send = call(
@@ -654,7 +775,7 @@
             shape((kn, rows, E), bf16),
             stored((total, E), f32),
             stored((rows, E), bf16),
-            shape((n_far, E), bf16),
+            stored((n_far, E), bf16),
             stored((rows, E), bf16),
             shape((parts, edge_rows, E), bf16),
         ),
@@ -691,43 +812,64 @@
         ),
         cost=pl.CostEstimate(flops=16 * total * D * D, bytes_accessed=total * E * 12, transcendentals=2 * total * E),
     )(*read(place_row, place_col, edges, edge_cot, sent), far_sent, *read(edge_w1, edge_w2, edge_w3),
-      edge_b1, edge_b2, edge_b3, norm3_gain, norm3_bias)
+      *read(edge_b1, edge_b2, edge_b3, norm3_gain, norm3_bias))
 
     far_back, edge_packed = together((exchange(far_sum, blocks), edge_packed))
-    back = call(returned_kernel, shape((rows, 2 * E), bf16))(own_sum, local_sum, far_back, wanted)
-    back_a, back_b = shared_sum(back, "nbr")
+    back = call(returned_kernel, shape((rows, 2 * E), bf16))(*read(own_sum, local_sum), far_back, wanted)
+    for bit in nbr_bits[:-1]:
+        back = add_low(back, swap(back, "nbr", bit))
+    back, edge_packed = together((back, edge_packed))
+    back_a, back_b = back, swap(back, "nbr", nbr_bits[-1])
     edge_part = scattered_sum(edge_packed, "nbr", nbr_bits).reshape(edge_rows, E)
 
     wide, narrow = FF // parts, D // parts
-    node_rows = up_to(D + wide + narrow + edge_rows // 2, 16 * blocks)
-    mixed_grad, up, node_bias, node_packed = call(
+    node_rows = up_to(D + wide + edge_rows // 2, 16 * blocks)
+    mixed_grad, up, node_bias, node_packed, msg_w3_part = call(
         functools.partial(node_backward_kernel, parts),
         (
             shape((rows, D), f32),
             shape((rows, D), f32),
             shape((16, D), f32),
             shape((node_rows, D), bf16),
+            shape((narrow, D), bf16),
         ),
-        scratch=[pltpu.VMEM((rows, FF), bf16)],
-        in_specs=[smem] + [vmem] * 21,
+        scratch=[
+            pltpu.VMEM((FF, D), bf16),
+            pltpu.VMEM((rows, FF), bf16),
+            pltpu.VMEM((D, FF), bf16),
+            pltpu.VMEM((rows, D), f32),
+            pltpu.VMEM((D, D), bf16),
+            pltpu.VMEM((rows, D), bf16),
+            pltpu.VMEM((rows, FF), bf16),
+            pltpu.VMEM((rows, D), bf16),
+            pltpu.SemaphoreType.DMA((8,)),
+        ],
+        in_specs=[smem] + [vmem] * 12 + [pl.BlockSpec(memory_space=pltpu.HBM)] * 8,
     )(
-        nbr_place, back_a, back_b, count_a, count_b, *read(node_cot), mask_row, *read(total_act, first_low, normed1, inv1),
-        *read(hidden, hidden_slope, normed2, inv2, edge_w1), msg_w3, ffn_w1, ffn_w2, norm1_gain, norm2_gain, edge_part,
+        nbr_place, back_a, back_b, count_a, count_b, *read(node_cot, mask_row, inv1, normed2, inv2, edge_w1),
+        *read(norm1_gain, norm2_gain, ffn_w2, hidden_slope, ffn_w1, normed1, msg_w3, first_low, hidden, total_act),
     )
     bits = bits_of("res")
     order_a, order_b = bits, bits[1:2] + bits[:1] + bits[2:]
-    part_a = halved_sum(node_packed[: node_rows // 2], "res", order_a[0])
-    part_b = halved_sum(node_packed[node_rows // 2 :], "res", order_b[0])
-
-    msg_rows = up_to(first_rows + narrow + 16, 8 * blocks)
-    edges_grad, own_sum, far_sum, local_sum, msg_packed = call(
-        functools.partial(message_backward_kernel, order),
+    rows_ab = node_rows // 2
+    part_a = halve([(node_packed, 0)], rows_ab, "res", order_a[0])
+    lead = D + wide - rows_ab
+    edge_pair = jnp.pad(edge_part.reshape(2, edge_rows // 2, E), ((0, 0), (0, 0), (0, 256 - E)))
+    edge_pair = jnp.concatenate([edge_pair[0], edge_pair[1]], axis=1)
+    edge_pair = jnp.pad(edge_pair, ((lead, rows_ab - lead - edge_rows // 2), (0, 0)))
+    part_b = halve([(node_packed, rows_ab), (edge_pair, 0)], rows_ab, "res", order_b[0])
+
+    msg_rows = first_rows + narrow + 16
+    share_rows = up_to(msg_rows + narrow, 8 * blocks)
+    edges_grad, own_sum, far_sum, local_sum, msg_kept, msg_given = call(
+        functools.partial(message_backward_kernel, parts),
         (
             shape((kn, rows, E), f32),
             shape((rows, D), bf16),
             shape((n_far, D), bf16),
             shape((rows, D), bf16),
-            shape((parts, msg_rows, D), bf16),
+            shape((parts // 2, msg_rows, D), bf16),
+            shape((parts // 2, msg_rows, D), bf16),
         ),
         scratch=[
             pltpu.VMEM((width, D), f32),
@@ -735,9 +877,11 @@
             pltpu.VMEM((D, D), f32),
             pltpu.VMEM((16, D), f32),
             pltpu.VMEM((rows, D), f32),
+            pltpu.VMEM((3 * D + E, D), bf16),
         ],
         grid=grid,
         in_specs=[
+            smem,
             fixed(SLOT, rows),
             edge_tile,
             flat,
@@ -751,84 +895,100 @@
             fixed(D, D),
             fixed(16, D),
         ],
-        out_specs=(edge_tile, fixed(rows, D), fixed(n_far, D), fixed(rows, D), fixed(parts, msg_rows, D)),
+        out_specs=(edge_tile, fixed(rows, D), fixed(n_far, D), fixed(rows, D))
+        + (fixed(parts // 2, msg_rows, D),) * 2,
         cost=pl.CostEstimate(flops=16 * total * D * D, bytes_accessed=total * D * 10, transcendentals=0),
-    )(*read(place_row, edges, act1, d1, d2), up, *read(base, nodes), far_nodes, *read(msg_w1, msg_w2), node_bias)
-
-    far_sum, msg_part, part_a, part_b = together((far_sum, msg_packed, part_a, part_b))
-    msg_part = halved_sum(msg_part, "nbr", nbr_bits[0])
-    part_a = halved_sum(part_a, "res", order_a[1])
-    part_b = halved_sum(part_b, "res", order_b[1])
-    far_sum, msg_part, part_a, part_b = together((far_sum, msg_part, part_a, part_b))
-    msg_part = scattered_sum(msg_part, "nbr", nbr_bits[1:]).reshape(msg_rows, D)
-    far_back = exchange(far_sum, blocks)
-    part_a = scattered_sum(part_a, "res", order_a[2:])
-    part_b = scattered_sum(part_b, "res", order_b[2:])
-    far_back, msg_part, part_a, part_b = together((far_back, msg_part, part_a, part_b))
-    msg_part = halved_sum(msg_part, "res", bits[0])
+    )(nbr_place & 1, *read(place_row, edges, act1, d1, d2), up, *read(base, nodes), far_nodes, *read(msg_w1, msg_w2), node_bias)
+
+    far_sum, msg_kept, msg_given, part_a, part_b = held_together(far_sum, msg_kept, msg_given, part_a, part_b)
+    flat_rows = parts // 2 * msg_rows
+    msg_part = add_low(msg_kept, swap(msg_given, "nbr", 1)).reshape(flat_rows, D)
+    part_a = halved_sum(total_of(part_a, rows_ab // 2), "res", order_a[1])
+    part_b = halved_sum(total_of(part_b, rows_ab // 2), "res", order_b[1])
+    middle, last = bits[2:-1], bits[-1]
+    part_a = scattered_sum(part_a, "res", middle)
+    part_b = scattered_sum(part_b, "res", middle)
+    both = after(jnp.stack([part_a, part_b]), msg_part)
+    msg_sum = scattered_sum(msg_part, "nbr", nbr_bits[1:])
+    both = halved_sum(both, "res", last, 1)
+    msg_sum = jnp.concatenate([msg_sum, msg_w3_part, jnp.zeros((share_rows - msg_rows - narrow, D), bf16)], axis=0)
+    msg_quarter = quarter_sum(msg_sum, "res", bits[:2])
+    both = rejoined(after(both, msg_sum) if 4 == 4 else both, "res", last, 1)
+    far_back = exchange(after(far_sum, both), blocks)
     back = call(returned_last_kernel, shape((rows, D), bf16))(own_sum, local_sum, far_back, wanted, msg_w1)
     for bit in nbr_bits[:-1]:
         back = add_low(back, swap(back, "nbr", bit))
-    part_a = gathered_rows(part_a, "res", order_a[:1:-1])
-    part_b = gathered_rows(part_b, "res", order_b[:1:-1])
-    back, msg_part, part_a, part_b = together((back, msg_part, part_a, part_b))
-    msg_part = scattered_sum(msg_part, "res", bits[1:-1])
     back_b = swap(back, "nbr", nbr_bits[-1])
-    part_a = rejoined(part_a, "res", order_a[1])
-    part_b = rejoined(part_b, "res", order_b[1])
-    back, back_b, msg_part, part_a, part_b = together((back, back_b, msg_part, part_a, part_b))
-    nodes_grad = mixed_grad + (back.astype(f32) + back_b.astype(f32))
-    msg_part = add_low(msg_part, swap(msg_part, "res", bits[-1]))
-    part_a = rejoined(part_a, "res", order_a[0])
-    part_b = rejoined(part_b, "res", order_b[0])
-    msg_part, part_a, part_b = together((msg_part, part_a, part_b))
-    msg_share = gathered_rows(msg_part, "res", bits[-2::-1]).astype(f32)
-    node_share = jnp.concatenate([part_a, part_b], axis=0).astype(f32)
-
-    ffn_w1_grad = jnp.concatenate([node_share[j * narrow : (j + 1) * narrow] for j in range(FF // D)], axis=1)
-    ffn_w2_grad = node_share[D : D + wide]
-    at = D + wide + narrow
-    msg_w3_grad = node_share[D + wide : at]
-    half = edge_rows // 2
-    edge_share = jnp.concatenate([node_share[at : at + half, :E], node_share[at : at + half, 256 : 256 + E]], axis=0)
-    edge_w1_grad = edge_share[:first_rows]
-    edge_w2_grad = edge_share[first_rows : first_rows + second_rows]
-    edge_w3_grad = edge_share[first_rows + second_rows : first_rows + 2 * second_rows]
-    place = lax.axis_index("nbr")
-    edge_bias = edge_share[first_rows + 2 * second_rows : first_rows + 2 * second_rows + 8]
-    edge_bias = lax.dynamic_slice_in_dim(edge_bias, place * second_rows, second_rows, 1)
-    msg_w1_grad = msg_share[:first_rows]
-    msg_w2_grad = msg_share[first_rows : first_rows + narrow]
-    bias_all = msg_share[first_rows + narrow : first_rows + narrow + 16]
-    bias = lax.dynamic_slice_in_dim(bias_all[:8], place * narrow, narrow, 1)
-    ffn_b1_grad = lax.dynamic_index_in_dim(bias_all[8 : 8 + FF // D], place, 0, keepdims=False)
+    msg_part = scattered_sum(msg_quarter, "res", middle)
+    msg_part = add_low(msg_part, swap(msg_part, "res", last))
+    part_a, part_b = after(both[0], msg_quarter), after(both[1], msg_quarter)
+    part_a = rejoined(gathered_rows(part_a, "res", middle[::-1]), "res", order_a[1])
+    part_b = rejoined(gathered_rows(part_b, "res", middle[::-1]), "res", order_b[1])
+    part_a, part_b = after(part_a, msg_part), after(part_b, msg_part)
+    other_a = swap(part_a, "res", order_a[0])
+    other_b = swap(part_b, "res", order_b[0])
+    msg_parts = quarters(gathered_rows(msg_part, "res", middle[::-1]), "res", bits[:2])
+
+    def side(bit):
+        return (lax.axis_index("res") // bit) & 1
+
+    node_at = jnp.stack([lax.axis_index("nbr"), side(order_a[0]), side(order_b[0])]).astype(jnp.int32)
+    msg_at = jnp.stack([lax.axis_index("nbr"), 2 * side(bits[0]) + side(bits[1])]).astype(jnp.int32)
+    (
+        nodes_grad, ffn_w1_grad, ffn_w2_grad, edge_w1_grad, edge_w2_grad, edge_w3_grad,
+        edge_b1_grad, edge_b2_grad, edge_b3_grad, norm3_gain_grad, norm3_bias_grad,
+    ) = call(
+        functools.partial(node_weights_kernel, parts, edge_rows // 2),
+        (
+            shape((rows, D), f32),
+            shape((narrow, FF), f32),
+            shape((wide, D), f32),
+            shape((E, first_rows), f32),
+            shape((second_rows, E), f32),
+            shape((second_rows, E), f32),
+        )
+        + (shape((second_rows,), f32),) * 5,
+        scratch=[pltpu.VMEM((node_rows, D), bf16)],
+        in_specs=[smem] + [vmem] * 7,
+    )(node_at, part_a, other_a, part_b, other_b, mixed_grad, back, back_b)
+    (
+        msg_w1_grad, msg_w2_grad, msg_w3_grad, msg_b1_grad, msg_b2_grad, msg_b3_grad, norm1_gain_grad, norm1_bias_grad,
+        ffn_b2_grad, norm2_gain_grad, norm2_bias_grad, ffn_b1_grad,
+    ) = call(
+        functools.partial(message_weights_kernel, parts),
+        (shape((first_rows, D), f32), shape((narrow, D), f32), shape((narrow, D), f32))
+        + (shape((narrow,), f32),) * 8
+        + (shape((wide,), f32),),
+        scratch=[pltpu.VMEM((share_rows, D), bf16)],
+        in_specs=[smem] + [vmem] * 4,
+    )(msg_at, *msg_parts)
     return (
         sent,
         edges_out.transpose(1, 0, 2),
         nodes_grad,
         edges_grad.transpose(1, 0, 2),
         msg_w1_grad,
-        bias[0],
+        msg_b1_grad,
         msg_w2_grad,
-        bias[1],
+        msg_b2_grad,
         msg_w3_grad,
-        bias[2],
-        bias[3],
-        bias[4],
+        msg_b3_grad,
+        norm1_gain_grad,
+        norm1_bias_grad,
         ffn_w1_grad,
         ffn_b1_grad,
         ffn_w2_grad,
-        bias[5],
-        bias[6],
-        bias[7],
-        edge_w1_grad,
-        edge_bias[0],
+        ffn_b2_grad,
+        norm2_gain_grad,
+        norm2_bias_grad,
+        edge_w1_grad.T,
+        edge_b1_grad,
         edge_w2_grad,
-        edge_bias[1],
+        edge_b2_grad,
         edge_w3_grad,
-        edge_bias[2],
-        edge_bias[3],
-        edge_bias[4],
+        edge_b3_grad,
+        norm3_gain_grad,
+        norm3_bias_grad,
     )
 
 

time: 207 us -> 194 us (0.937)
  local copies, waits for them, and re-layouts: 14.7 us -> 0.33 us
  blocking collectives: 36 us -> 46.8 us
  starting transfers between devices: 38.8 us -> 29.6 us
  Pallas kernels: 53.8 us -> 60.4 us
  other arithmetic: 10.6 us -> 6.43 us
  waiting for transfers between devices: 49.7 us -> 46.9 us
    all_to_all x3 -> x4, blocking collectives: 36 us -> 46.8 us  [exchange(): return lax.all_to_all(shaped, 'res', 0, 0, tiled=True).reshape(values.shape)]
    all_to_all x2 -> x1, waiting for transfers between devices: 10.1 us -> 0.01 us  [exchange(): return lax.all_to_all(shaped, 'res', 0, 0, tiled=True).reshape(values.shape)]
    ppermute x29, waiting for transfers between devices: 39.7 us -> 46.9 us  [swap(): lax.ppermute(values, axis, [(i, i ^ bit) for i in range(lax.axis_size(axi...]
    unnamed x75 -> x30, local copies, waits for them, and re-layouts: 6.21 us -> 0.09 us
    ppermute x29, starting transfers between devices: 31.3 us -> 26.1 us  [swap(): lax.ppermute(values, axis, [(i, i ^ bit) for i in range(lax.axis_size(axi...]
    pallas_call x1 -> x3, Pallas kernels: 12.6 us -> 16.8 us  [the longest x1 12.8 us: on_device(): call(functools.partial(message_backward_kernel, parts), (shape((kn, rows,...]
    all_to_all x2 -> x1, starting transfers between devices: 7.44 us -> 3.56 us  [exchange(): return lax.all_to_all(shaped, 'res', 0, 0, tiled=True).reshape(values.shape)]
    dynamic_slice x14 -> x7, local copies, waits for them, and re-layouts: 3.87 us -> 0.19 us  [the longest x6 0.16 us: halved_sum(): given = lax.dynamic_slice_in_dim(values, (1 - side) * half, half, dim)]
  transfers between devices with their start and end apart: 31 -> 30, of which waited for: 21 -> 15; matrix products, arithmetic and copies ran while one was open for 6% -> 3% of each run, Pallas kernels for 7% -> 11%
where the time goes in v3:
time: 194 us; the launch traced here: 193 us
  Pallas kernels  60.4 us (31%)
  waiting for transfers between devices  46.9 us (24%)
  blocking collectives  46.8 us (24%)
  starting transfers between devices  29.6 us (15%)
  other arithmetic  6.43 us (3%)
    ppermute x29, waiting for transfers between devices, swap(): lax.ppermute(values, axis, [(i, i ^ bit) for i in range(lax.axis_size(axi...  46.9 us
    all_to_all x4, blocking collectives, exchange(): return lax.all_to_all(shaped, 'res', 0, 0, tiled=True).reshape(values.shape)  46.8 us
    ppermute x29, starting transfers between devices, swap(): lax.ppermute(values, axis, [(i, i ^ bit) for i in range(lax.axis_size(axi...  26.1 us
    pallas_call x1, Pallas kernels, on_device(): call(functools.partial(edge_kernel, order), (shape((kn, rows, E), bf16),...  14.8 us
    pallas_call x1, Pallas kernels, on_device(): call(message_forward_kernel, (stored((total, D), bf16), stored((total, D)...  13.9 us
    pallas_call x1, Pallas kernels, on_device(): call(functools.partial(message_backward_kernel, parts), (shape((kn, rows,...  12.8 us
    pallas_call x1, Pallas kernels, on_device(): call(functools.partial(node_backward_kernel, parts), (shape((rows, D), f3...  6.15 us
    pallas_call x1, Pallas kernels, on_device(): call(node_forward_kernel, (stored((rows, D), bf16), stored((rows, D), bf1...  3.92 us
  transfers between devices with their start and end apart: 30, of which 15 were waited for; matrix products, arithmetic and copies ran while one was open for 3% of the time, Pallas kernels for 11%

profile of v3, /device:TPU:0, one launch (start us, length us, event | category | flops | bytes accessed | tf_op | source)
XLA Modules:
  0.0 192.9 jit_solution(4858577004115384237)
XLA Ops:
  0.7 2.8 %shard_map.467 = (s32[16,192]{1,0:T(8,128)S(1)}, f32[192,16]{1,0:T(8,128)S(1)}, bf16[256,128]{1,0:T(8,128)(2,1)S(1)}, bf16[192,128]{1,0:T(8,128)(2,1)S(1)}) custom-call(s32[1]{0:T(128)} %bitcast.me_ref, s32[15,192]{1,0:T(8,128)} %bitcast.59, s32[1,192]{1,0:T(1,128)} %bitcast.49), custom_call_target="tpu_custom_call" | custom-call | tf_op jit(solution)/shard_map/pallas_call | solution.py:711
  3.5 14.0 %all_to_all.25 = bf16[8,32,128]{2,1,0:T(8,128)(2,1)S(1)} all-to-all(bf16[8,32,128]{2,1,0:T(8,128)(2,1)S(1)} %bitcast.48), channel_id=1, replica_groups=mesh['res'=8,'nbr'=4] {'res'}, dimensions={0} | all-to-all | bytes 131072 | tf_op jit(solution)/shard_map/all_to_all | solution.py:619
  18.8 10.6 %all_to_all.26 = bf16[8,32,512]{2,1,0:T(8,128)(2,1)S(1)} all-to-all(bf16[8,32,512]{2,1,0:T(8,128)(2,1)S(1)} %bitcast.54), channel_id=1, replica_groups=mesh['res'=8,'nbr'=4] {'res'}, dimensions={0} | all-to-all | bytes 524288 | tf_op jit(solution)/shard_map/all_to_all | solution.py:619
  29.5 13.9 %shard_map.468 = (bf16[2880,512]{1,0:T(8,128)(2,1)}, bf16[2880,512]{1,0:T(8,128)(2,1)}, bf16[2880,512]{1,0:T(8,128)(2,1)}, bf16[192,512]{1,0:T(8,128)(2,1)S(1)}) custom-call(f32[192,16]{1,0:T(8,128)} %copy-done.13, bf16[15,192,192]{2,1,0:T(8,128)(2,1)} %bitcast.61, bf16[192,512]{1,0:T(8,128)(2,1)} %nodes_ref.5, bf16[256,512]{1,0:T(8,128)(2,1)S(1)} %bitcast.44, ...), custom_call_target="tpu_custom_call" | custom-call | flops 12079595520 | bytes 11796480 | tf_op jit(solution)/shard_map/pallas_call | solution.py:732
  47.1 5.9 %collective-permute-done.3.count_b = bf16[192,128]{1,0:T(8,128)(2,1)S(1)} collective-permute-done((bf16[192,128]{1,0:T(8,128)(2,1)S(1)}, bf16[192,128]{1,0:T(8,128)(2,1)S(1)}, u32[]{:S(2)}, u32[]{:S(2)}) %collective-permute-start.3) | collective-permute-done | bytes 49184 | tf_op jit(solution)/shard_map/ppermute | solution.py:524
  53.1 3.9 %shard_map.469 = (bf16[192,512]{1,0:T(8,128)(2,1)}, bf16[192,512]{1,0:T(8,128)(2,1)}, f32[192,512]{1,0:T(8,128)}, f32[192,1]{1,0:T(8,128)}, bf16[192,2048]{1,0:T...) custom-call(bf16[192,512]{1,0:T(8,128)(2,1)S(1)} %add_convert_fusion, ...), custom_call_target="tpu_custom_call" | custom-call | tf_op jit(solution)/shard_map/pallas_call | solution.py:752
  57.0 11.4 %all_to_all.27 = bf16[8,32,512]{2,1,0:T(8,128)(2,1)S(1)} all-to-all(bf16[8,32,512]{2,1,0:T(8,128)(2,1)S(1)} %bitcast.46), channel_id=1, replica_groups=mesh['res'=8,'nbr'=4] {'res'}, dimensions={0} | all-to-all | bytes 524288 | tf_op jit(solution)/shard_map/all_to_all | solution.py:619
  68.4 14.8 %shard_map.470 = (bf16[15,192,192]{2,1,0:T(8,128)(2,1)}, f32[2880,192]{1,0:T(8,128)}, bf16[192,192]{1,0:T(8,128)(2,1)}, bf16[256,192]{1,0:T(8,128)(2,1)}, bf16[1...) custom-call(s32[16,192]{1,0:T(8,128)} %copy-done.14, f32[192,16]{1,0:T(8,128)} %copy-done.13, ...), custom_call_target="tpu_custom_call" | custom-call | flops 12079595520 | bytes 6635520 | tf_op jit(solution)/shard_map/pallas_call | solution.py:772
  83.3 10.8 %all_to_all.28 = bf16[8,32,192]{2,1,0:T(8,128)(2,1)S(1)} all-to-all(bf16[8,32,192]{2,1,0:T(8,128)(2,1)} %bitcast.58), channel_id=1, replica_groups=mesh['res'=8,'nbr'=4] {'res'}, dimensions={0} | all-to-all | bytes 196608 | tf_op jit(solution)/shard_map/all_to_all | solution.py:619
  100.5 3.3 %collective-permute-done.5.back_b = bf16[192,384]{1,0:T(8,128)(2,1)S(1)} collective-permute-done((bf16[192,384]{1,0:T(8,128)(2,1)S(1)}, bf16[192,384]{1,0:T(8,128)(2,1)S(1)}, u32[]{:S(2)}, u32[]{:S(2)}) %collective-permute-start.5) | collective-permute-done | bytes 147488 | tf_op jit(solution)/shard_map/ppermute | solution.py:524
  103.8 6.1 %shard_map.472 = (f32[192,512]{1,0:T(8,128)S(1)}, f32[192,512]{1,0:T(8,128)S(1)}, f32[16,512]{1,0:T(8,128)S(1)}, bf16[1280,512]{1,0:T(8,128)(2,1)S(1)}, bf16[128,512]{1,0:T(8,128)(2,1)S(1)}) custom-call(s32[1]{0:T(128)} %bitcast.13.place_ref, bf16[192,384]{1,0:T(8,128)(2,1)S(1)} %add_convert_fusion.14.back_a, ...), custom_call_target="tpu_custom_call" | custom-call | tf_op jit(solution)/shard_map/pallas_call | solution.py:827
  111.7 12.8 %shard_map.473 = (f32[15,192,192]{2,1,0:T(8,128)}, bf16[192,512]{1,0:T(8,128)(2,1)S(1)}, bf16[256,512]{1,0:T(8,128)(2,1)}, bf16[192,512]{1,0:T(8,128)(2,1)S(1)},...) custom-call(s32[1]{0:T(128)S(6)} %and.66.core_ref, s32[16,192]{1,0:T(8,128)} %copy-done.14, ...), custom_call_target="tpu_custom_call" | custom-call | flops 12079595520 | bytes 14745600 | tf_op jit(solution)/shard_map/pallas_call | solution.py:864
  125.7 2.0 %collective-permute-start.10 = (bf16[160,512]{1,0:T(8,128)(2,1)S(1)}, bf16[160,512]{1,0:T(8,128)(2,1)S(1)}, u32[]{:S(2)}, u32[]{:S(2)}) collective-permute-start(bf16[160,512]{1,0:T(8,128)(2,1)S(1)} %constant_dynamic-slice_fusion.3), channel_id=1, source_target_pairs={{0,8},{4,12},{8,0},{12,4},{16,24},{20,28},{24,16},{28,20},{1,9},{5... | collective-permute-start | bytes 491528 | tf_op jit(solution)/shard_map/ppermute | solution.py:524
  127.7 2.4 %collective-permute-done.11 = bf16[160,512]{1,0:T(8,128)(2,1)S(1)} collective-permute-done((bf16[160,512]{1,0:T(8,128)(2,1)S(1)}, bf16[160,512]{1,0:T(8,128)(2,1)S(1)}, u32[]{:S(2)}, u32[]{:S(2)}) %collective-permute-start.11) | collective-permute-done | bytes 163872 | tf_op jit(solution)/shard_map/ppermute | solution.py:524
  130.2 2.5 %collective-permute-done.10 = bf16[160,512]{1,0:T(8,128)(2,1)S(1)} collective-permute-done((bf16[160,512]{1,0:T(8,128)(2,1)S(1)}, bf16[160,512]{1,0:T(8,128)(2,1)S(1)}, u32[]{:S(2)}, u32[]{:S(2)}) %collective-permute-start.10) | collective-permute-done | bytes 163872 | tf_op jit(solution)/shard_map/ppermute | solution.py:524
  135.5 9.3 %collective-permute-done.13 = bf16[2,80,512]{2,1,0:T(8,128)(2,1)S(1)} collective-permute-done((bf16[2,80,512]{2,1,0:T(8,128)(2,1)S(1)}, bf16[2,80,512]{2,1,0:T(8,128)(2,1)S(1)}, u32[]{:S(2)}, u32[]{:S(2)}) %collective-permute-start.13) | collective-permute-done | bytes 163872 | tf_op jit(solution)/shard_map/ppermute | solution.py:524
  149.2 1.8 collective-permute-start.17
  151.5 2.7 %collective-permute-done.15 = bf16[2,80,512]{2,1,0:T(8,128)(2,1)S(1)} collective-permute-done((bf16[2,80,512]{2,1,0:T(8,128)(2,1)S(1)}, bf16[2,80,512]{2,1,0:T(8,128)(2,1)S(1)}, u32[]{:S(2)}, u32[]{:S(2)}) %collective-permute-start.15) | collective-permute-done | bytes 163872 | tf_op jit(solution)/shard_map/ppermute | solution.py:524
  154.3 3.6 %all-to-all-start.4 = ((bf16[8,32,512]{2,1,0:T(8,128)(2,1)}), bf16[8,32,512]{2,1,0:T(8,128)(2,1)S(1)}, u32[]{:S(2)}, u32[]{:S(2)}) async-start(bf16[8,32,512]{2,1,0:T(8,128)(2,1)} %bitcast.26), calls=%async_computation.4 | async-start | bytes 524288 | tf_op jit(solution)/shard_map/all_to_all | solution.py:619
  157.9 2.2 %collective-permute-done.16 = bf16[144,512]{1,0:T(8,128)(2,1)} collective-permute-done((bf16[144,512]{1,0:T(8,128)(2,1)S(1)}, bf16[144,512]{1,0:T(8,128)(2,1)}, u32[]{:S(2)}, u32[]{:S(2)}) %collective-permute-start.16) | collective-permute-done | bytes 147488 | tf_op jit(solution)/shard_map/ppermute | solution.py:524
  165.0 8.4 %collective-permute-done.20 = bf16[144,512]{1,0:T(8,128)(2,1)S(1)} collective-permute-done((bf16[144,512]{1,0:T(8,128)(2,1)S(1)}, bf16[144,512]{1,0:T(8,128)(2,1)S(1)}, u32[]{:S(2)}, u32[]{:S(2)}) %collective-permute-start.20) | collective-permute-done | bytes 147488 | tf_op jit(solution)/shard_map/ppermute | solution.py:524
  175.1 1.9 %collective-permute-start.28 = (bf16[144,512]{1,0:T(8,128)(2,1)S(1)}, bf16[144,512]{1,0:T(8,128)(2,1)S(1)}, u32[]{:S(2)}, u32[]{:S(2)}) collective-permute-start(bf16[144,512]{1,0:T(8,128)(2,1)S(1)} %add_convert_fusion.12.p0), channel_id=1, source_target_pairs={{0,12},{4,8},{8,4},{12,0},{16,28},{20,24},{24,20},{28,16},{1,13},{... | collective-permute-start | bytes 442376 | tf_op jit(solution)/shard_map/ppermute | solution.py:524
  184.3 5.3 %collective-permute-done.21.a1 = bf16[320,512]{1,0:T(8,128)(2,1)S(1)} collective-permute-done((bf16[320,512]{1,0:T(8,128)(2,1)S(1)}, bf16[320,512]{1,0:T(8,128)(2,1)S(1)}, u32[]{:S(2)}, u32[]{:S(2)}) %collective-permute-start.21) | collective-permute-done | bytes 327712 | tf_op jit(solution)/shard_map/ppermute | solution.py:524
  190.5 2.4 %shard_map.475 = (f32[192,512]{1,0:T(8,128)}, f32[128,2048]{1,0:T(8,128)}, f32[512,512]{1,0:T(8,128)}, f32[192,304]{1,0:T(8,128)}, f32[48,192]{1,0:T(8,128)}, /*...) custom-call(s32[3]{0:T(128)S(1)} %pad_add_fusion.at_ref, ...), custom_call_target="tpu_custom_call" | custom-call | tf_op jit(solution)/shard_map/pallas_call | solution.py:940
  (115 shorter events, 36.8 us)
Async XLA Ops:
  44.9 8.1 %collective-permute-start.1 = (bf16[192,512]{1,0:T(8,128)(2,1)S(1)}, bf16[192,512]{1,0:T(8,128)(2,1)S(1)}, u32[]{:S(2)}, u32[]{:S(2)}) collective-permute-start(bf16[192,512]{1,0:T(8,128)(2,1)S(1)} %add_convert_fusion.8.sum_a), channel_id=1, source_target_pairs={{0,2},{1,3},{2,0},{3,1},{4,6},{5,7},{6,4},{7,5},{8,10},{9,11},{10,... | collective-permute-start | bytes 589832 | tf_op jit(solution)/shard_map/ppermute | solution.py:524
  46.5 6.5 %collective-permute-start.3 = (bf16[192,128]{1,0:T(8,128)(2,1)S(1)}, bf16[192,128]{1,0:T(8,128)(2,1)S(1)}, u32[]{:S(2)}, u32[]{:S(2)}) collective-permute-start(bf16[192,128]{1,0:T(8,128)(2,1)S(1)} %add_convert_fusion.15.count_a), channel_id=1, source_target_pairs={{0,2},{1,3},{2,0},{3,1},{4,6},{5,7},{6,4},{7,5},{8,10},{9,11},{10,... | collective-permute-start | bytes 147464 | tf_op jit(solution)/shard_map/ppermute | solution.py:524
  97.1 6.7 %collective-permute-start.5 = (bf16[192,384]{1,0:T(8,128)(2,1)S(1)}, bf16[192,384]{1,0:T(8,128)(2,1)S(1)}, u32[]{:S(2)}, u32[]{:S(2)}) collective-permute-start(bf16[192,384]{1,0:T(8,128)(2,1)S(1)} %add_convert_fusion.14.back_a), channel_id=1, source_target_pairs={{0,2},{1,3},{2,0},{3,1},{4,6},{5,7},{6,4},{7,5},{8,10},{9,11},{10,... | collective-permute-start | bytes 442376 | tf_op jit(solution)/shard_map/ppermute | solution.py:524
  98.9 11.4 %collective-permute-start.8 = (bf16[1,416,192]{2,1,0:T(8,128)(2,1)S(1)}, bf16[1,416,192]{2,1,0:T(8,128)(2,1)S(1)}, u32[]{:S(2)}, u32[]{:S(2)}) collective-permute-start(bf16[1,416,192]{2,1,0:T(8,128)(2,1)S(1)} %constant_dynamic-slice_fusion.4), channel_id=1, source_target_pairs={{0,2},{1,3},{2,0},{3,1},{4,6},{5,7},{6,4},{7,5},{8,10},{9,11},{10,... | collective-permute-start | bytes 479240 | tf_op jit(solution)/shard_map/ppermute | solution.py:524
  110.0 14.5 %collective-permute-start.6 = (bf16[320,512]{1,0:T(8,128)(2,1)S(1)}, bf16[320,512]{1,0:T(8,128)(2,1)S(1)}, u32[]{:S(2)}, u32[]{:S(2)}) collective-permute-start(bf16[320,512]{1,0:T(8,128)(2,1)S(1)} %constant_dynamic-slice_fusion.6), channel_id=1, source_target_pairs={{0,4},{4,0},{8,12},{12,8},{16,20},{20,16},{24,28},{28,24},{1,5},{5... | collective-permute-start | bytes 983048 | tf_op jit(solution)/shard_map/ppermute | solution.py:524
  110.5 14.0 %collective-permute-start.9 = (bf16[320,512]{1,0:T(8,128)(2,1)S(1)}, bf16[320,512]{1,0:T(8,128)(2,1)S(1)}, u32[]{:S(2)}, u32[]{:S(2)}) collective-permute-start(bf16[320,512]{1,0:T(8,128)(2,1)S(1)} %add_convert_fusion.5), channel_id=1, source_target_pairs={{0,8},{4,12},{8,0},{12,4},{16,24},{20,28},{24,16},{28,20},{1,9},{5... | collective-permute-start | bytes 983048 | tf_op jit(solution)/shard_map/ppermute | solution.py:524
  125.6 7.1 %collective-permute-start.12 = (bf16[2,448,512]{2,1,0:T(8,128)(2,1)S(1)}, bf16[2,448,512]{2,1,0:T(8,128)(2,1)S(1)}, u32[]{:S(2)}, u32[]{:S(2)}) collective-permute-start(bf16[2,448,512]{2,1,0:T(8,128)(2,1)S(1)} %get-tuple-element.147), channel_id=1, source_target_pairs={{0,1},{1,0},{2,3},{3,2},{4,5},{5,4},{6,7},{7,6},{8,9},{9,8},{10,11... | collective-permute-start | bytes 2752520 | tf_op jit(solution)/shard_map/ppermute | solution.py:524
  125.7 6.9 %collective-permute-start.10 = (bf16[160,512]{1,0:T(8,128)(2,1)S(1)}, bf16[160,512]{1,0:T(8,128)(2,1)S(1)}, u32[]{:S(2)}, u32[]{:S(2)}) collective-permute-start(bf16[160,512]{1,0:T(8,128)(2,1)S(1)} %constant_dynamic-slice_fusion.3), channel_id=1, source_target_pairs={{0,8},{4,12},{8,0},{12,4},{16,24},{20,28},{24,16},{28,20},{1,9},{5... | collective-permute-start | bytes 491528 | tf_op jit(solution)/shard_map/ppermute | solution.py:524
  133.0 12.5 %collective-permute-start.14 = (bf16[448,512]{1,0:T(8,128)(2,1)S(1)}, bf16[448,512]{1,0:T(8,128)(2,1)}, u32[]{:S(2)}, u32[]{:S(2)}) collective-permute-start(bf16[448,512]{1,0:T(8,128)(2,1)S(1)} %constant_dynamic-slice_fusion), channel_id=1, source_target_pairs={{0,2},{1,3},{2,0},{3,1},{4,6},{5,7},{6,4},{7,5},{8,10},{9,11},{10,... | collective-permute-start | bytes 1376264 | tf_op jit(solution)/shard_map/ppermute | solution.py:524
  134.6 10.2 %collective-permute-start.13 = (bf16[2,80,512]{2,1,0:T(8,128)(2,1)S(1)}, bf16[2,80,512]{2,1,0:T(8,128)(2,1)S(1)}, u32[]{:S(2)}, u32[]{:S(2)}) collective-permute-start(bf16[2,80,512]{2,1,0:T(8,128)(2,1)S(1)} %constant_dynamic-slice_fusion.1), channel_id=1, source_target_pairs={{0,16},{4,20},{8,24},{12,28},{16,0},{20,4},{24,8},{28,12},{1,17},{... | collective-permute-start | bytes 491528 | tf_op jit(solution)/shard_map/ppermute | solution.py:524
  144.9 9.3 %collective-permute-start.15 = (bf16[2,80,512]{2,1,0:T(8,128)(2,1)S(1)}, bf16[2,80,512]{2,1,0:T(8,128)(2,1)S(1)}, u32[]{:S(2)}, u32[]{:S(2)}) collective-permute-start(bf16[2,80,512]{2,1,0:T(8,128)(2,1)S(1)} %add_convert_fusion.9), channel_id=1, source_target_pairs={{0,16},{4,20},{8,24},{12,28},{16,0},{20,4},{24,8},{28,12},{1,17},{... | collective-permute-start | bytes 491528 | tf_op jit(solution)/shard_map/ppermute | solution.py:524
  148.0 9.8 %collective-permute-start.18 = (bf16[144,512]{1,0:T(8,128)(2,1)}, bf16[144,512]{1,0:T(8,128)(2,1)}, u32[]{:S(2)}, u32[]{:S(2)}) collective-permute-start(bf16[144,512]{1,0:T(8,128)(2,1)} %get-tuple-element.186), channel_id=1, source_target_pairs={{0,12},{4,8},{8,4},{12,0},{16,28},{20,24},{24,20},{28,16},{1,13},{... | collective-permute-start | bytes 442376 | tf_op jit(solution)/shard_map/ppermute | solution.py:524
  149.2 8.6 %collective-permute-start.17 = (bf16[144,512]{1,0:T(8,128)(2,1)}, bf16[144,512]{1,0:T(8,128)(2,1)}, u32[]{:S(2)}, u32[]{:S(2)}) collective-permute-start(bf16[144,512]{1,0:T(8,128)(2,1)} %get-tuple-element.185), channel_id=1, source_target_pairs={{0,4},{4,0},{8,12},{12,8},{16,20},{20,16},{24,28},{28,24},{1,5},{5... | collective-permute-start | bytes 442376 | tf_op jit(solution)/shard_map/ppermute | solution.py:524
  151.1 9.0 %collective-permute-start.16 = (bf16[144,512]{1,0:T(8,128)(2,1)S(1)}, bf16[144,512]{1,0:T(8,128)(2,1)}, u32[]{:S(2)}, u32[]{:S(2)}) collective-permute-start(bf16[144,512]{1,0:T(8,128)(2,1)S(1)} %get-tuple-element.184), channel_id=1, source_target_pairs={{0,8},{4,12},{8,0},{12,4},{16,24},{20,28},{24,16},{28,20},{1,9},{5... | collective-permute-start | bytes 442376 | tf_op jit(solution)/shard_map/ppermute | solution.py:524
  154.3 22.8 %all-to-all-start.4 = ((bf16[8,32,512]{2,1,0:T(8,128)(2,1)}), bf16[8,32,512]{2,1,0:T(8,128)(2,1)S(1)}, u32[]{:S(2)}, u32[]{:S(2)}) async-start(bf16[8,32,512]{2,1,0:T(8,128)(2,1)} %bitcast.26), calls=%async_computation.4 | async-start | bytes 524288 | tf_op jit(solution)/shard_map/all_to_all | solution.py:619
  161.2 12.2 %collective-permute-start.20 = (bf16[144,512]{1,0:T(8,128)(2,1)S(1)}, bf16[144,512]{1,0:T(8,128)(2,1)S(1)}, u32[]{:S(2)}, u32[]{:S(2)}) collective-permute-start(bf16[144,512]{1,0:T(8,128)(2,1)S(1)} %add_convert_fusion.13), channel_id=1, source_target_pairs={{0,16},{4,20},{8,24},{12,28},{16,0},{20,4},{24,8},{28,12},{1,17},{... | collective-permute-start | bytes 442376 | tf_op jit(solution)/shard_map/ppermute | solution.py:524
  162.0 15.7 %collective-permute-start.19 = (bf16[160,512]{1,0:T(8,128)(2,1)S(1)}, bf16[160,512]{1,0:T(8,128)(2,1)}, u32[]{:S(2)}, u32[]{:S(2)}) collective-permute-start(bf16[160,512]{1,0:T(8,128)(2,1)S(1)} %get-tuple-element.151), channel_id=1, source_target_pairs={{0,8},{4,12},{8,0},{12,4},{16,24},{20,28},{24,16},{28,20},{1,9},{5... | collective-permute-start | bytes 491528 | tf_op jit(solution)/shard_map/ppermute | solution.py:524
  163.6 15.4 %collective-permute-start.22 = (bf16[160,512]{1,0:T(8,128)(2,1)S(1)}, bf16[160,512]{1,0:T(8,128)(2,1)S(1)}, u32[]{:S(2)}, u32[]{:S(2)}) collective-permute-start(bf16[160,512]{1,0:T(8,128)(2,1)S(1)} %get-tuple-element.153), channel_id=1, source_target_pairs={{0,4},{4,0},{8,12},{12,8},{16,20},{20,16},{24,28},{28,24},{1,5},{5... | collective-permute-start | bytes 491528 | tf_op jit(solution)/shard_map/ppermute | solution.py:524
  173.5 7.3 %collective-permute-start.26 = (bf16[144,512]{1,0:T(8,128)(2,1)S(1)}, bf16[144,512]{1,0:T(8,128)(2,1)S(1)}, u32[]{:S(2)}, u32[]{:S(2)}) collective-permute-start(bf16[144,512]{1,0:T(8,128)(2,1)S(1)} %add_convert_fusion.12.p0), channel_id=1, source_target_pairs={{0,8},{4,12},{8,0},{12,4},{16,24},{20,28},{24,16},{28,20},{1,9},{5... | collective-permute-start | bytes 442376 | tf_op jit(solution)/shard_map/ppermute | solution.py:524
  173.6 7.9 %collective-permute-start.27 = (bf16[144,512]{1,0:T(8,128)(2,1)S(1)}, bf16[144,512]{1,0:T(8,128)(2,1)S(1)}, u32[]{:S(2)}, u32[]{:S(2)}) collective-permute-start(bf16[144,512]{1,0:T(8,128)(2,1)S(1)} %add_convert_fusion.12.p0), channel_id=1, source_target_pairs={{0,4},{4,0},{8,12},{12,8},{16,20},{20,16},{24,28},{28,24},{1,5},{5... | collective-permute-start | bytes 442376 | tf_op jit(solution)/shard_map/ppermute | solution.py:524
  175.1 7.6 %collective-permute-start.28 = (bf16[144,512]{1,0:T(8,128)(2,1)S(1)}, bf16[144,512]{1,0:T(8,128)(2,1)S(1)}, u32[]{:S(2)}, u32[]{:S(2)}) collective-permute-start(bf16[144,512]{1,0:T(8,128)(2,1)S(1)} %add_convert_fusion.12.p0), channel_id=1, source_target_pairs={{0,12},{4,8},{8,4},{12,0},{16,28},{20,24},{24,20},{28,16},{1,13},{... | collective-permute-start | bytes 442376 | tf_op jit(solution)/shard_map/ppermute | solution.py:524
  178.9 10.7 %collective-permute-start.21 = (bf16[320,512]{1,0:T(8,128)(2,1)S(1)}, bf16[320,512]{1,0:T(8,128)(2,1)S(1)}, u32[]{:S(2)}, u32[]{:S(2)}) collective-permute-start(bf16[320,512]{1,0:T(8,128)(2,1)S(1)} %maximum_select_fusion.1.a0), channel_id=1, source_target_pairs={{0,4},{4,0},{8,12},{12,8},{16,20},{20,16},{24,28},{28,24},{1,5},{5... | collective-permute-start | bytes 983048 | tf_op jit(solution)/shard_map/ppermute | solution.py:524
  180.6 9.9 %collective-permute-start.23 = (bf16[320,512]{1,0:T(8,128)(2,1)S(1)}, bf16[320,512]{1,0:T(8,128)(2,1)S(1)}, u32[]{:S(2)}, u32[]{:S(2)}) collective-permute-start(bf16[320,512]{1,0:T(8,128)(2,1)S(1)} %maximum_select_fusion.2.b0), channel_id=1, source_target_pairs={{0,8},{4,12},{8,0},{12,4},{16,24},{20,28},{24,16},{28,20},{1,9},{5... | collective-permute-start | bytes 983048 | tf_op jit(solution)/shard_map/ppermute | solution.py:524
  180.8 9.7 %collective-permute-start.25 = (bf16[192,512]{1,0:T(8,128)(2,1)S(1)}, bf16[192,512]{1,0:T(8,128)(2,1)S(1)}, u32[]{:S(2)}, u32[]{:S(2)}) collective-permute-start(bf16[192,512]{1,0:T(8,128)(2,1)S(1)} %add_convert_fusion.7.back_a), channel_id=1, source_target_pairs={{0,2},{1,3},{2,0},{3,1},{4,6},{5,7},{6,4},{7,5},{8,10},{9,11},{10,... | collective-permute-start | bytes 589832 | tf_op jit(solution)/shard_map/ppermute | solution.py:524
  (21 other events, 387.7 us)

commit v4 on v3

--- a/solution.py
+++ b/solution.py
@@ -39,6 +39,12 @@
     half = 0.5 + 0.5 * t
     act = v * half
     return act, half + act * (1.0 - t) * (c0 + (3.0 * c1) * square)
+
+
+def gelu(v):
+    t = jnp.tanh(v * (0.7978845608028654 + (0.044715 * 0.7978845608028654) * (v * v)))
+    half = 0.5 * v
+    return half + half * t
 
 
 def norm_forward(values):
@@ -161,7 +167,7 @@
 
 def message_forward_kernel(
     col_ref, edges_ref, nodes_ref, far_ref, w1_ref, w2_ref, b1_ref, b2_ref,
-    act1_ref, d1_ref, d2_ref, sum_ref, table, own, acc,
+    act1_ref, pre1_ref, pre2_ref, sum_ref, table, own, acc,
 ):
     step = pl.program_id(0)
     last = pl.num_programs(0) - 1
@@ -181,18 +187,20 @@
     columns = columns_of(col_ref, step * kt, kt)
     hot = jnp.concatenate([one_hot(column, width) for column in columns], axis=0)
     pre1 = spread(own[...], mm(hot, table[...]) + mm(edge, w1_ref[2 * D :, :]))
-    act, slope = gelu_pair(pre1)
-    act1 = act.astype(bf16)
+    pre1_ref[...] = pre1.astype(bf16)
+    act1 = gelu(pre1).astype(bf16)
     act1_ref[...] = act1
-    d1_ref[...] = slope.astype(bf16)
-    act, slope = gelu_pair(mm(act1, w2_ref[...]) + row_of(b2_ref))
-    weight = kept_weight(columns)
-    d2_ref[...] = (slope * weight).astype(bf16)
-    acc[...] += gathered(act.astype(bf16).astype(f32) * weight, rows)
+    pre2 = jnp.where(kept_weight(columns) > 0.0, mm(act1, w2_ref[...]) + row_of(b2_ref), -30.0)
+    pre2_ref[...] = pre2.astype(bf16)
+    acc[...] += gathered(gelu(pre2), rows)
 
     @pl.when(step == last)
     def _():
         sum_ref[...] = acc[...].astype(bf16)
+
+
+def slope_kernel(pre_ref, slope_ref):
+    slope_ref[...] = gelu_pair(pre_ref[...].astype(f32))[1].astype(bf16)
 
 
 def node_forward_kernel(
@@ -230,9 +238,9 @@
 
 
 def edge_kernel(
-    order, row_ref, col_ref, edges_ref, cot_ref, sent_ref, far_ref, w1_ref, w2_ref, w3_ref, b1_ref, b2_ref, b3_ref, gain_ref, shift_ref,
-    out_ref, base_ref, own_ref, far_grad_ref, local_grad_ref, packed_ref,
-    table, own, sums, w1_acc, w2_acc, w3_acc, bias_acc, own_acc,
+    row_ref, col_ref, edges_ref, cot_ref, sent_ref, far_ref, w1_ref, w2_ref, w3_ref, b1_ref, b2_ref, b3_ref, gain_ref, shift_ref,
+    out_ref, base_ref, own_ref, far_grad_ref, local_grad_ref, w1_acc, w2_acc, w3_acc, bias_acc,
+    table, own, sums, own_acc,
 ):
     step = pl.program_id(0)
     last = pl.num_programs(0) - 1
@@ -289,30 +297,43 @@
     @pl.when(step == last)
     def _():
         total = sums[...]
-        own_low = own_acc[...].astype(bf16)
-        own_ref[...] = own_low
+        own_ref[...] = own_acc[...].astype(bf16)
         far_grad_ref[...] = total[:n_far].astype(bf16)
         local_grad_ref[...] = total[n_far:].astype(bf16)
-        sent = sent_ref[...]
-        parts = len(order)
-        first = (2 * D + E) // parts
-        second = E // parts
-        whole = jnp.concatenate(
+
+
+def edge_weights_kernel(
+    order, sent_ref, far_ref, own_ref, far_grad_ref, local_grad_ref, w1_ref, w2_ref, w3_ref, bias_ref, packed_ref
+):
+    parts = len(order)
+    first, second = (2 * D + E) // parts, E // parts
+    sent = sent_ref[...]
+    whole = jnp.concatenate(
+        [
+            mm_tn(sent, own_ref[...]),
+            mm_tn(far_ref[...], far_grad_ref[...]) + mm_tn(sent, local_grad_ref[...]),
+            w1_ref[...],
+        ],
+        axis=0,
+    ).astype(bf16)
+    second_w = w2_ref[...].astype(bf16)
+    third_w = w3_ref[...].astype(bf16)
+    bias = bias_ref[...].astype(bf16)
+    half = packed_ref.shape[1]
+    for q, n in enumerate(order):
+        rows = jnp.concatenate(
             [
-                mm_tn(sent, own_low),
-                mm_tn(far_ref[...], total[:n_far].astype(bf16)) + mm_tn(sent, total[n_far:].astype(bf16)),
-                w1_acc[...],
+                whole[n * first : (n + 1) * first],
+                second_w[n * second : (n + 1) * second],
+                third_w[n * second : (n + 1) * second],
+                bias,
             ],
             axis=0,
-        ).astype(bf16)
-        second_w = w2_acc[...].astype(bf16)
-        third_w = w3_acc[...].astype(bf16)
-        bias = bias_acc[...].astype(bf16)
-        for q, n in enumerate(order):
-            packed_ref[q, :first, :] = whole[n * first : (n + 1) * first]
-            packed_ref[q, first : first + second, :] = second_w[n * second : (n + 1) * second]
-            packed_ref[q, first + second : first + 2 * second, :] = third_w[n * second : (n + 1) * second]
-            packed_ref[q, first + 2 * second :, :] = bias
+        )
+        packed_ref[q, :, :E] = rows[:half]
+        packed_ref[q, :, 256 : 256 + E] = rows[half:]
+        packed_ref[q, :, E:256] = jnp.zeros((half, 256 - E), bf16)
+        packed_ref[q, :, 256 + E :] = jnp.zeros((half, 256 - E), bf16)
 
 
 def returned_kernel(own_ref, local_ref, back_ref, want_ref, out_ref):
@@ -328,30 +349,35 @@
     out_ref[...] = grad.astype(bf16)
 
 
+def fetch_kernel(*refs):
+    *refs, arrivals = refs
+    count = len(refs) // 2
+    copies = [pltpu.make_async_copy(refs[i], refs[count + i], arrivals.at[i]) for i in range(count)]
+    for copy in copies:
+        copy.start()
+    for copy in copies:
+        copy.wait()
+
+
+def fetched(*values):
+    size = sum(value.size * value.dtype.itemsize for value in values)
+    return pl.pallas_call(
+        fetch_kernel,
+        out_shape=tuple(pltpu.VMEM(value.shape, value.dtype) for value in values),
+        in_specs=[pl.BlockSpec(memory_space=pltpu.HBM)] * len(values),
+        out_specs=tuple(pl.BlockSpec(memory_space=pltpu.VMEM) for _ in values),
+        scratch_shapes=[pltpu.SemaphoreType.DMA((len(values),))],
+        compiler_params=pltpu.CompilerParams(vmem_limit_bytes=VMEM),
+        cost_estimate=pl.CostEstimate(flops=0, bytes_accessed=2 * size, transcendentals=0),
+    )(*read(*values))
+
+
 def node_backward_kernel(
-    parts, place_ref, back_a, back_b, count_a, count_b, cot_ref, mask_ref, inv1_ref, normed2_ref, inv2_ref, ew1_ref,
-    gain1_ref, gain2_ref, f2_far, slope_far, f1_far, normed1_far, w3_far, low_far, hid_far, total_far,
-    mixed_ref, up_ref, bias_ref, packed_ref, w3_grad_ref,
-    f2_ref, slope_ref, f1_ref, normed1_ref, w3_ref, low_ref, hid_ref, total_ref, arrivals,
+    parts, place_ref, back_a, back_b, count_a, count_b, cot_ref, normed2_ref, ew1_ref, f2_ref, slope_ref, f1_ref,
+    normed1_ref, w3_ref, low_ref, hid_ref, total_ref, mask_ref, inv1_ref, inv2_ref, gain1_ref, gain2_ref,
+    mixed_ref, up_ref, bias_ref, packed_ref,
 ):
     rows = cot_ref.shape[0]
-    fetches = [
-        pltpu.make_async_copy(source, target, arrivals.at[i])
-        for i, (source, target) in enumerate(
-            (
-                (f2_far, f2_ref),
-                (slope_far, slope_ref),
-                (f1_far, f1_ref),
-                (normed1_far, normed1_ref),
-                (w3_far, w3_ref),
-                (low_far, low_ref),
-                (hid_far, hid_ref),
-                (total_far, total_ref),
-            )
-        )
-    ]
-    for fetch in fetches:
-        fetch.start()
     place = place_ref[0]
     present = present_column(mask_ref, rows)
     count = (count_a[...].astype(f32) + count_b[...].astype(f32))[:, :1]
@@ -361,17 +387,12 @@
     normed2 = normed2_ref[...]
     sum_grad = norm_backward(up, normed2, inv2_ref[...], row_of(gain2_ref))
     branch_grad = sum_grad.astype(bf16)
-    fetches[0].wait()
-    fetches[1].wait()
     hidden_grad = (slope_ref[...].astype(f32) * mm_nt(branch_grad, f2_ref[...])).astype(bf16)
-    fetches[2].wait()
     first_grad = sum_grad + mm_nt(hidden_grad, f1_ref[...])
-    fetches[3].wait()
     normed1 = normed1_ref[...]
     mixed_grad = norm_backward(first_grad, normed1, inv1_ref[...], row_of(gain1_ref))
     mixed_ref[...] = mixed_grad
     message_grad = (mixed_grad / jnp.maximum(count, 1.0)).astype(bf16)
-    fetches[4].wait()
     up_ref[...] = mm_nt(message_grad, w3_ref[...])
     row = iota((16, 1), 0)
     hidden_sum = column_sum(hidden_grad.astype(f32))
@@ -387,17 +408,16 @@
         bias = bias + jnp.where(row == 8 + j, hidden_sum[:, j * D : (j + 1) * D], 0.0)
     bias_ref[...] = bias * (1.0 / parts)
     wide, narrow = FF // parts, D // parts
-    for fetch in fetches[5:]:
-        fetch.wait()
     low = low_ref[:, pl.ds(pl.multiple_of(place * narrow, narrow), narrow)]
     for j in range(FF // D):
         packed_ref[j * narrow : (j + 1) * narrow, :] = mm_tn(low, hidden_grad[:, j * D : (j + 1) * D]).astype(bf16)
     hid = hid_ref[:, pl.ds(pl.multiple_of(place * wide, wide), wide)]
     packed_ref[D : D + wide, :] = mm_tn(hid, branch_grad).astype(bf16)
     total = total_ref[:, pl.ds(pl.multiple_of(place * narrow, narrow), narrow)]
-    w3_grad_ref[...] = mm_tn(total, message_grad).astype(bf16)
-    at = D + wide
-    packed_ref[at:, :] = jnp.zeros((packed_ref.shape[0] - at, D), bf16)
+    packed_ref[D + wide : D + wide + narrow, :] = mm_tn(total, message_grad).astype(bf16)
+    at = D + wide + narrow
+    if packed_ref.shape[0] > at:
+        packed_ref[at:, :] = jnp.zeros((packed_ref.shape[0] - at, D), bf16)
 
 
 def message_backward_kernel(
@@ -419,18 +439,20 @@
 
     edge = edges_ref[...].reshape(kt * rows, E)
     slope2 = d2_ref[...].astype(f32).reshape(kt, rows, D)
-    low2 = (slope2 * up_ref[...][None]).astype(bf16).reshape(kt * rows, D)
+    grad2 = (slope2 * up_ref[...][None]).reshape(kt * rows, D)
+    low2 = grad2.astype(bf16)
     w2_acc[...] += mm_tn(act1_ref[...], low2)
-    low1 = (d1_ref[...].astype(f32) * mm_nt(low2, w2_ref[...])).astype(bf16)
+    grad1 = d1_ref[...].astype(f32) * mm_nt(low2, w2_ref[...])
+    low1 = grad1.astype(bf16)
     w1_acc[...] += mm_tn(edge, low1)
     slot_sums(row_ref, step * kt, kt, width, low1, sums)
     grad = base_ref[...] + mm_nt(low1, w1_ref[2 * D :, :])
     out_ref[...] = grad.reshape(kt, rows, E)
-    own_sum = gathered(low1.astype(f32), rows)
+    own_sum = gathered(grad1, rows)
     own_acc[...] += own_sum
     row = iota((16, 1), 0)
     bias_acc[...] += jnp.where(row == 0, column_sum(own_sum), 0.0) + jnp.where(
-        row == 1, column_sum(low2.astype(f32)), 0.0
+        row == 1, column_sum(grad2), 0.0
     )
 
     @pl.when(step == last)
@@ -475,49 +497,49 @@
 
 
 def node_weights_kernel(
-    parts, half, at_ref, a0, a1, b0, b1, mixed_ref, back_a, back_b, nodes_ref,
-    f1_ref, f2_ref, ew1_ref, ew2_ref, ew3_ref, eb1_ref, eb2_ref, eb3_ref, eg_ref, es_ref, whole,
+    parts, at_ref, a0, a1, b0, b1, mixed_ref, back_a, back_b, nodes_ref, f1_ref, f2_ref, w3_ref, whole
 ):
     nodes_ref[...] = mixed_ref[...] + (back_a[...].astype(f32) + back_b[...].astype(f32))
     top = whole.shape[0] // 2
     low, high = whole.at[:top], whole.at[top:]
-    joined(low, at_ref[1], a0)
-    joined(low, 1 - at_ref[1], a1)
-    joined(high, at_ref[2], b0)
-    joined(high, 1 - at_ref[2], b1)
-    place = at_ref[0]
+    joined(low, at_ref[0], a0)
+    joined(low, 1 - at_ref[0], a1)
+    joined(high, at_ref[1], b0)
+    joined(high, 1 - at_ref[1], b1)
     wide, narrow = FF // parts, D // parts
     for j in range(FF // D):
         f1_ref[:, j * D : (j + 1) * D] = whole[j * narrow : (j + 1) * narrow, :].astype(f32)
-    at = D + wide
-    f2_ref[...] = whole[D:at, :].astype(f32)
-    edge = jnp.concatenate([whole[at : at + half, :E], whole[at : at + half, 256 : 256 + E]], axis=0).astype(f32)
-    first, second = (2 * D + E) // parts, E // parts
-    ew1_ref[...] = edge[:first].T
-    ew2_ref[...] = edge[first : first + second]
-    ew3_ref[...] = edge[first + second : first + 2 * second]
-    rows = picked_lanes(edge[first + 2 * second : first + 2 * second + 8], place, parts)
-    for j, ref in enumerate((eb1_ref, eb2_ref, eb3_ref, eg_ref, es_ref)):
-        ref[...] = rows[j : j + 1].reshape(second)
-
-
-def message_weights_kernel(parts, at_ref, p0, p1, p2, p3, w1_ref, w2_ref, w3_ref, *refs):
+    f2_ref[...] = whole[D : D + wide, :].astype(f32)
+    w3_ref[...] = whole[D + wide : D + wide + narrow, :].astype(f32)
+
+
+def edge_message_weights_kernel(
+    parts, half, at_ref, p0, p1, p2, p3, w1_ref, w2_ref, ew1_ref, ew2_ref, ew3_ref, *refs
+):
     *vectors, fb1_ref, whole = refs
     for mask, piece in enumerate((p0, p1, p2, p3)):
         joined(whole, at_ref[1] ^ mask, piece)
     place = at_ref[0]
-    first, narrow = (2 * D + E) // parts, D // parts
+    first, narrow, second = (2 * D + E) // parts, D // parts, E // parts
     w1_ref[...] = whole[:first, :].astype(f32)
     w2_ref[...] = whole[first : first + narrow, :].astype(f32)
-    w3_ref[...] = whole[first + narrow + 16 : first + 2 * narrow + 16, :].astype(f32)
-    bias = whole[first + narrow : first + narrow + 16, :].astype(f32)
+    at = first + narrow
+    bias = whole[at : at + 16, :].astype(f32)
     rows = picked_lanes(bias[:8], place, parts)
-    for j, ref in enumerate(vectors):
+    for j, ref in enumerate(vectors[5:]):
         ref[...] = rows[j : j + 1].reshape(narrow)
     hidden = jnp.zeros((1, D), f32)
     for n in range(FF // D):
         hidden = hidden + jnp.where(place == n, bias[8 + n : 9 + n], 0.0)
     fb1_ref[...] = hidden.reshape(FF // parts)
+    at += 16
+    edge = jnp.concatenate([whole[at : at + half, :E], whole[at : at + half, 256 : 256 + E]], axis=0).astype(f32)
+    ew1_ref[...] = edge[:first].T
+    ew2_ref[...] = edge[first : first + second]
+    ew3_ref[...] = edge[first + second : first + 2 * second]
+    rows = picked_lanes(edge[first + 2 * second : first + 2 * second + 8], place, parts)
+    for j, ref in enumerate(vectors[:5]):
+        ref[...] = rows[j : j + 1].reshape(second)
 
 
 def swap(values, axis, bit):
@@ -729,7 +751,7 @@
     edge_tile = tiled(kt, rows, E)
     flat = tiled(kt * rows, D)
     flat_edge = tiled(kt * rows, E)
-    act1, d1, d2, act_sum = call(
+    act1, pre1, pre2, act_sum = call(
         message_forward_kernel,
         (stored((total, D), bf16), stored((total, D), bf16), stored((total, D), bf16), shape((rows, D), bf16)),
         scratch=[pltpu.VMEM((width, D), bf16), pltpu.VMEM((rows, D), f32), pltpu.VMEM((rows, D), f32)],
@@ -747,7 +769,20 @@
         out_specs=(flat, flat, flat, fixed(rows, D)),
         cost=pl.CostEstimate(flops=16 * total * D * D, bytes_accessed=total * D * 8, transcendentals=2 * total * D),
     )(*read(place_col, edges, nodes), far_nodes, *read(msg_w1, msg_w2, msg_b1, msg_b2))
+
+    def slope_of(pre):
+        return call(
+            slope_kernel,
+            stored((total, D), bf16),
+            grid=grid,
+            in_specs=[flat],
+            out_specs=flat,
+            cost=pl.CostEstimate(flops=10 * total * D, bytes_accessed=total * D * 4, transcendentals=total * D),
+        )(*read(pre))
+
+    d1 = slope_of(pre1)
     sum_a, sum_b = shared_sum(act_sum, "nbr")
+    sum_b = after(sum_b, d1)
 
     total_act, first_low, normed1, inv1, hidden, hidden_slope, normed2, inv2, sent, send = call(
         node_forward_kernel,
@@ -765,28 +800,28 @@
         ),
     )(sum_a, sum_b, count_a, count_b, nodes, mask_row, wanted, msg_w3, ffn_w1, ffn_w2,
       msg_b3, norm1_gain, norm1_bias, ffn_b1, ffn_b2, norm2_gain, norm2_bias)
-    far_sent = exchange(send, blocks)
+    d2 = slope_of(after(pre2, send))
+    far_sent = after(exchange(send, blocks), d2)
 
     first_rows, second_rows = (2 * D + E) // parts, E // parts
-    edge_rows = up_to(first_rows + 2 * second_rows + 16, 32)
-    edges_out, base, own_sum, far_sum, local_sum, edge_packed = call(
-        functools.partial(edge_kernel, order),
+    edge_rows = up_to(first_rows + 2 * second_rows + 16, 32) // 2
+    edges_out, base, own_sum, far_sum, local_sum, *edge_sums = call(
+        edge_kernel,
         (
             shape((kn, rows, E), bf16),
             stored((total, E), f32),
             stored((rows, E), bf16),
             stored((n_far, E), bf16),
             stored((rows, E), bf16),
-            shape((parts, edge_rows, E), bf16),
+            stored((E, E), f32),
+            stored((E, E), f32),
+            stored((E, E), f32),
+            stored((16, E), f32),
         ),
         scratch=[
             pltpu.VMEM((width, E), bf16),
             pltpu.VMEM((rows, E), f32),
             pltpu.VMEM((width, E), f32),
-            pltpu.VMEM((E, E), f32),
-            pltpu.VMEM((E, E), f32),
-            pltpu.VMEM((E, E), f32),
-            pltpu.VMEM((16, E), f32),
             pltpu.VMEM((rows, E), f32),
         ],
         grid=grid,
@@ -808,59 +843,53 @@
             fixed(rows, E),
             fixed(n_far, E),
             fixed(rows, E),
-            fixed(parts, edge_rows, E),
+            fixed(E, E),
+            fixed(E, E),
+            fixed(E, E),
+            fixed(16, E),
         ),
         cost=pl.CostEstimate(flops=16 * total * D * D, bytes_accessed=total * E * 12, transcendentals=2 * total * E),
     )(*read(place_row, place_col, edges, edge_cot, sent), far_sent, *read(edge_w1, edge_w2, edge_w3),
       *read(edge_b1, edge_b2, edge_b3, norm3_gain, norm3_bias))
 
-    far_back, edge_packed = together((exchange(far_sum, blocks), edge_packed))
+    edge_packed = call(
+        functools.partial(edge_weights_kernel, order),
+        stored((parts, edge_rows, D), bf16),
+        cost=pl.CostEstimate(flops=10**9, bytes_accessed=10**6, transcendentals=0),
+    )(*read(sent, far_sent, own_sum, far_sum, local_sum, *edge_sums))
+    far_back = after(exchange(far_sum, blocks), edge_packed)
     back = call(returned_kernel, shape((rows, 2 * E), bf16))(*read(own_sum, local_sum), far_back, wanted)
     for bit in nbr_bits[:-1]:
         back = add_low(back, swap(back, "nbr", bit))
-    back, edge_packed = together((back, edge_packed))
+    kept = fetched(
+        after(node_cot, back), normed2, edge_w1, ffn_w2, hidden_slope, ffn_w1, normed1, msg_w3, first_low, hidden, total_act
+    )
     back_a, back_b = back, swap(back, "nbr", nbr_bits[-1])
-    edge_part = scattered_sum(edge_packed, "nbr", nbr_bits).reshape(edge_rows, E)
 
     wide, narrow = FF // parts, D // parts
-    node_rows = up_to(D + wide + edge_rows // 2, 16 * blocks)
-    mixed_grad, up, node_bias, node_packed, msg_w3_part = call(
+    node_rows = up_to(D + wide + narrow, 16 * blocks)
+    mixed_grad, up, node_bias, node_packed = call(
         functools.partial(node_backward_kernel, parts),
         (
             shape((rows, D), f32),
             shape((rows, D), f32),
             shape((16, D), f32),
             shape((node_rows, D), bf16),
-            shape((narrow, D), bf16),
         ),
-        scratch=[
-            pltpu.VMEM((FF, D), bf16),
-            pltpu.VMEM((rows, FF), bf16),
-            pltpu.VMEM((D, FF), bf16),
-            pltpu.VMEM((rows, D), f32),
-            pltpu.VMEM((D, D), bf16),
-            pltpu.VMEM((rows, D), bf16),
-            pltpu.VMEM((rows, FF), bf16),
-            pltpu.VMEM((rows, D), bf16),
-            pltpu.SemaphoreType.DMA((8,)),
-        ],
-        in_specs=[smem] + [vmem] * 12 + [pl.BlockSpec(memory_space=pltpu.HBM)] * 8,
+        in_specs=[smem] + [vmem] * 20,
     )(
-        nbr_place, back_a, back_b, count_a, count_b, *read(node_cot, mask_row, inv1, normed2, inv2, edge_w1),
-        *read(norm1_gain, norm2_gain, ffn_w2, hidden_slope, ffn_w1, normed1, msg_w3, first_low, hidden, total_act),
+        nbr_place, back_a, back_b, count_a, count_b, *kept, mask_row, inv1, inv2, norm1_gain, norm2_gain,
     )
     bits = bits_of("res")
     order_a, order_b = bits, bits[1:2] + bits[:1] + bits[2:]
     rows_ab = node_rows // 2
     part_a = halve([(node_packed, 0)], rows_ab, "res", order_a[0])
-    lead = D + wide - rows_ab
-    edge_pair = jnp.pad(edge_part.reshape(2, edge_rows // 2, E), ((0, 0), (0, 0), (0, 256 - E)))
-    edge_pair = jnp.concatenate([edge_pair[0], edge_pair[1]], axis=1)
-    edge_pair = jnp.pad(edge_pair, ((lead, rows_ab - lead - edge_rows // 2), (0, 0)))
-    part_b = halve([(node_packed, rows_ab), (edge_pair, 0)], rows_ab, "res", order_b[0])
+    part_b = halve([(node_packed, rows_ab)], rows_ab, "res", order_b[0])
+    edge_packed = after(edge_packed, up)
+    edge_part = scattered_sum(edge_packed.reshape(parts * edge_rows, D), "nbr", nbr_bits)
 
     msg_rows = first_rows + narrow + 16
-    share_rows = up_to(msg_rows + narrow, 8 * blocks)
+    share_rows = up_to(msg_rows + edge_rows, max(64, 8 * blocks))
     edges_grad, own_sum, far_sum, local_sum, msg_kept, msg_given = call(
         functools.partial(message_backward_kernel, parts),
         (
@@ -911,17 +940,17 @@
     both = after(jnp.stack([part_a, part_b]), msg_part)
     msg_sum = scattered_sum(msg_part, "nbr", nbr_bits[1:])
     both = halved_sum(both, "res", last, 1)
-    msg_sum = jnp.concatenate([msg_sum, msg_w3_part, jnp.zeros((share_rows - msg_rows - narrow, D), bf16)], axis=0)
+    msg_sum = jnp.concatenate([msg_sum, edge_part, jnp.zeros((share_rows - msg_rows - edge_rows, D), bf16)], axis=0)
     msg_quarter = quarter_sum(msg_sum, "res", bits[:2])
-    both = rejoined(after(both, msg_sum) if 4 == 4 else both, "res", last, 1)
-    far_back = exchange(after(far_sum, both), blocks)
+    both = rejoined(after(both, msg_sum), "res", last, 1)
+    far_back = exchange(after(far_sum, msg_sum), blocks)
     back = call(returned_last_kernel, shape((rows, D), bf16))(own_sum, local_sum, far_back, wanted, msg_w1)
     for bit in nbr_bits[:-1]:
         back = add_low(back, swap(back, "nbr", bit))
     back_b = swap(back, "nbr", nbr_bits[-1])
     msg_part = scattered_sum(msg_quarter, "res", middle)
     msg_part = add_low(msg_part, swap(msg_part, "res", last))
-    part_a, part_b = after(both[0], msg_quarter), after(both[1], msg_quarter)
+    part_a, part_b = both[0], both[1]
     part_a = rejoined(gathered_rows(part_a, "res", middle[::-1]), "res", order_a[1])
     part_b = rejoined(gathered_rows(part_b, "res", middle[::-1]), "res", order_b[1])
     part_a, part_b = after(part_a, msg_part), after(part_b, msg_part)
@@ -932,31 +961,29 @@
     def side(bit):
         return (lax.axis_index("res") // bit) & 1
 
-    node_at = jnp.stack([lax.axis_index("nbr"), side(order_a[0]), side(order_b[0])]).astype(jnp.int32)
+    node_at = jnp.stack([side(order_a[0]), side(order_b[0])]).astype(jnp.int32)
     msg_at = jnp.stack([lax.axis_index("nbr"), 2 * side(bits[0]) + side(bits[1])]).astype(jnp.int32)
+    nodes_grad, ffn_w1_grad, ffn_w2_grad, msg_w3_grad = call(
+        functools.partial(node_weights_kernel, parts),
+        (shape((rows, D), f32), shape((narrow, FF), f32), shape((wide, D), f32), shape((narrow, D), f32)),
+        scratch=[pltpu.VMEM((node_rows, D), bf16)],
+        in_specs=[smem] + [vmem] * 7,
+    )(node_at, part_a, other_a, part_b, other_b, mixed_grad, back, back_b)
     (
-        nodes_grad, ffn_w1_grad, ffn_w2_grad, edge_w1_grad, edge_w2_grad, edge_w3_grad,
+        msg_w1_grad, msg_w2_grad, edge_w1_grad, edge_w2_grad, edge_w3_grad,
         edge_b1_grad, edge_b2_grad, edge_b3_grad, norm3_gain_grad, norm3_bias_grad,
+        msg_b1_grad, msg_b2_grad, msg_b3_grad, norm1_gain_grad, norm1_bias_grad,
+        ffn_b2_grad, norm2_gain_grad, norm2_bias_grad, ffn_b1_grad,
     ) = call(
-        functools.partial(node_weights_kernel, parts, edge_rows // 2),
+        functools.partial(edge_message_weights_kernel, parts, edge_rows),
         (
-            shape((rows, D), f32),
-            shape((narrow, FF), f32),
-            shape((wide, D), f32),
+            shape((first_rows, D), f32),
+            shape((narrow, D), f32),
             shape((E, first_rows), f32),
             shape((second_rows, E), f32),
             shape((second_rows, E), f32),
         )
-        + (shape((second_rows,), f32),) * 5,
-        scratch=[pltpu.VMEM((node_rows, D), bf16)],
-        in_specs=[smem] + [vmem] * 7,
-    )(node_at, part_a, other_a, part_b, other_b, mixed_grad, back, back_b)
-    (
-        msg_w1_grad, msg_w2_grad, msg_w3_grad, msg_b1_grad, msg_b2_grad, msg_b3_grad, norm1_gain_grad, norm1_bias_grad,
-        ffn_b2_grad, norm2_gain_grad, norm2_bias_grad, ffn_b1_grad,
-    ) = call(
-        functools.partial(message_weights_kernel, parts),
-        (shape((first_rows, D), f32), shape((narrow, D), f32), shape((narrow, D), f32))
+        + (shape((second_rows,), f32),) * 5
         + (shape((narrow,), f32),) * 8
         + (shape((wide,), f32),),
         scratch=[pltpu.VMEM((share_rows, D), bf16)],

time: 194 us -> 184 us (0.948)
  blocking collectives: 46.8 us -> 24.6 us
  Pallas kernels: 60.4 us -> 71.6 us
  starting transfers between devices: 29.6 us -> 38.9 us
  waiting for transfers between devices: 46.9 us -> 40.4 us
  other arithmetic: 6.43 us -> 4.05 us
    all_to_all x4 -> x2, blocking collectives: 46.8 us -> 24.6 us  [exchange(): return lax.all_to_all(shaped, 'res', 0, 0, tiled=True).reshape(values.shape)]
    pallas_call x3 -> x7, Pallas kernels: 18.8 us -> 36.6 us  [the longest x1 14.8 us: on_device(): call(edge_kernel, (shape((kn, rows, E), bf16), stored((total, E), f32), s...]
    ppermute x29, waiting for transfers between devices: 46.9 us -> 32.8 us  [swap(): lax.ppermute(values, axis, [(i, i ^ bit) for i in range(lax.axis_size(axi...]
    all_to_all x1 -> x3, starting transfers between devices: 3.56 us -> 11.3 us  [exchange(): return lax.all_to_all(shaped, 'res', 0, 0, tiled=True).reshape(values.shape)]
    all_to_all x1 -> x3, waiting for transfers between devices: 0.01 us -> 7.59 us  [exchange(): return lax.all_to_all(shaped, 'res', 0, 0, tiled=True).reshape(values.shape)]
    pallas_call x1, Pallas kernels: 6.15 us -> 2.62 us  [on_device(): call(functools.partial(node_backward_kernel, parts), (shape((rows, D), f3...]
    pallas_call x1, Pallas kernels: 13.9 us -> 11 us  [on_device(): call(message_forward_kernel, (stored((total, D), bf16), stored((total, D)...]
  transfers between devices with their start and end apart: 30 -> 32, of which waited for: 15 -> 18; matrix products, arithmetic and copies ran while one was open for 3% -> 2% of each run, Pallas kernels for 11% -> 18%
where the time goes in v4:
time: 184 us; the launch traced here: 183 us
  Pallas kernels  71.6 us (39%)
  waiting for transfers between devices  40.4 us (22%)
  starting transfers between devices  38.9 us (21%)
  blocking collectives  24.6 us (13%)
  other arithmetic  4.05 us (2%)
    ppermute x29, waiting for transfers between devices, swap(): lax.ppermute(values, axis, [(i, i ^ bit) for i in range(lax.axis_size(axi...  32.8 us
    ppermute x29, starting transfers between devices, swap(): lax.ppermute(values, axis, [(i, i ^ bit) for i in range(lax.axis_size(axi...  27.6 us
    all_to_all x2, blocking collectives, exchange(): return lax.all_to_all(shaped, 'res', 0, 0, tiled=True).reshape(values.shape)  24.6 us
    pallas_call x1, Pallas kernels, on_device(): call(edge_kernel, (shape((kn, rows, E), bf16), stored((total, E), f32), s...  14.8 us
    pallas_call x1, Pallas kernels, on_device(): call(functools.partial(message_backward_kernel, parts), (shape((kn, rows,...  12.7 us
    pallas_call x2, Pallas kernels, slope_of(): call(slope_kernel, stored((total, D), bf16), grid=grid, in_specs=[flat],...  11.6 us
    all_to_all x3, starting transfers between devices, exchange(): return lax.all_to_all(shaped, 'res', 0, 0, tiled=True).reshape(values.shape)  11.3 us
    pallas_call x1, Pallas kernels, on_device(): call(message_forward_kernel, (stored((total, D), bf16), stored((total, D)...  11 us
  transfers between devices with their start and end apart: 32, of which 18 were waited for; matrix products, arithmetic and copies ran while one was open for 2% of the time, Pallas kernels for 18%

profile of v4, /device:TPU:0, one launch (start us, length us, event | category | flops | bytes accessed | tf_op | source)
XLA Modules:
  0.0 183.1 jit_solution(9977047505473104886)
XLA Ops:
  0.7 2.8 %shard_map.467 = (s32[16,192]{1,0:T(8,128)S(1)}, f32[192,16]{1,0:T(8,128)S(1)}, bf16[256,128]{1,0:T(8,128)(2,1)S(1)}, bf16[192,128]{1,0:T(8,128)(2,1)S(1)}) custom-call(s32[1]{0:T(128)} %bitcast.me_ref, s32[15,192]{1,0:T(8,128)} %bitcast.56, s32[1,192]{1,0:T(1,128)} %bitcast.45), custom_call_target="tpu_custom_call" | custom-call | tf_op jit(solution)/shard_map/pallas_call | solution.py:733
  3.5 14.0 %all_to_all.25 = bf16[8,32,128]{2,1,0:T(8,128)(2,1)S(1)} all-to-all(bf16[8,32,128]{2,1,0:T(8,128)(2,1)S(1)} %bitcast.44), channel_id=1, replica_groups=mesh['res'=8,'nbr'=4] {'res'}, dimensions={0} | all-to-all | bytes 131072 | tf_op jit(solution)/shard_map/all_to_all | solution.py:641
  18.8 10.6 %all_to_all.26 = bf16[8,32,512]{2,1,0:T(8,128)(2,1)S(1)} all-to-all(bf16[8,32,512]{2,1,0:T(8,128)(2,1)S(1)} %bitcast.50), channel_id=1, replica_groups=mesh['res'=8,'nbr'=4] {'res'}, dimensions={0} | all-to-all | bytes 524288 | tf_op jit(solution)/shard_map/all_to_all | solution.py:641
  29.4 11.0 %shard_map.468 = (bf16[2880,512]{1,0:T(8,128)(2,1)}, bf16[2880,512]{1,0:T(8,128)(2,1)}, bf16[2880,512]{1,0:T(8,128)(2,1)}, bf16[192,512]{1,0:T(8,128)(2,1)S(1)}) custom-call(f32[192,16]{1,0:T(8,128)} %copy-done.18, bf16[15,192,192]{2,1,0:T(8,128)(2,1)} %bitcast.58, bf16[192,512]{1,0:T(8,128)(2,1)} %nodes_ref.5, bf16[256,512]{1,0:T(8,128)(2,1)S(1)} %bitcast.40, ...), custom_call_target="tpu_custom_call" | custom-call | flops 12079595520 | bytes 11796480 | tf_op jit(solution)/shard_map/pallas_call | solution.py:754
  44.2 5.9 %shard_map.469.d1_ref = bf16[2880,512]{1,0:T(8,128)(2,1)} custom-call(bf16[2880,512]{1,0:T(8,128)(2,1)} %get-tuple-element.122.pre_ref), custom_call_target="tpu_custom_call" | custom-call | flops 14745600 | bytes 5898240 | tf_op jit(solution)/shard_map/pallas_call | solution.py:774
  50.2 4.0 %shard_map.470 = (bf16[192,512]{1,0:T(8,128)(2,1)}, bf16[192,512]{1,0:T(8,128)(2,1)}, f32[192,512]{1,0:T(8,128)}, f32[192,1]{1,0:T(8,128)}, bf16[192,2048]{1,0:T...) custom-call(bf16[192,512]{1,0:T(8,128)(2,1)S(1)} %add_convert_fusion, ...), custom_call_target="tpu_custom_call" | custom-call | tf_op jit(solution)/shard_map/pallas_call | solution.py:787
  54.2 3.6 %all-to-all-start.2 = ((bf16[8,32,512]{2,1,0:T(8,128)(2,1)}), bf16[8,32,512]{2,1,0:T(8,128)(2,1)S(1)}, u32[]{:S(2)}, u32[]{:S(2)}) async-start(bf16[8,32,512]{2,1,0:T(8,128)(2,1)} %bitcast.9), calls=%async_computation.2 | async-start | bytes 524288 | tf_op jit(solution)/shard_map/all_to_all | solution.py:641
  57.8 5.7 %shard_map.471.d2_ref = bf16[2880,512]{1,0:T(8,128)(2,1)} custom-call(bf16[2880,512]{1,0:T(8,128)(2,1)} %get-tuple-element.129.pre_ref), custom_call_target="tpu_custom_call" | custom-call | flops 14745600 | bytes 5898240 | tf_op jit(solution)/shard_map/pallas_call | solution.py:774
  63.6 2.9 %all-to-all-done.2 = bf16[8,32,512]{2,1,0:T(8,128)(2,1)S(1)} async-done(((bf16[8,32,512]{2,1,0:T(8,128)(2,1)}), bf16[8,32,512]{2,1,0:T(8,128)(2,1)S(1)}, u32[]{:S(2)}, u32[]{:S(2)}) %all-to-all-start.2) | async-done | bytes 262176 | tf_op jit(solution)/shard_map/all_to_all | solution.py:641
  66.5 14.8 %shard_map.472 = (bf16[15,192,192]{2,1,0:T(8,128)(2,1)}, f32[2880,192]{1,0:T(8,128)}, bf16[192,192]{1,0:T(8,128)(2,1)}, bf16[256,192]{1,0:T(8,128)(2,1)}, bf16[1...) custom-call(s32[16,192]{1,0:T(8,128)} %copy-done.19, ...), custom_call_target="tpu_custom_call" | custom-call | flops 12079595520 | bytes 6635520 | tf_op jit(solution)/shard_map/pallas_call | solution.py:808
  81.3 3.6 %all-to-all-start.3 = ((bf16[8,32,192]{2,1,0:T(8,128)(2,1)}), bf16[8,32,192]{2,1,0:T(8,128)(2,1)S(1)}, u32[]{:S(2)}, u32[]{:S(2)}) async-start(bf16[8,32,192]{2,1,0:T(8,128)(2,1)} %bitcast.55), calls=%async_computation.3 | async-start | bytes 262144 | tf_op jit(solution)/shard_map/all_to_all | solution.py:641
  85.0 2.7 %shard_map.473 = bf16[4,208,512]{2,1,0:T(8,128)(2,1)} custom-call(bf16[192,512]{1,0:T(8,128)(2,1)} %get-tuple-element.91.sent_ref, bf16[256,512]{1,0:T(8,128)(2,1)} %bitcast.43, bf16[192,192]{1,0:T(8,128)(2,1)} %get-tuple-element.133.own_ref, bf16[256,192]{1,0:T(8,128)(2,1)} %get-tuple-element.135.far_grad_ref, ...), custom_call_target="tpu_custom_call" | custom-call | flops 1000000000 | bytes 1000000 | tf_op jit(solution)/shard_map/pallas_call | solution.py:855
  87.6 4.6 %all-to-all-done.3 = bf16[8,32,192]{2,1,0:T(8,128)(2,1)S(1)} async-done(((bf16[8,32,192]{2,1,0:T(8,128)(2,1)}), bf16[8,32,192]{2,1,0:T(8,128)(2,1)S(1)}, u32[]{:S(2)}, u32[]{:S(2)}) %all-to-all-start.3) | async-done | bytes 98336 | tf_op jit(solution)/shard_map/all_to_all | solution.py:641
  96.7 3.5 %shard_map.475 = (bf16[192,512]{1,0:T(8,128)(2,1)S(1)}, f32[192,512]{1,0:T(8,128)S(1)}, bf16[192,1216]{1,0:T(8,128)(2,1)S(1)}, bf16[2048,512]{1,0:T(8,128)(2,1)S...) custom-call(bf16[192,512]{1,0:T(8,128)(2,1)} %refs_0_, ...), custom_call_target="tpu_custom_call" | custom-call | bytes 16269312 | tf_op jit(solution)/shard_map/pallas_call | solution.py:364
  101.0 2.6 %shard_map.476 = (f32[192,512]{1,0:T(8,128)S(1)}, f32[192,512]{1,0:T(8,128)S(1)}, f32[16,512]{1,0:T(8,128)S(1)}, bf16[1152,512]{1,0:T(8,128)(2,1)S(1)}) custom-call(s32[1]{0:T(128)} %bitcast.15.place_ref, bf16[192,384]{1,0:T(8,128)(2,1)S(1)} %add_convert_fusion.13.back_a, bf16[192,384]{1,0:T(8,128)(2,1)S(1)} %collective-permute-done.5.back_b, ...), custom_call_target="tpu_custom_call" | custom-call | tf_op jit(solution)/shard_map/pallas_call | solution.py:871
  105.2 12.7 %shard_map.477 = (f32[15,192,192]{2,1,0:T(8,128)}, bf16[192,512]{1,0:T(8,128)(2,1)S(1)}, bf16[256,512]{1,0:T(8,128)(2,1)}, bf16[192,512]{1,0:T(8,128)(2,1)S(1)},...) custom-call(s32[1]{0:T(128)S(6)} %and.66.core_ref, s32[16,192]{1,0:T(8,128)} %copy-done.19, ...), custom_call_target="tpu_custom_call" | custom-call | flops 12079595520 | bytes 14745600 | tf_op jit(solution)/shard_map/pallas_call | solution.py:893
  129.4 6.4 %collective-permute-done.11 = bf16[2,72,512]{2,1,0:T(8,128)(2,1)S(1)} collective-permute-done((bf16[2,72,512]{2,1,0:T(8,128)(2,1)S(1)}, bf16[2,72,512]{2,1,0:T(8,128)(2,1)S(1)}, u32[]{:S(2)}, u32[]{:S(2)}) %collective-permute-start.11) | collective-permute-done | bytes 147488 | tf_op jit(solution)/shard_map/ppermute | solution.py:546
  135.9 2.3 %collective-permute-done.12 = bf16[448,512]{1,0:T(8,128)(2,1)S(1)} collective-permute-done((bf16[448,512]{1,0:T(8,128)(2,1)S(1)}, bf16[448,512]{1,0:T(8,128)(2,1)S(1)}, u32[]{:S(2)}, u32[]{:S(2)}) %collective-permute-start.12) | collective-permute-done | bytes 458784 | tf_op jit(solution)/shard_map/ppermute | solution.py:546
  143.2 4.1 %all-to-all-start.4 = ((bf16[8,32,512]{2,1,0:T(8,128)(2,1)}), bf16[8,32,512]{2,1,0:T(8,128)(2,1)S(1)}, u32[]{:S(2)}, u32[]{:S(2)}) async-start(bf16[8,32,512]{2,1,0:T(8,128)(2,1)} %bitcast.24), calls=%async_computation.4 | async-start | bytes 524288 | tf_op jit(solution)/shard_map/all_to_all | solution.py:641
  152.0 3.0 %collective-permute-done.19 = bf16[176,512]{1,0:T(8,128)(2,1)} collective-permute-done((bf16[176,512]{1,0:T(8,128)(2,1)S(1)}, bf16[176,512]{1,0:T(8,128)(2,1)}, u32[]{:S(2)}, u32[]{:S(2)}) %collective-permute-start.19) | collective-permute-done | bytes 180256 | tf_op jit(solution)/shard_map/ppermute | solution.py:546
  156.5 5.6 %collective-permute-done.16 = bf16[144,512]{1,0:T(8,128)(2,1)S(1)} collective-permute-done((bf16[144,512]{1,0:T(8,128)(2,1)S(1)}, bf16[144,512]{1,0:T(8,128)(2,1)S(1)}, u32[]{:S(2)}, u32[]{:S(2)}) %collective-permute-start.16) | collective-permute-done | bytes 147488 | tf_op jit(solution)/shard_map/ppermute | solution.py:546
  162.9 2.4 %collective-permute-done.20 = bf16[176,512]{1,0:T(8,128)(2,1)S(1)} collective-permute-done((bf16[176,512]{1,0:T(8,128)(2,1)S(1)}, bf16[176,512]{1,0:T(8,128)(2,1)S(1)}, u32[]{:S(2)}, u32[]{:S(2)}) %collective-permute-start.20) | collective-permute-done | bytes 180256 | tf_op jit(solution)/shard_map/ppermute | solution.py:546
  165.4 2.2 %collective-permute-start.27 = (bf16[176,512]{1,0:T(8,128)(2,1)S(1)}, bf16[176,512]{1,0:T(8,128)(2,1)S(1)}, u32[]{:S(2)}, u32[]{:S(2)}) collective-permute-start(bf16[176,512]{1,0:T(8,128)(2,1)S(1)} %add_convert_fusion.8.p0), channel_id=1, source_target_pairs={{0,4},{4,0},{8,12},{12,8},{16,20},{20,16},{24,28},{28,24},{1,5},{5... | collective-permute-start | bytes 540680 | tf_op jit(solution)/shard_map/ppermute | solution.py:546
  174.6 3.2 %collective-permute-done.28.p3 = bf16[176,512]{1,0:T(8,128)(2,1)S(1)} collective-permute-done((bf16[176,512]{1,0:T(8,128)(2,1)S(1)}, bf16[176,512]{1,0:T(8,128)(2,1)S(1)}, u32[]{:S(2)}, u32[]{:S(2)}) %collective-permute-start.28) | collective-permute-done | bytes 180256 | tf_op jit(solution)/shard_map/ppermute | solution.py:546
  (135 shorter events, 47.5 us)
Async XLA Ops:
  41.9 8.2 %collective-permute-start.1 = (bf16[192,512]{1,0:T(8,128)(2,1)S(1)}, bf16[192,512]{1,0:T(8,128)(2,1)S(1)}, u32[]{:S(2)}, u32[]{:S(2)}) collective-permute-start(bf16[192,512]{1,0:T(8,128)(2,1)S(1)} %add_convert_fusion.7.sum_a), channel_id=1, source_target_pairs={{0,2},{1,3},{2,0},{3,1},{4,6},{5,7},{6,4},{7,5},{8,10},{9,11},{10,... | collective-permute-start | bytes 589832 | tf_op jit(solution)/shard_map/ppermute | solution.py:546
  54.2 12.3 %all-to-all-start.2 = ((bf16[8,32,512]{2,1,0:T(8,128)(2,1)}), bf16[8,32,512]{2,1,0:T(8,128)(2,1)S(1)}, u32[]{:S(2)}, u32[]{:S(2)}) async-start(bf16[8,32,512]{2,1,0:T(8,128)(2,1)} %bitcast.9), calls=%async_computation.2 | async-start | bytes 524288 | tf_op jit(solution)/shard_map/all_to_all | solution.py:641
  81.3 10.9 %all-to-all-start.3 = ((bf16[8,32,192]{2,1,0:T(8,128)(2,1)}), bf16[8,32,192]{2,1,0:T(8,128)(2,1)S(1)}, u32[]{:S(2)}, u32[]{:S(2)}) async-start(bf16[8,32,192]{2,1,0:T(8,128)(2,1)} %bitcast.55), calls=%async_computation.3 | async-start | bytes 262144 | tf_op jit(solution)/shard_map/all_to_all | solution.py:641
  103.7 14.2 %collective-permute-start.6 = (bf16[288,512]{1,0:T(8,128)(2,1)S(1)}, bf16[288,512]{1,0:T(8,128)(2,1)S(1)}, u32[]{:S(2)}, u32[]{:S(2)}) collective-permute-start(bf16[288,512]{1,0:T(8,128)(2,1)S(1)} %get-tuple-element.209), channel_id=1, source_target_pairs={{0,4},{4,0},{8,12},{12,8},{16,20},{20,16},{24,28},{28,24},{1,5},{5... | collective-permute-start | bytes 884744 | tf_op jit(solution)/shard_map/ppermute | solution.py:546
  104.0 13.9 %collective-permute-start.7 = (bf16[288,512]{1,0:T(8,128)(2,1)S(1)}, bf16[288,512]{1,0:T(8,128)(2,1)S(1)}, u32[]{:S(2)}, u32[]{:S(2)}) collective-permute-start(bf16[288,512]{1,0:T(8,128)(2,1)S(1)} %get-tuple-element.208), channel_id=1, source_target_pairs={{0,8},{4,12},{8,0},{12,4},{16,24},{20,28},{24,16},{28,20},{1,9},{5... | collective-permute-start | bytes 884744 | tf_op jit(solution)/shard_map/ppermute | solution.py:546
  105.1 16.4 %collective-permute-start.13 = (bf16[416,512]{1,0:T(8,128)(2,1)S(1)}, bf16[416,512]{1,0:T(8,128)(2,1)S(1)}, u32[]{:S(2)}, u32[]{:S(2)}) collective-permute-start(bf16[416,512]{1,0:T(8,128)(2,1)S(1)} %constant_dynamic-slice_fusion.4), channel_id=1, source_target_pairs={{0,1},{1,0},{2,3},{3,2},{4,5},{5,4},{6,7},{7,6},{8,9},{9,8},{10,11... | collective-permute-start | bytes 1277960 | tf_op jit(solution)/shard_map/ppermute | solution.py:546
  117.9 7.5 %collective-permute-start.10 = (bf16[2,448,512]{2,1,0:T(8,128)(2,1)S(1)}, bf16[2,448,512]{2,1,0:T(8,128)(2,1)S(1)}, u32[]{:S(2)}, u32[]{:S(2)}) collective-permute-start(bf16[2,448,512]{2,1,0:T(8,128)(2,1)S(1)} %get-tuple-element.173), channel_id=1, source_target_pairs={{0,1},{1,0},{2,3},{3,2},{4,5},{5,4},{6,7},{7,6},{8,9},{9,8},{10,11... | collective-permute-start | bytes 2752520 | tf_op jit(solution)/shard_map/ppermute | solution.py:546
  121.7 7.7 %collective-permute-start.14 = (bf16[208,512]{1,0:T(8,128)(2,1)S(1)}, bf16[208,512]{1,0:T(8,128)(2,1)S(1)}, u32[]{:S(2)}, u32[]{:S(2)}) collective-permute-start(bf16[208,512]{1,0:T(8,128)(2,1)S(1)} %constant_dynamic-slice_fusion.3), channel_id=1, source_target_pairs={{0,2},{1,3},{2,0},{3,1},{4,6},{5,7},{6,4},{7,5},{8,10},{9,11},{10,... | collective-permute-start | bytes 638984 | tf_op jit(solution)/shard_map/ppermute | solution.py:546
  125.7 12.5 %collective-permute-start.12 = (bf16[448,512]{1,0:T(8,128)(2,1)S(1)}, bf16[448,512]{1,0:T(8,128)(2,1)S(1)}, u32[]{:S(2)}, u32[]{:S(2)}) collective-permute-start(bf16[448,512]{1,0:T(8,128)(2,1)S(1)} %constant_dynamic-slice_fusion.5), channel_id=1, source_target_pairs={{0,2},{1,3},{2,0},{3,1},{4,6},{5,7},{6,4},{7,5},{8,10},{9,11},{10,... | collective-permute-start | bytes 1376264 | tf_op jit(solution)/shard_map/ppermute | solution.py:546
  127.3 8.6 %collective-permute-start.11 = (bf16[2,72,512]{2,1,0:T(8,128)(2,1)S(1)}, bf16[2,72,512]{2,1,0:T(8,128)(2,1)S(1)}, u32[]{:S(2)}, u32[]{:S(2)}) collective-permute-start(bf16[2,72,512]{2,1,0:T(8,128)(2,1)S(1)} %constant_dynamic-slice_fusion.6), channel_id=1, source_target_pairs={{0,16},{4,20},{8,24},{12,28},{16,0},{20,4},{24,8},{28,12},{1,17},{... | collective-permute-start | bytes 442376 | tf_op jit(solution)/shard_map/ppermute | solution.py:546
  138.6 8.8 %collective-permute-start.15 = (bf16[2,72,512]{2,1,0:T(8,128)(2,1)S(1)}, bf16[2,72,512]{2,1,0:T(8,128)(2,1)}, u32[]{:S(2)}, u32[]{:S(2)}) collective-permute-start(bf16[2,72,512]{2,1,0:T(8,128)(2,1)S(1)} %add_convert_fusion.10), channel_id=1, source_target_pairs={{0,16},{4,20},{8,24},{12,28},{16,0},{20,4},{24,8},{28,12},{1,17},{... | collective-permute-start | bytes 442376 | tf_op jit(solution)/shard_map/ppermute | solution.py:546
  139.7 12.3 %collective-permute-start.17 = (bf16[176,512]{1,0:T(8,128)(2,1)}, bf16[176,512]{1,0:T(8,128)(2,1)}, u32[]{:S(2)}, u32[]{:S(2)}) collective-permute-start(bf16[176,512]{1,0:T(8,128)(2,1)} %get-tuple-element.210), channel_id=1, source_target_pairs={{0,8},{4,12},{8,0},{12,4},{16,24},{20,28},{24,16},{28,20},{1,9},{5... | collective-permute-start | bytes 540680 | tf_op jit(solution)/shard_map/ppermute | solution.py:546
  140.5 11.5 %collective-permute-start.18 = (bf16[176,512]{1,0:T(8,128)(2,1)S(1)}, bf16[176,512]{1,0:T(8,128)(2,1)}, u32[]{:S(2)}, u32[]{:S(2)}) collective-permute-start(bf16[176,512]{1,0:T(8,128)(2,1)S(1)} %get-tuple-element.212), channel_id=1, source_target_pairs={{0,4},{4,0},{8,12},{12,8},{16,20},{20,16},{24,28},{28,24},{1,5},{5... | collective-permute-start | bytes 540680 | tf_op jit(solution)/shard_map/ppermute | solution.py:546
  141.5 13.5 %collective-permute-start.19 = (bf16[176,512]{1,0:T(8,128)(2,1)S(1)}, bf16[176,512]{1,0:T(8,128)(2,1)}, u32[]{:S(2)}, u32[]{:S(2)}) collective-permute-start(bf16[176,512]{1,0:T(8,128)(2,1)S(1)} %get-tuple-element.211), channel_id=1, source_target_pairs={{0,12},{4,8},{8,4},{12,0},{16,28},{20,24},{24,20},{28,16},{1,13},{... | collective-permute-start | bytes 540680 | tf_op jit(solution)/shard_map/ppermute | solution.py:546
  143.2 18.9 %all-to-all-start.4 = ((bf16[8,32,512]{2,1,0:T(8,128)(2,1)}), bf16[8,32,512]{2,1,0:T(8,128)(2,1)S(1)}, u32[]{:S(2)}, u32[]{:S(2)}) async-start(bf16[8,32,512]{2,1,0:T(8,128)(2,1)} %bitcast.24), calls=%async_computation.4 | async-start | bytes 524288 | tf_op jit(solution)/shard_map/all_to_all | solution.py:641
  148.5 7.9 %collective-permute-start.22 = (bf16[144,512]{1,0:T(8,128)(2,1)S(1)}, bf16[144,512]{1,0:T(8,128)(2,1)S(1)}, u32[]{:S(2)}, u32[]{:S(2)}) collective-permute-start(bf16[144,512]{1,0:T(8,128)(2,1)S(1)} %get-tuple-element.213), channel_id=1, source_target_pairs={{0,4},{4,0},{8,12},{12,8},{16,20},{20,16},{24,28},{28,24},{1,5},{5... | collective-permute-start | bytes 442376 | tf_op jit(solution)/shard_map/ppermute | solution.py:546
  150.5 11.5 %collective-permute-start.16 = (bf16[144,512]{1,0:T(8,128)(2,1)S(1)}, bf16[144,512]{1,0:T(8,128)(2,1)S(1)}, u32[]{:S(2)}, u32[]{:S(2)}) collective-permute-start(bf16[144,512]{1,0:T(8,128)(2,1)S(1)} %get-tuple-element.214), channel_id=1, source_target_pairs={{0,8},{4,12},{8,0},{12,4},{16,24},{20,28},{24,16},{28,20},{1,9},{5... | collective-permute-start | bytes 442376 | tf_op jit(solution)/shard_map/ppermute | solution.py:546
  156.3 9.0 %collective-permute-start.20 = (bf16[176,512]{1,0:T(8,128)(2,1)S(1)}, bf16[176,512]{1,0:T(8,128)(2,1)S(1)}, u32[]{:S(2)}, u32[]{:S(2)}) collective-permute-start(bf16[176,512]{1,0:T(8,128)(2,1)S(1)} %add_convert_fusion.9), channel_id=1, source_target_pairs={{0,16},{4,20},{8,24},{12,28},{16,0},{20,4},{24,8},{28,12},{1,17},{... | collective-permute-start | bytes 540680 | tf_op jit(solution)/shard_map/ppermute | solution.py:546
  165.3 7.6 %collective-permute-start.26 = (bf16[176,512]{1,0:T(8,128)(2,1)S(1)}, bf16[176,512]{1,0:T(8,128)(2,1)S(1)}, u32[]{:S(2)}, u32[]{:S(2)}) collective-permute-start(bf16[176,512]{1,0:T(8,128)(2,1)S(1)} %add_convert_fusion.8.p0), channel_id=1, source_target_pairs={{0,8},{4,12},{8,0},{12,4},{16,24},{20,28},{24,16},{28,20},{1,9},{5... | collective-permute-start | bytes 540680 | tf_op jit(solution)/shard_map/ppermute | solution.py:546
  165.4 9.2 %collective-permute-start.27 = (bf16[176,512]{1,0:T(8,128)(2,1)S(1)}, bf16[176,512]{1,0:T(8,128)(2,1)S(1)}, u32[]{:S(2)}, u32[]{:S(2)}) collective-permute-start(bf16[176,512]{1,0:T(8,128)(2,1)S(1)} %add_convert_fusion.8.p0), channel_id=1, source_target_pairs={{0,4},{4,0},{8,12},{12,8},{16,20},{20,16},{24,28},{28,24},{1,5},{5... | collective-permute-start | bytes 540680 | tf_op jit(solution)/shard_map/ppermute | solution.py:546
  167.7 10.2 %collective-permute-start.28 = (bf16[176,512]{1,0:T(8,128)(2,1)S(1)}, bf16[176,512]{1,0:T(8,128)(2,1)S(1)}, u32[]{:S(2)}, u32[]{:S(2)}) collective-permute-start(bf16[176,512]{1,0:T(8,128)(2,1)S(1)} %add_convert_fusion.8.p0), channel_id=1, source_target_pairs={{0,12},{4,8},{8,4},{12,0},{16,28},{20,24},{24,20},{28,16},{1,13},{... | collective-permute-start | bytes 540680 | tf_op jit(solution)/shard_map/ppermute | solution.py:546
  169.0 11.2 %collective-permute-start.23 = (bf16[288,512]{1,0:T(8,128)(2,1)S(1)}, bf16[288,512]{1,0:T(8,128)(2,1)S(1)}, u32[]{:S(2)}, u32[]{:S(2)}) collective-permute-start(bf16[288,512]{1,0:T(8,128)(2,1)S(1)} %maximum_select_fusion.2.b0), channel_id=1, source_target_pairs={{0,8},{4,12},{8,0},{12,4},{16,24},{20,28},{24,16},{28,20},{1,9},{5... | collective-permute-start | bytes 884744 | tf_op jit(solution)/shard_map/ppermute | solution.py:546
  169.6 11.2 %collective-permute-start.21 = (bf16[288,512]{1,0:T(8,128)(2,1)S(1)}, bf16[288,512]{1,0:T(8,128)(2,1)S(1)}, u32[]{:S(2)}, u32[]{:S(2)}) collective-permute-start(bf16[288,512]{1,0:T(8,128)(2,1)S(1)} %maximum_select_fusion.1.a0), channel_id=1, source_target_pairs={{0,4},{4,0},{8,12},{12,8},{16,20},{20,16},{24,28},{28,24},{1,5},{5... | collective-permute-start | bytes 884744 | tf_op jit(solution)/shard_map/ppermute | solution.py:546
  172.9 7.9 %collective-permute-start.25 = (bf16[192,512]{1,0:T(8,128)(2,1)S(1)}, bf16[192,512]{1,0:T(8,128)(2,1)S(1)}, u32[]{:S(2)}, u32[]{:S(2)}) collective-permute-start(bf16[192,512]{1,0:T(8,128)(2,1)S(1)} %add_convert_fusion.6.back_a), channel_id=1, source_target_pairs={{0,2},{1,3},{2,0},{3,1},{4,6},{5,7},{6,4},{7,5},{8,10},{9,11},{10,... | collective-permute-start | bytes 589832 | tf_op jit(solution)/shard_map/ppermute | solution.py:546
  (30 other events, 203.1 us)

commit v5 on v4

--- a/solution.py
+++ b/solution.py
@@ -183,16 +183,21 @@
         own[...] = mm(nodes_ref[...], w1_ref[:D, :]) + row_of(b1_ref)
         acc[...] = jnp.zeros_like(acc)
 
-    edge = edges_ref[...].reshape(kt * rows, E)
+    each = range(kt)
+    places = [pl.ds(j * rows, rows) for j in each]
     columns = columns_of(col_ref, step * kt, kt)
-    hot = jnp.concatenate([one_hot(column, width) for column in columns], axis=0)
-    pre1 = spread(own[...], mm(hot, table[...]) + mm(edge, w1_ref[2 * D :, :]))
-    pre1_ref[...] = pre1.astype(bf16)
-    act1 = gelu(pre1).astype(bf16)
-    act1_ref[...] = act1
-    pre2 = jnp.where(kept_weight(columns) > 0.0, mm(act1, w2_ref[...]) + row_of(b2_ref), -30.0)
-    pre2_ref[...] = pre2.astype(bf16)
-    acc[...] += gathered(gelu(pre2), rows)
+    pre1 = [mm(one_hot(columns[j], width), table[...]) + mm(edges_ref[j], w1_ref[2 * D :, :]) for j in each]
+    act1 = []
+    for j in each:
+        total = pre1[j] + own[...]
+        pre1_ref[places[j], :] = total.astype(bf16)
+        act1.append(gelu(total).astype(bf16))
+        act1_ref[places[j], :] = act1[j]
+    pre2 = [mm(act1[j], w2_ref[...]) for j in each]
+    for j in each:
+        total = jnp.where(columns[j] >= 0, pre2[j] + row_of(b2_ref), -30.0)
+        pre2_ref[places[j], :] = total.astype(bf16)
+        acc[...] += gelu(total)
 
     @pl.when(step == last)
     def _():
@@ -751,14 +756,15 @@
     edge_tile = tiled(kt, rows, E)
     flat = tiled(kt * rows, D)
     flat_edge = tiled(kt * rows, E)
+    kf = 3 if kn % 3 == 0 else 1
     act1, pre1, pre2, act_sum = call(
         message_forward_kernel,
         (stored((total, D), bf16), stored((total, D), bf16), stored((total, D), bf16), shape((rows, D), bf16)),
         scratch=[pltpu.VMEM((width, D), bf16), pltpu.VMEM((rows, D), f32), pltpu.VMEM((rows, D), f32)],
-        grid=grid,
+        grid=(kn // kf,),
         in_specs=[
             fixed(rows, SLOT),
-            edge_tile,
+            tiled(kf, rows, E),
             fixed(rows, D),
             fixed(n_far, D),
             fixed(2 * D + E, D),
@@ -766,7 +772,7 @@
             fixed(D),
             fixed(D),
         ],
-        out_specs=(flat, flat, flat, fixed(rows, D)),
+        out_specs=(tiled(kf * rows, D),) * 3 + (fixed(rows, D),),
         cost=pl.CostEstimate(flops=16 * total * D * D, bytes_accessed=total * D * 8, transcendentals=2 * total * D),
     )(*read(place_col, edges, nodes), far_nodes, *read(msg_w1, msg_w2, msg_b1, msg_b2))
 
@@ -862,8 +868,10 @@
     for bit in nbr_bits[:-1]:
         back = add_low(back, swap(back, "nbr", bit))
     kept = fetched(
-        after(node_cot, back), normed2, edge_w1, ffn_w2, hidden_slope, ffn_w1, normed1, msg_w3, first_low, hidden, total_act
-    )
+        after(node_cot, back), normed2, edge_w1, ffn_w2, hidden_slope, ffn_w1, normed1, msg_w3, first_low, hidden, total_act,
+        msg_w1, msg_w2, nodes, far_nodes
+    )
+    *kept, ready_w1, ready_w2, ready_nodes, ready_far = kept
     back_a, back_b = back, swap(back, "nbr", nbr_bits[-1])
 
     wide, narrow = FF // parts, D // parts
@@ -927,7 +935,7 @@
         out_specs=(edge_tile, fixed(rows, D), fixed(n_far, D), fixed(rows, D))
         + (fixed(parts // 2, msg_rows, D),) * 2,
         cost=pl.CostEstimate(flops=16 * total * D * D, bytes_accessed=total * D * 10, transcendentals=0),
-    )(nbr_place & 1, *read(place_row, edges, act1, d1, d2), up, *read(base, nodes), far_nodes, *read(msg_w1, msg_w2), node_bias)
+    )(nbr_place & 1, *read(place_row, edges, act1, d1, d2), up, *read(base), ready_nodes, ready_far, ready_w1, ready_w2, node_bias)
 
     far_sum, msg_kept, msg_given, part_a, part_b = held_together(far_sum, msg_kept, msg_given, part_a, part_b)
     flat_rows = parts // 2 * msg_rows

time: 184 us -> 182 us (0.989)
  no operation moved by 1% of the time
where the time goes in v5:
time: 182 us
  Pallas kernels  70.9 us (39%)
  waiting for transfers between devices  39.7 us (22%)
  starting transfers between devices  38.9 us (21%)
  blocking collectives  24.6 us (14%)
  other arithmetic  4.06 us (2%)
    ppermute x29, waiting for transfers between devices, swap(): lax.ppermute(values, axis, [(i, i ^ bit) for i in range(lax.axis_size(axi...  32.1 us
    ppermute x29, starting transfers between devices, swap(): lax.ppermute(values, axis, [(i, i ^ bit) for i in range(lax.axis_size(axi...  27.6 us
    all_to_all x2, blocking collectives, exchange(): return lax.all_to_all(shaped, 'res', 0, 0, tiled=True).reshape(values.shape)  24.6 us
    pallas_call x1, Pallas kernels, on_device(): call(edge_kernel, (shape((kn, rows, E), bf16), stored((total, E), f32), s...  14.8 us
    pallas_call x1, Pallas kernels, on_device(): call(functools.partial(message_backward_kernel, parts), (shape((kn, rows,...  12 us
    pallas_call x2, Pallas kernels, slope_of(): call(slope_kernel, stored((total, D), bf16), grid=grid, in_specs=[flat],...  11.6 us
    all_to_all x3, starting transfers between devices, exchange(): return lax.all_to_all(shaped, 'res', 0, 0, tiled=True).reshape(values.shape)  11.3 us
    pallas_call x1, Pallas kernels, on_device(): call(message_forward_kernel, (stored((total, D), bf16), stored((total, D)...  10.2 us
  transfers between devices with their start and end apart: 32, of which 18 were waited for; matrix products, arithmetic and copies ran while one was open for 2% of the time, Pallas kernels for 18%

profile of v5, /device:TPU:0, one launch (start us, length us, event | category | flops | bytes accessed | tf_op | source)
XLA Modules:
  0.0 181.6 jit_solution(14560629880297896609)
XLA Ops:
  0.7 2.8 %shard_map.467 = (s32[16,192]{1,0:T(8,128)S(1)}, f32[192,16]{1,0:T(8,128)S(1)}, bf16[256,128]{1,0:T(8,128)(2,1)S(1)}, bf16[192,128]{1,0:T(8,128)(2,1)S(1)}) custom-call(s32[1]{0:T(128)} %bitcast.me_ref, s32[15,192]{1,0:T(8,128)} %bitcast.56, s32[1,192]{1,0:T(1,128)} %bitcast.45), custom_call_target="tpu_custom_call" | custom-call | tf_op jit(solution)/shard_map/pallas_call | solution.py:738
  3.5 14.0 %all_to_all.25 = bf16[8,32,128]{2,1,0:T(8,128)(2,1)S(1)} all-to-all(bf16[8,32,128]{2,1,0:T(8,128)(2,1)S(1)} %bitcast.44), channel_id=1, replica_groups=mesh['res'=8,'nbr'=4] {'res'}, dimensions={0} | all-to-all | bytes 131072 | tf_op jit(solution)/shard_map/all_to_all | solution.py:646
  18.8 10.6 %all_to_all.26 = bf16[8,32,512]{2,1,0:T(8,128)(2,1)S(1)} all-to-all(bf16[8,32,512]{2,1,0:T(8,128)(2,1)S(1)} %bitcast.50), channel_id=1, replica_groups=mesh['res'=8,'nbr'=4] {'res'}, dimensions={0} | all-to-all | bytes 524288 | tf_op jit(solution)/shard_map/all_to_all | solution.py:646
  29.4 10.2 %shard_map.468 = (bf16[2880,512]{1,0:T(8,128)(2,1)}, bf16[2880,512]{1,0:T(8,128)(2,1)}, bf16[2880,512]{1,0:T(8,128)(2,1)}, bf16[192,512]{1,0:T(8,128)(2,1)S(1)}) custom-call(f32[192,16]{1,0:T(8,128)} %copy-done.17, bf16[15,192,192]{2,1,0:T(8,128)(2,1)} %bitcast.58, bf16[192,512]{1,0:T(8,128)(2,1)} %refs_13_.1, bf16[256,512]{1,0:T(8,128)(2,1)S(1)} %bitcast.38, ...), custom_call_target="tpu_custom_call" | custom-call | flops 12079595520 | bytes 11796480 | tf_op jit(solution)/shard_map/pallas_call | solution.py:760
  43.5 5.9 %shard_map.469.d1_ref = bf16[2880,512]{1,0:T(8,128)(2,1)} custom-call(bf16[2880,512]{1,0:T(8,128)(2,1)} %get-tuple-element.126.pre_ref), custom_call_target="tpu_custom_call" | custom-call | flops 14745600 | bytes 5898240 | tf_op jit(solution)/shard_map/pallas_call | solution.py:780
  49.5 4.0 %shard_map.470 = (bf16[192,512]{1,0:T(8,128)(2,1)}, bf16[192,512]{1,0:T(8,128)(2,1)}, f32[192,512]{1,0:T(8,128)}, f32[192,1]{1,0:T(8,128)}, bf16[192,2048]{1,0:T...) custom-call(bf16[192,512]{1,0:T(8,128)(2,1)S(1)} %add_convert_fusion, ...), custom_call_target="tpu_custom_call" | custom-call | tf_op jit(solution)/shard_map/pallas_call | solution.py:793
  53.5 3.6 %all-to-all-start.2 = ((bf16[8,32,512]{2,1,0:T(8,128)(2,1)}), bf16[8,32,512]{2,1,0:T(8,128)(2,1)S(1)}, u32[]{:S(2)}, u32[]{:S(2)}) async-start(bf16[8,32,512]{2,1,0:T(8,128)(2,1)} %bitcast.9), calls=%async_computation.2 | async-start | bytes 524288 | tf_op jit(solution)/shard_map/all_to_all | solution.py:646
  57.1 5.8 %shard_map.471.d2_ref = bf16[2880,512]{1,0:T(8,128)(2,1)} custom-call(bf16[2880,512]{1,0:T(8,128)(2,1)} %get-tuple-element.133.pre_ref), custom_call_target="tpu_custom_call" | custom-call | flops 14745600 | bytes 5898240 | tf_op jit(solution)/shard_map/pallas_call | solution.py:780
  62.9 2.9 %all-to-all-done.2 = bf16[8,32,512]{2,1,0:T(8,128)(2,1)S(1)} async-done(((bf16[8,32,512]{2,1,0:T(8,128)(2,1)}), bf16[8,32,512]{2,1,0:T(8,128)(2,1)S(1)}, u32[]{:S(2)}, u32[]{:S(2)}) %all-to-all-start.2) | async-done | bytes 262176 | tf_op jit(solution)/shard_map/all_to_all | solution.py:646
  65.8 14.8 %shard_map.472 = (bf16[15,192,192]{2,1,0:T(8,128)(2,1)}, f32[2880,192]{1,0:T(8,128)}, bf16[192,192]{1,0:T(8,128)(2,1)}, bf16[256,192]{1,0:T(8,128)(2,1)}, bf16[1...) custom-call(s32[16,192]{1,0:T(8,128)} %copy-done.18, ...), custom_call_target="tpu_custom_call" | custom-call | flops 12079595520 | bytes 6635520 | tf_op jit(solution)/shard_map/pallas_call | solution.py:814
  80.6 3.6 %all-to-all-start.3 = ((bf16[8,32,192]{2,1,0:T(8,128)(2,1)}), bf16[8,32,192]{2,1,0:T(8,128)(2,1)S(1)}, u32[]{:S(2)}, u32[]{:S(2)}) async-start(bf16[8,32,192]{2,1,0:T(8,128)(2,1)} %bitcast.55), calls=%async_computation.3 | async-start | bytes 262144 | tf_op jit(solution)/shard_map/all_to_all | solution.py:646
  84.2 2.7 %shard_map.473 = bf16[4,208,512]{2,1,0:T(8,128)(2,1)} custom-call(bf16[192,512]{1,0:T(8,128)(2,1)} %get-tuple-element.95.sent_ref, bf16[256,512]{1,0:T(8,128)(2,1)} %bitcast.43, bf16[192,192]{1,0:T(8,128)(2,1)} %get-tuple-element.137.own_ref, bf16[256,192]{1,0:T(8,128)(2,1)} %get-tuple-element.139.far_grad_ref, ...), custom_call_target="tpu_custom_call" | custom-call | flops 1000000000 | bytes 1000000 | tf_op jit(solution)/shard_map/pallas_call | solution.py:861
  86.9 4.6 %all-to-all-done.3 = bf16[8,32,192]{2,1,0:T(8,128)(2,1)S(1)} async-done(((bf16[8,32,192]{2,1,0:T(8,128)(2,1)}), bf16[8,32,192]{2,1,0:T(8,128)(2,1)S(1)}, u32[]{:S(2)}, u32[]{:S(2)}) %all-to-all-start.3) | async-done | bytes 98336 | tf_op jit(solution)/shard_map/all_to_all | solution.py:646
  96.0 4.2 %shard_map.475 = (bf16[192,512]{1,0:T(8,128)(2,1)S(1)}, f32[192,512]{1,0:T(8,128)S(1)}, bf16[192,1216]{1,0:T(8,128)(2,1)S(1)}, bf16[2048,512]{1,0:T(8,128)(2,1)S...) custom-call(bf16[192,512]{1,0:T(8,128)(2,1)} %refs_0_, ...), custom_call_target="tpu_custom_call" | custom-call | bytes 20725760 | tf_op jit(solution)/shard_map/pallas_call | solution.py:369
  100.3 2.6 %shard_map.476 = (f32[192,512]{1,0:T(8,128)S(1)}, f32[192,512]{1,0:T(8,128)S(1)}, f32[16,512]{1,0:T(8,128)S(1)}, bf16[1152,512]{1,0:T(8,128)(2,1)S(1)}) custom-call(s32[1]{0:T(128)} %bitcast.15.place_ref, bf16[192,384]{1,0:T(8,128)(2,1)S(1)} %add_convert_fusion.13.back_a, bf16[192,384]{1,0:T(8,128)(2,1)S(1)} %collective-permute-done.5.back_b, ...), custom_call_target="tpu_custom_call" | custom-call | tf_op jit(solution)/shard_map/pallas_call | solution.py:879
  104.4 12.0 %shard_map.477 = (f32[15,192,192]{2,1,0:T(8,128)}, bf16[192,512]{1,0:T(8,128)(2,1)S(1)}, bf16[256,512]{1,0:T(8,128)(2,1)}, bf16[192,512]{1,0:T(8,128)(2,1)S(1)},...) custom-call(s32[1]{0:T(128)S(6)} %and.66.core_ref, s32[16,192]{1,0:T(8,128)} %copy-done.18, ...), custom_call_target="tpu_custom_call" | custom-call | flops 12079595520 | bytes 14745600 | tf_op jit(solution)/shard_map/pallas_call | solution.py:901
  128.0 6.4 %collective-permute-done.11 = bf16[2,72,512]{2,1,0:T(8,128)(2,1)S(1)} collective-permute-done((bf16[2,72,512]{2,1,0:T(8,128)(2,1)S(1)}, bf16[2,72,512]{2,1,0:T(8,128)(2,1)S(1)}, u32[]{:S(2)}, u32[]{:S(2)}) %collective-permute-start.11) | collective-permute-done | bytes 147488 | tf_op jit(solution)/shard_map/ppermute | solution.py:551
  134.5 2.3 %collective-permute-done.12 = bf16[448,512]{1,0:T(8,128)(2,1)S(1)} collective-permute-done((bf16[448,512]{1,0:T(8,128)(2,1)S(1)}, bf16[448,512]{1,0:T(8,128)(2,1)S(1)}, u32[]{:S(2)}, u32[]{:S(2)}) %collective-permute-start.12) | collective-permute-done | bytes 458784 | tf_op jit(solution)/shard_map/ppermute | solution.py:551
  141.8 4.1 %all-to-all-start.4 = ((bf16[8,32,512]{2,1,0:T(8,128)(2,1)}), bf16[8,32,512]{2,1,0:T(8,128)(2,1)S(1)}, u32[]{:S(2)}, u32[]{:S(2)}) async-start(bf16[8,32,512]{2,1,0:T(8,128)(2,1)} %bitcast.24), calls=%async_computation.4 | async-start | bytes 524288 | tf_op jit(solution)/shard_map/all_to_all | solution.py:646
  150.6 3.0 %collective-permute-done.19 = bf16[176,512]{1,0:T(8,128)(2,1)} collective-permute-done((bf16[176,512]{1,0:T(8,128)(2,1)S(1)}, bf16[176,512]{1,0:T(8,128)(2,1)}, u32[]{:S(2)}, u32[]{:S(2)}) %collective-permute-start.19) | collective-permute-done | bytes 180256 | tf_op jit(solution)/shard_map/ppermute | solution.py:551
  155.0 5.6 %collective-permute-done.16 = bf16[144,512]{1,0:T(8,128)(2,1)S(1)} collective-permute-done((bf16[144,512]{1,0:T(8,128)(2,1)S(1)}, bf16[144,512]{1,0:T(8,128)(2,1)S(1)}, u32[]{:S(2)}, u32[]{:S(2)}) %collective-permute-start.16) | collective-permute-done | bytes 147488 | tf_op jit(solution)/shard_map/ppermute | solution.py:551
  161.4 2.4 %collective-permute-done.20 = bf16[176,512]{1,0:T(8,128)(2,1)S(1)} collective-permute-done((bf16[176,512]{1,0:T(8,128)(2,1)S(1)}, bf16[176,512]{1,0:T(8,128)(2,1)S(1)}, u32[]{:S(2)}, u32[]{:S(2)}) %collective-permute-start.20) | collective-permute-done | bytes 180256 | tf_op jit(solution)/shard_map/ppermute | solution.py:551
  164.0 2.2 %collective-permute-start.27 = (bf16[176,512]{1,0:T(8,128)(2,1)S(1)}, bf16[176,512]{1,0:T(8,128)(2,1)S(1)}, u32[]{:S(2)}, u32[]{:S(2)}) collective-permute-start(bf16[176,512]{1,0:T(8,128)(2,1)S(1)} %add_convert_fusion.8.p0), channel_id=1, source_target_pairs={{0,4},{4,0},{8,12},{12,8},{16,20},{20,16},{24,28},{28,24},{1,5},{5... | collective-permute-start | bytes 540680 | tf_op jit(solution)/shard_map/ppermute | solution.py:551
  173.2 3.2 %collective-permute-done.28.p3 = bf16[176,512]{1,0:T(8,128)(2,1)S(1)} collective-permute-done((bf16[176,512]{1,0:T(8,128)(2,1)S(1)}, bf16[176,512]{1,0:T(8,128)(2,1)S(1)}, u32[]{:S(2)}, u32[]{:S(2)}) %collective-permute-start.28) | collective-permute-done | bytes 180256 | tf_op jit(solution)/shard_map/ppermute | solution.py:551
  (133 shorter events, 46.9 us)
Async XLA Ops:
  41.2 8.2 %collective-permute-start.1 = (bf16[192,512]{1,0:T(8,128)(2,1)S(1)}, bf16[192,512]{1,0:T(8,128)(2,1)S(1)}, u32[]{:S(2)}, u32[]{:S(2)}) collective-permute-start(bf16[192,512]{1,0:T(8,128)(2,1)S(1)} %add_convert_fusion.7.sum_a), channel_id=1, source_target_pairs={{0,2},{1,3},{2,0},{3,1},{4,6},{5,7},{6,4},{7,5},{8,10},{9,11},{10,... | collective-permute-start | bytes 589832 | tf_op jit(solution)/shard_map/ppermute | solution.py:551
  53.5 12.3 %all-to-all-start.2 = ((bf16[8,32,512]{2,1,0:T(8,128)(2,1)}), bf16[8,32,512]{2,1,0:T(8,128)(2,1)S(1)}, u32[]{:S(2)}, u32[]{:S(2)}) async-start(bf16[8,32,512]{2,1,0:T(8,128)(2,1)} %bitcast.9), calls=%async_computation.2 | async-start | bytes 524288 | tf_op jit(solution)/shard_map/all_to_all | solution.py:646
  80.6 10.9 %all-to-all-start.3 = ((bf16[8,32,192]{2,1,0:T(8,128)(2,1)}), bf16[8,32,192]{2,1,0:T(8,128)(2,1)S(1)}, u32[]{:S(2)}, u32[]{:S(2)}) async-start(bf16[8,32,192]{2,1,0:T(8,128)(2,1)} %bitcast.55), calls=%async_computation.3 | async-start | bytes 262144 | tf_op jit(solution)/shard_map/all_to_all | solution.py:646
  102.9 13.5 %collective-permute-start.6 = (bf16[288,512]{1,0:T(8,128)(2,1)S(1)}, bf16[288,512]{1,0:T(8,128)(2,1)S(1)}, u32[]{:S(2)}, u32[]{:S(2)}) collective-permute-start(bf16[288,512]{1,0:T(8,128)(2,1)S(1)} %get-tuple-element.217), channel_id=1, source_target_pairs={{0,4},{4,0},{8,12},{12,8},{16,20},{20,16},{24,28},{28,24},{1,5},{5... | collective-permute-start | bytes 884744 | tf_op jit(solution)/shard_map/ppermute | solution.py:551
  103.2 13.2 %collective-permute-start.7 = (bf16[288,512]{1,0:T(8,128)(2,1)S(1)}, bf16[288,512]{1,0:T(8,128)(2,1)S(1)}, u32[]{:S(2)}, u32[]{:S(2)}) collective-permute-start(bf16[288,512]{1,0:T(8,128)(2,1)S(1)} %get-tuple-element.216), channel_id=1, source_target_pairs={{0,8},{4,12},{8,0},{12,4},{16,24},{20,28},{24,16},{28,20},{1,9},{5... | collective-permute-start | bytes 884744 | tf_op jit(solution)/shard_map/ppermute | solution.py:551
  104.4 15.8 %collective-permute-start.13 = (bf16[416,512]{1,0:T(8,128)(2,1)S(1)}, bf16[416,512]{1,0:T(8,128)(2,1)S(1)}, u32[]{:S(2)}, u32[]{:S(2)}) collective-permute-start(bf16[416,512]{1,0:T(8,128)(2,1)S(1)} %constant_dynamic-slice_fusion.4), channel_id=1, source_target_pairs={{0,1},{1,0},{2,3},{3,2},{4,5},{5,4},{6,7},{7,6},{8,9},{9,8},{10,11... | collective-permute-start | bytes 1277960 | tf_op jit(solution)/shard_map/ppermute | solution.py:551
  116.4 7.5 %collective-permute-start.10 = (bf16[2,448,512]{2,1,0:T(8,128)(2,1)S(1)}, bf16[2,448,512]{2,1,0:T(8,128)(2,1)S(1)}, u32[]{:S(2)}, u32[]{:S(2)}) collective-permute-start(bf16[2,448,512]{2,1,0:T(8,128)(2,1)S(1)} %get-tuple-element.181), channel_id=1, source_target_pairs={{0,1},{1,0},{2,3},{3,2},{4,5},{5,4},{6,7},{7,6},{8,9},{9,8},{10,11... | collective-permute-start | bytes 2752520 | tf_op jit(solution)/shard_map/ppermute | solution.py:551
  120.3 7.7 %collective-permute-start.14 = (bf16[208,512]{1,0:T(8,128)(2,1)S(1)}, bf16[208,512]{1,0:T(8,128)(2,1)S(1)}, u32[]{:S(2)}, u32[]{:S(2)}) collective-permute-start(bf16[208,512]{1,0:T(8,128)(2,1)S(1)} %constant_dynamic-slice_fusion.3), channel_id=1, source_target_pairs={{0,2},{1,3},{2,0},{3,1},{4,6},{5,7},{6,4},{7,5},{8,10},{9,11},{10,... | collective-permute-start | bytes 638984 | tf_op jit(solution)/shard_map/ppermute | solution.py:551
  124.3 12.5 %collective-permute-start.12 = (bf16[448,512]{1,0:T(8,128)(2,1)S(1)}, bf16[448,512]{1,0:T(8,128)(2,1)S(1)}, u32[]{:S(2)}, u32[]{:S(2)}) collective-permute-start(bf16[448,512]{1,0:T(8,128)(2,1)S(1)} %constant_dynamic-slice_fusion.5), channel_id=1, source_target_pairs={{0,2},{1,3},{2,0},{3,1},{4,6},{5,7},{6,4},{7,5},{8,10},{9,11},{10,... | collective-permute-start | bytes 1376264 | tf_op jit(solution)/shard_map/ppermute | solution.py:551
  125.9 8.6 %collective-permute-start.11 = (bf16[2,72,512]{2,1,0:T(8,128)(2,1)S(1)}, bf16[2,72,512]{2,1,0:T(8,128)(2,1)S(1)}, u32[]{:S(2)}, u32[]{:S(2)}) collective-permute-start(bf16[2,72,512]{2,1,0:T(8,128)(2,1)S(1)} %constant_dynamic-slice_fusion.6), channel_id=1, source_target_pairs={{0,16},{4,20},{8,24},{12,28},{16,0},{20,4},{24,8},{28,12},{1,17},{... | collective-permute-start | bytes 442376 | tf_op jit(solution)/shard_map/ppermute | solution.py:551
  137.1 8.8 %collective-permute-start.15 = (bf16[2,72,512]{2,1,0:T(8,128)(2,1)S(1)}, bf16[2,72,512]{2,1,0:T(8,128)(2,1)}, u32[]{:S(2)}, u32[]{:S(2)}) collective-permute-start(bf16[2,72,512]{2,1,0:T(8,128)(2,1)S(1)} %add_convert_fusion.10), channel_id=1, source_target_pairs={{0,16},{4,20},{8,24},{12,28},{16,0},{20,4},{24,8},{28,12},{1,17},{... | collective-permute-start | bytes 442376 | tf_op jit(solution)/shard_map/ppermute | solution.py:551
  138.3 12.3 %collective-permute-start.17 = (bf16[176,512]{1,0:T(8,128)(2,1)}, bf16[176,512]{1,0:T(8,128)(2,1)}, u32[]{:S(2)}, u32[]{:S(2)}) collective-permute-start(bf16[176,512]{1,0:T(8,128)(2,1)} %get-tuple-element.218), channel_id=1, source_target_pairs={{0,8},{4,12},{8,0},{12,4},{16,24},{20,28},{24,16},{28,20},{1,9},{5... | collective-permute-start | bytes 540680 | tf_op jit(solution)/shard_map/ppermute | solution.py:551
  139.0 11.5 %collective-permute-start.18 = (bf16[176,512]{1,0:T(8,128)(2,1)S(1)}, bf16[176,512]{1,0:T(8,128)(2,1)}, u32[]{:S(2)}, u32[]{:S(2)}) collective-permute-start(bf16[176,512]{1,0:T(8,128)(2,1)S(1)} %get-tuple-element.220), channel_id=1, source_target_pairs={{0,4},{4,0},{8,12},{12,8},{16,20},{20,16},{24,28},{28,24},{1,5},{5... | collective-permute-start | bytes 540680 | tf_op jit(solution)/shard_map/ppermute | solution.py:551
  140.1 13.4 %collective-permute-start.19 = (bf16[176,512]{1,0:T(8,128)(2,1)S(1)}, bf16[176,512]{1,0:T(8,128)(2,1)}, u32[]{:S(2)}, u32[]{:S(2)}) collective-permute-start(bf16[176,512]{1,0:T(8,128)(2,1)S(1)} %get-tuple-element.219), channel_id=1, source_target_pairs={{0,12},{4,8},{8,4},{12,0},{16,28},{20,24},{24,20},{28,16},{1,13},{... | collective-permute-start | bytes 540680 | tf_op jit(solution)/shard_map/ppermute | solution.py:551
  141.8 18.9 %all-to-all-start.4 = ((bf16[8,32,512]{2,1,0:T(8,128)(2,1)}), bf16[8,32,512]{2,1,0:T(8,128)(2,1)S(1)}, u32[]{:S(2)}, u32[]{:S(2)}) async-start(bf16[8,32,512]{2,1,0:T(8,128)(2,1)} %bitcast.24), calls=%async_computation.4 | async-start | bytes 524288 | tf_op jit(solution)/shard_map/all_to_all | solution.py:646
  147.0 7.9 %collective-permute-start.22 = (bf16[144,512]{1,0:T(8,128)(2,1)S(1)}, bf16[144,512]{1,0:T(8,128)(2,1)S(1)}, u32[]{:S(2)}, u32[]{:S(2)}) collective-permute-start(bf16[144,512]{1,0:T(8,128)(2,1)S(1)} %get-tuple-element.221), channel_id=1, source_target_pairs={{0,4},{4,0},{8,12},{12,8},{16,20},{20,16},{24,28},{28,24},{1,5},{5... | collective-permute-start | bytes 442376 | tf_op jit(solution)/shard_map/ppermute | solution.py:551
  149.1 11.5 %collective-permute-start.16 = (bf16[144,512]{1,0:T(8,128)(2,1)S(1)}, bf16[144,512]{1,0:T(8,128)(2,1)S(1)}, u32[]{:S(2)}, u32[]{:S(2)}) collective-permute-start(bf16[144,512]{1,0:T(8,128)(2,1)S(1)} %get-tuple-element.222), channel_id=1, source_target_pairs={{0,8},{4,12},{8,0},{12,4},{16,24},{20,28},{24,16},{28,20},{1,9},{5... | collective-permute-start | bytes 442376 | tf_op jit(solution)/shard_map/ppermute | solution.py:551
  154.8 9.0 %collective-permute-start.20 = (bf16[176,512]{1,0:T(8,128)(2,1)S(1)}, bf16[176,512]{1,0:T(8,128)(2,1)S(1)}, u32[]{:S(2)}, u32[]{:S(2)}) collective-permute-start(bf16[176,512]{1,0:T(8,128)(2,1)S(1)} %add_convert_fusion.9), channel_id=1, source_target_pairs={{0,16},{4,20},{8,24},{12,28},{16,0},{20,4},{24,8},{28,12},{1,17},{... | collective-permute-start | bytes 540680 | tf_op jit(solution)/shard_map/ppermute | solution.py:551
  163.9 7.6 %collective-permute-start.26 = (bf16[176,512]{1,0:T(8,128)(2,1)S(1)}, bf16[176,512]{1,0:T(8,128)(2,1)S(1)}, u32[]{:S(2)}, u32[]{:S(2)}) collective-permute-start(bf16[176,512]{1,0:T(8,128)(2,1)S(1)} %add_convert_fusion.8.p0), channel_id=1, source_target_pairs={{0,8},{4,12},{8,0},{12,4},{16,24},{20,28},{24,16},{28,20},{1,9},{5... | collective-permute-start | bytes 540680 | tf_op jit(solution)/shard_map/ppermute | solution.py:551
  164.0 9.2 %collective-permute-start.27 = (bf16[176,512]{1,0:T(8,128)(2,1)S(1)}, bf16[176,512]{1,0:T(8,128)(2,1)S(1)}, u32[]{:S(2)}, u32[]{:S(2)}) collective-permute-start(bf16[176,512]{1,0:T(8,128)(2,1)S(1)} %add_convert_fusion.8.p0), channel_id=1, source_target_pairs={{0,4},{4,0},{8,12},{12,8},{16,20},{20,16},{24,28},{28,24},{1,5},{5... | collective-permute-start | bytes 540680 | tf_op jit(solution)/shard_map/ppermute | solution.py:551
  166.2 10.2 %collective-permute-start.28 = (bf16[176,512]{1,0:T(8,128)(2,1)S(1)}, bf16[176,512]{1,0:T(8,128)(2,1)S(1)}, u32[]{:S(2)}, u32[]{:S(2)}) collective-permute-start(bf16[176,512]{1,0:T(8,128)(2,1)S(1)} %add_convert_fusion.8.p0), channel_id=1, source_target_pairs={{0,12},{4,8},{8,4},{12,0},{16,28},{20,24},{24,20},{28,16},{1,13},{... | collective-permute-start | bytes 540680 | tf_op jit(solution)/shard_map/ppermute | solution.py:551
  167.6 11.2 %collective-permute-start.23 = (bf16[288,512]{1,0:T(8,128)(2,1)S(1)}, bf16[288,512]{1,0:T(8,128)(2,1)S(1)}, u32[]{:S(2)}, u32[]{:S(2)}) collective-permute-start(bf16[288,512]{1,0:T(8,128)(2,1)S(1)} %maximum_select_fusion.2.b0), channel_id=1, source_target_pairs={{0,8},{4,12},{8,0},{12,4},{16,24},{20,28},{24,16},{28,20},{1,9},{5... | collective-permute-start | bytes 884744 | tf_op jit(solution)/shard_map/ppermute | solution.py:551
  168.2 11.2 %collective-permute-start.21 = (bf16[288,512]{1,0:T(8,128)(2,1)S(1)}, bf16[288,512]{1,0:T(8,128)(2,1)S(1)}, u32[]{:S(2)}, u32[]{:S(2)}) collective-permute-start(bf16[288,512]{1,0:T(8,128)(2,1)S(1)} %maximum_select_fusion.1.a0), channel_id=1, source_target_pairs={{0,4},{4,0},{8,12},{12,8},{16,20},{20,16},{24,28},{28,24},{1,5},{5... | collective-permute-start | bytes 884744 | tf_op jit(solution)/shard_map/ppermute | solution.py:551
  171.5 7.9 %collective-permute-start.25 = (bf16[192,512]{1,0:T(8,128)(2,1)S(1)}, bf16[192,512]{1,0:T(8,128)(2,1)S(1)}, u32[]{:S(2)}, u32[]{:S(2)}) collective-permute-start(bf16[192,512]{1,0:T(8,128)(2,1)S(1)} %add_convert_fusion.6.back_a), channel_id=1, source_target_pairs={{0,2},{1,3},{2,0},{3,1},{4,6},{5,7},{6,4},{7,5},{8,10},{9,11},{10,... | collective-permute-start | bytes 589832 | tf_op jit(solution)/shard_map/ppermute | solution.py:551
  (29 other events, 232.2 us)

commit v6 on v5

--- a/solution.py
+++ b/solution.py
@@ -116,7 +116,7 @@
         acc[...] += mm(hot, values[j * n : (j + 1) * n])
 
 
-def index_kernel(blocks, me_ref, near_ref, mask_ref, row_ref, col_ref, want_ref, count_ref):
+def index_kernel(blocks, me_ref, near_ref, mask_ref, row_ref, col_ref, want_ref):
     kn, rows = near_ref.shape
     me = me_ref[0].astype(f32)
     lanes = max(16, blocks)
@@ -161,8 +161,6 @@
     place = jnp.concatenate([place, jnp.full((SLOT - kn, rows), -1.0, f32)], axis=0)
     row_ref[...] = place.astype(jnp.int32)
     col_ref[...] = place.T
-    counts = jnp.sum((col_ref[...] >= 0.0).astype(f32), axis=1, keepdims=True)
-    count_ref[...] = jnp.broadcast_to(counts, count_ref.shape).astype(bf16)
 
 
 def message_forward_kernel(
@@ -201,7 +199,9 @@
 
     @pl.when(step == last)
     def _():
-        sum_ref[...] = acc[...].astype(bf16)
+        sum_ref[:, :D] = acc[...].astype(bf16)
+        counts = jnp.sum((col_ref[...] >= 0.0).astype(f32), axis=1, keepdims=True)
+        sum_ref[:, D:] = jnp.broadcast_to(counts, (sum_ref.shape[0], 128)).astype(bf16)
 
 
 def slope_kernel(pre_ref, slope_ref):
@@ -209,15 +209,16 @@
 
 
 def node_forward_kernel(
-    sum_a, sum_b, count_a, count_b, nodes_ref, mask_ref, want_ref, w3_ref, f1_ref, f2_ref,
+    sum_a, sum_b, nodes_ref, mask_ref, want_ref, w3_ref, f1_ref, f2_ref,
     b3_ref, gain1_ref, bias1_ref, fb1_ref, fb2_ref, gain2_ref, bias2_ref,
-    total_ref, low_ref, normed1_ref, inv1_ref, hid_ref, slope_ref, normed2_ref, inv2_ref, sent_ref, send_ref,
+    total_ref, low_ref, normed1_ref, inv1_ref, hid_ref, slope_ref, normed2_ref, inv2_ref, count_ref, sent_ref, send_ref,
 ):
     rows = nodes_ref.shape[0]
     present = present_column(mask_ref, rows)
-    count = count_a[...].astype(f32) + count_b[...].astype(f32)
-    count = count[:, :1]
-    total = sum_a[...].astype(f32) + sum_b[...].astype(f32)
+    counts = sum_a[:, D:].astype(f32) + sum_b[:, D:].astype(f32)
+    count_ref[...] = counts
+    count = counts[:, :1]
+    total = sum_a[:, :D].astype(f32) + sum_b[:, :D].astype(f32)
     high = total.astype(bf16)
     total_ref[...] = high
     rest = (total - high.astype(f32)).astype(bf16)
@@ -378,14 +379,14 @@
 
 
 def node_backward_kernel(
-    parts, place_ref, back_a, back_b, count_a, count_b, cot_ref, normed2_ref, ew1_ref, f2_ref, slope_ref, f1_ref,
+    parts, place_ref, back_a, back_b, count_ref, cot_ref, normed2_ref, ew1_ref, f2_ref, slope_ref, f1_ref,
     normed1_ref, w3_ref, low_ref, hid_ref, total_ref, mask_ref, inv1_ref, inv2_ref, gain1_ref, gain2_ref,
     mixed_ref, up_ref, bias_ref, packed_ref,
 ):
     rows = cot_ref.shape[0]
     place = place_ref[0]
     present = present_column(mask_ref, rows)
-    count = (count_a[...].astype(f32) + count_b[...].astype(f32))[:, :1]
+    count = count_ref[...][:, :1]
     back = (back_a[...].astype(f32) + back_b[...].astype(f32)).astype(bf16)
     node_back = mm(back[:, :E], ew1_ref[:, :D]) + mm(back[:, E:], ew1_ref[:, D : 2 * D])
     up = present * (cot_ref[...].astype(f32) + node_back)
@@ -735,13 +736,12 @@
     def tiled(*dims):
         return pl.BlockSpec(dims, lambda i: (i,) + (0,) * (len(dims) - 1))
 
-    place_row, place_col, want, counts = call(
+    place_row, place_col, want = call(
         functools.partial(index_kernel, blocks),
         (
             shape((SLOT, rows), jnp.int32),
             shape((rows, SLOT), f32),
             shape((n_far, 128), bf16),
-            shape((rows, 128), bf16),
         ),
         in_specs=[smem, vmem, vmem],
     )(res_place, *read(neighbours.T, mask_row))
@@ -750,8 +750,6 @@
 
     picks = (wanted[:, :1].astype(jnp.int32) == iota((n_far, rows), 1)).astype(bf16)
     far_nodes = exchange(mm(picks, nodes).astype(bf16), blocks)
-    far_nodes, counts = together((far_nodes, counts))
-    count_a, count_b = shared_sum(counts, "nbr")
 
     edge_tile = tiled(kt, rows, E)
     flat = tiled(kt * rows, D)
@@ -759,7 +757,7 @@
     kf = 3 if kn % 3 == 0 else 1
     act1, pre1, pre2, act_sum = call(
         message_forward_kernel,
-        (stored((total, D), bf16), stored((total, D), bf16), stored((total, D), bf16), shape((rows, D), bf16)),
+        (stored((total, D), bf16),) * 3 + (shape((rows, D + 128), bf16),),
         scratch=[pltpu.VMEM((width, D), bf16), pltpu.VMEM((rows, D), f32), pltpu.VMEM((rows, D), f32)],
         grid=(kn // kf,),
         in_specs=[
@@ -772,7 +770,7 @@
             fixed(D),
             fixed(D),
         ],
-        out_specs=(tiled(kf * rows, D),) * 3 + (fixed(rows, D),),
+        out_specs=(tiled(kf * rows, D),) * 3 + (fixed(rows, D + 128),),
         cost=pl.CostEstimate(flops=16 * total * D * D, bytes_accessed=total * D * 8, transcendentals=2 * total * D),
     )(*read(place_col, edges, nodes), far_nodes, *read(msg_w1, msg_w2, msg_b1, msg_b2))
 
@@ -790,7 +788,7 @@
     sum_a, sum_b = shared_sum(act_sum, "nbr")
     sum_b = after(sum_b, d1)
 
-    total_act, first_low, normed1, inv1, hidden, hidden_slope, normed2, inv2, sent, send = call(
+    total_act, first_low, normed1, inv1, hidden, hidden_slope, normed2, inv2, counts, sent, send = call(
         node_forward_kernel,
         (
             stored((rows, D), bf16),
@@ -801,10 +799,11 @@
             stored((rows, FF), bf16),
             stored((rows, D), f32),
             stored((rows, 1), f32),
+            stored((rows, 128), f32),
             stored((rows, D), bf16),
             shape((n_far, D), bf16),
         ),
-    )(sum_a, sum_b, count_a, count_b, nodes, mask_row, wanted, msg_w3, ffn_w1, ffn_w2,
+    )(sum_a, sum_b, nodes, mask_row, wanted, msg_w3, ffn_w1, ffn_w2,
       msg_b3, norm1_gain, norm1_bias, ffn_b1, ffn_b2, norm2_gain, norm2_bias)
     d2 = slope_of(after(pre2, send))
     far_sent = after(exchange(send, blocks), d2)
@@ -868,7 +867,7 @@
     for bit in nbr_bits[:-1]:
         back = add_low(back, swap(back, "nbr", bit))
     kept = fetched(
-        after(node_cot, back), normed2, edge_w1, ffn_w2, hidden_slope, ffn_w1, normed1, msg_w3, first_low, hidden, total_act,
+        counts, after(node_cot, back), normed2, edge_w1, ffn_w2, hidden_slope, ffn_w1, normed1, msg_w3, first_low, hidden, total_act,
         msg_w1, msg_w2, nodes, far_nodes
     )
     *kept, ready_w1, ready_w2, ready_nodes, ready_far = kept
@@ -884,9 +883,9 @@
             shape((16, D), f32),
             shape((node_rows, D), bf16),
         ),
-        in_specs=[smem] + [vmem] * 20,
+        in_specs=[smem] + [vmem] * 19,
     )(
-        nbr_place, back_a, back_b, count_a, count_b, *kept, mask_row, inv1, inv2, norm1_gain, norm2_gain,
+        nbr_place, back_a, back_b, *kept, mask_row, inv1, inv2, norm1_gain, norm2_gain,
     )
     bits = bits_of("res")
     order_a, order_b = bits, bits[1:2] + bits[:1] + bits[2:]

time: 182 us -> 182 us (level)
  waiting for transfers between devices: 39.7 us -> 41.6 us
    ppermute x29 -> x27, waiting for transfers between devices: 32.1 us -> 34.3 us  [swap(): lax.ppermute(values, axis, [(i, i ^ bit) for i in range(lax.axis_size(axi...]
    ppermute x29 -> x27, starting transfers between devices: 27.6 us -> 26.3 us  [swap(): lax.ppermute(values, axis, [(i, i ^ bit) for i in range(lax.axis_size(axi...]
  transfers between devices with their start and end apart: 32 -> 30, of which waited for: 18 -> 19; matrix products, arithmetic and copies ran while one was open for 2% -> 2% of each run, Pallas kernels for 18% -> 18%
where the time goes in v6:
time: 182 us; the launch traced here: 181 us
  Pallas kernels  71 us (39%)
  waiting for transfers between devices  41.6 us (23%)
  starting transfers between devices  37.6 us (21%)
  blocking collectives  24.6 us (14%)
  other arithmetic  3.05 us (2%)
    ppermute x27, waiting for transfers between devices, swap(): lax.ppermute(values, axis, [(i, i ^ bit) for i in range(lax.axis_size(axi...  34.3 us
    ppermute x27, starting transfers between devices, swap(): lax.ppermute(values, axis, [(i, i ^ bit) for i in range(lax.axis_size(axi...  26.3 us
    all_to_all x2, blocking collectives, exchange(): return lax.all_to_all(shaped, 'res', 0, 0, tiled=True).reshape(values.shape)  24.6 us
    pallas_call x1, Pallas kernels, on_device(): call(edge_kernel, (shape((kn, rows, E), bf16), stored((total, E), f32), s...  14.8 us
    pallas_call x1, Pallas kernels, on_device(): call(functools.partial(message_backward_kernel, parts), (shape((kn, rows,...  12 us
    pallas_call x2, Pallas kernels, slope_of(): call(slope_kernel, stored((total, D), bf16), grid=grid, in_specs=[flat],...  11.7 us
    all_to_all x3, starting transfers between devices, exchange(): return lax.all_to_all(shaped, 'res', 0, 0, tiled=True).reshape(values.shape)  11.3 us
    pallas_call x1, Pallas kernels, on_device(): call(message_forward_kernel, (stored((total, D), bf16),) * 3 + (shape((ro...  10.3 us
  transfers between devices with their start and end apart: 30, of which 19 were waited for; matrix products, arithmetic and copies ran while one was open for 2% of the time, Pallas kernels for 18%

profile of v6, /device:TPU:0, one launch (start us, length us, event | category | flops | bytes accessed | tf_op | source)
XLA Modules:
  0.0 181.4 jit_solution(14322683435261473443)
XLA Ops:
  0.7 2.7 %shard_map.467 = (s32[16,192]{1,0:T(8,128)S(1)}, f32[192,16]{1,0:T(8,128)S(1)}, bf16[256,128]{1,0:T(8,128)(2,1)S(1)}) custom-call(s32[1]{0:T(128)} %bitcast.me_ref, s32[15,192]{1,0:T(8,128)} %bitcast.56, s32[1,192]{1,0:T(1,128)} %bitcast.45), custom_call_target="tpu_custom_call" | custom-call | tf_op jit(solution)/shard_map/pallas_call | solution.py:739
  3.4 14.0 %all_to_all.25 = bf16[8,32,128]{2,1,0:T(8,128)(2,1)S(1)} all-to-all(bf16[8,32,128]{2,1,0:T(8,128)(2,1)S(1)} %bitcast.44), channel_id=1, replica_groups=mesh['res'=8,'nbr'=4] {'res'}, dimensions={0} | all-to-all | bytes 131072 | tf_op jit(solution)/shard_map/all_to_all | solution.py:647
  18.7 10.6 %all_to_all.26 = bf16[8,32,512]{2,1,0:T(8,128)(2,1)S(1)} all-to-all(bf16[8,32,512]{2,1,0:T(8,128)(2,1)S(1)} %bitcast.50), channel_id=1, replica_groups=mesh['res'=8,'nbr'=4] {'res'}, dimensions={0} | all-to-all | bytes 524288 | tf_op jit(solution)/shard_map/all_to_all | solution.py:647
  29.3 10.3 %shard_map.468 = (bf16[2880,512]{1,0:T(8,128)(2,1)}, bf16[2880,512]{1,0:T(8,128)(2,1)}, bf16[2880,512]{1,0:T(8,128)(2,1)}, bf16[192,640]{1,0:T(8,128)(2,1)S(1)}) custom-call(f32[192,16]{1,0:T(8,128)} %copy-done.17, bf16[15,192,192]{2,1,0:T(8,128)(2,1)} %bitcast.58, bf16[192,512]{1,0:T(8,128)(2,1)} %refs_14_.1, bf16[256,512]{1,0:T(8,128)(2,1)S(1)} %bitcast.38, ...), custom_call_target="tpu_custom_call" | custom-call | flops 12079595520 | bytes 11796480 | tf_op jit(solution)/shard_map/pallas_call | solution.py:758
  42.9 5.9 %shard_map.469.d1_ref = bf16[2880,512]{1,0:T(8,128)(2,1)} custom-call(bf16[2880,512]{1,0:T(8,128)(2,1)} %get-tuple-element.123.pre_ref), custom_call_target="tpu_custom_call" | custom-call | flops 14745600 | bytes 5898240 | tf_op jit(solution)/shard_map/pallas_call | solution.py:778
  49.4 4.0 %shard_map.470 = (bf16[192,512]{1,0:T(8,128)(2,1)}, bf16[192,512]{1,0:T(8,128)(2,1)}, f32[192,512]{1,0:T(8,128)}, f32[192,1]{1,0:T(8,128)}, bf16[192,2048]{1,0:T...) custom-call(bf16[192,640]{1,0:T(8,128)(2,1)S(1)} %add_convert_fusion, ...), custom_call_target="tpu_custom_call" | custom-call | tf_op jit(solution)/shard_map/pallas_call | solution.py:791
  53.4 3.6 %all-to-all-start.2 = ((bf16[8,32,512]{2,1,0:T(8,128)(2,1)}), bf16[8,32,512]{2,1,0:T(8,128)(2,1)S(1)}, u32[]{:S(2)}, u32[]{:S(2)}) async-start(bf16[8,32,512]{2,1,0:T(8,128)(2,1)} %bitcast.9), calls=%async_computation.2 | async-start | bytes 524288 | tf_op jit(solution)/shard_map/all_to_all | solution.py:647
  57.0 5.8 %shard_map.471.d2_ref = bf16[2880,512]{1,0:T(8,128)(2,1)} custom-call(bf16[2880,512]{1,0:T(8,128)(2,1)} %get-tuple-element.129.pre_ref), custom_call_target="tpu_custom_call" | custom-call | flops 14745600 | bytes 5898240 | tf_op jit(solution)/shard_map/pallas_call | solution.py:778
  62.8 2.7 %all-to-all-done.2 = bf16[8,32,512]{2,1,0:T(8,128)(2,1)S(1)} async-done(((bf16[8,32,512]{2,1,0:T(8,128)(2,1)}), bf16[8,32,512]{2,1,0:T(8,128)(2,1)S(1)}, u32[]{:S(2)}, u32[]{:S(2)}) %all-to-all-start.2) | async-done | bytes 262176 | tf_op jit(solution)/shard_map/all_to_all | solution.py:647
  65.5 14.8 %shard_map.472 = (bf16[15,192,192]{2,1,0:T(8,128)(2,1)}, f32[2880,192]{1,0:T(8,128)}, bf16[192,192]{1,0:T(8,128)(2,1)}, bf16[256,192]{1,0:T(8,128)(2,1)}, bf16[1...) custom-call(s32[16,192]{1,0:T(8,128)} %copy-done.18, ...), custom_call_target="tpu_custom_call" | custom-call | flops 12079595520 | bytes 6635520 | tf_op jit(solution)/shard_map/pallas_call | solution.py:813
  80.3 3.6 %all-to-all-start.3 = ((bf16[8,32,192]{2,1,0:T(8,128)(2,1)}), bf16[8,32,192]{2,1,0:T(8,128)(2,1)S(1)}, u32[]{:S(2)}, u32[]{:S(2)}) async-start(bf16[8,32,192]{2,1,0:T(8,128)(2,1)} %bitcast.55), calls=%async_computation.3 | async-start | bytes 262144 | tf_op jit(solution)/shard_map/all_to_all | solution.py:647
  83.9 2.7 %shard_map.473 = bf16[4,208,512]{2,1,0:T(8,128)(2,1)} custom-call(bf16[192,512]{1,0:T(8,128)(2,1)} %get-tuple-element.94.sent_ref, bf16[256,512]{1,0:T(8,128)(2,1)} %bitcast.43, bf16[192,192]{1,0:T(8,128)(2,1)} %get-tuple-element.133.own_ref, bf16[256,192]{1,0:T(8,128)(2,1)} %get-tuple-element.135.far_grad_ref, ...), custom_call_target="tpu_custom_call" | custom-call | flops 1000000000 | bytes 1000000 | tf_op jit(solution)/shard_map/pallas_call | solution.py:860
  86.5 4.6 %all-to-all-done.3 = bf16[8,32,192]{2,1,0:T(8,128)(2,1)S(1)} async-done(((bf16[8,32,192]{2,1,0:T(8,128)(2,1)}), bf16[8,32,192]{2,1,0:T(8,128)(2,1)S(1)}, u32[]{:S(2)}, u32[]{:S(2)}) %all-to-all-start.3) | async-done | bytes 98336 | tf_op jit(solution)/shard_map/all_to_all | solution.py:647
  95.5 4.3 %shard_map.475 = (f32[192,128]{1,0:T(8,128)S(1)}, bf16[192,512]{1,0:T(8,128)(2,1)S(1)}, f32[192,512]{1,0:T(8,128)S(1)}, bf16[192,1216]{1,0:T(8,128)(2,1)S(1)}, b...) custom-call(f32[192,128]{1,0:T(8,128)} %get-tuple-element.141.refs_0, ...), custom_call_target="tpu_custom_call" | custom-call | bytes 20922368 | tf_op jit(solution)/shard_map/pallas_call | solution.py:370
  99.9 2.6 %shard_map.476 = (f32[192,512]{1,0:T(8,128)S(1)}, f32[192,512]{1,0:T(8,128)S(1)}, f32[16,512]{1,0:T(8,128)S(1)}, bf16[1152,512]{1,0:T(8,128)(2,1)S(1)}) custom-call(s32[1]{0:T(128)} %bitcast.15.place_ref, bf16[192,384]{1,0:T(8,128)(2,1)S(1)} %add_convert_fusion.13.back_a, bf16[192,384]{1,0:T(8,128)(2,1)S(1)} %collective-permute-done.3.back_b, ...), custom_call_target="tpu_custom_call" | custom-call | tf_op jit(solution)/shard_map/pallas_call | solution.py:878
  104.1 12.0 %shard_map.477 = (f32[15,192,192]{2,1,0:T(8,128)}, bf16[192,512]{1,0:T(8,128)(2,1)S(1)}, bf16[256,512]{1,0:T(8,128)(2,1)}, bf16[192,512]{1,0:T(8,128)(2,1)S(1)},...) custom-call(s32[1]{0:T(128)S(6)} %and.66.core_ref, s32[16,192]{1,0:T(8,128)} %copy-done.18, ...), custom_call_target="tpu_custom_call" | custom-call | flops 12079595520 | bytes 14745600 | tf_op jit(solution)/shard_map/pallas_call | solution.py:900
  127.7 6.3 %collective-permute-done.9 = bf16[2,72,512]{2,1,0:T(8,128)(2,1)S(1)} collective-permute-done((bf16[2,72,512]{2,1,0:T(8,128)(2,1)S(1)}, bf16[2,72,512]{2,1,0:T(8,128)(2,1)S(1)}, u32[]{:S(2)}, u32[]{:S(2)}) %collective-permute-start.9) | collective-permute-done | bytes 147488 | tf_op jit(solution)/shard_map/ppermute | solution.py:552
  134.0 2.4 %collective-permute-done.10 = bf16[448,512]{1,0:T(8,128)(2,1)S(1)} collective-permute-done((bf16[448,512]{1,0:T(8,128)(2,1)S(1)}, bf16[448,512]{1,0:T(8,128)(2,1)S(1)}, u32[]{:S(2)}, u32[]{:S(2)}) %collective-permute-start.10) | collective-permute-done | bytes 458784 | tf_op jit(solution)/shard_map/ppermute | solution.py:552
  141.5 4.1 %all-to-all-start.4 = ((bf16[8,32,512]{2,1,0:T(8,128)(2,1)}), bf16[8,32,512]{2,1,0:T(8,128)(2,1)S(1)}, u32[]{:S(2)}, u32[]{:S(2)}) async-start(bf16[8,32,512]{2,1,0:T(8,128)(2,1)} %bitcast.24), calls=%async_computation.4 | async-start | bytes 524288 | tf_op jit(solution)/shard_map/all_to_all | solution.py:647
  149.3 3.9 %collective-permute-done.17 = bf16[176,512]{1,0:T(8,128)(2,1)} collective-permute-done((bf16[176,512]{1,0:T(8,128)(2,1)S(1)}, bf16[176,512]{1,0:T(8,128)(2,1)}, u32[]{:S(2)}, u32[]{:S(2)}) %collective-permute-start.17) | collective-permute-done | bytes 180256 | tf_op jit(solution)/shard_map/ppermute | solution.py:552
  154.6 6.0 %collective-permute-done.14 = bf16[144,512]{1,0:T(8,128)(2,1)S(1)} collective-permute-done((bf16[144,512]{1,0:T(8,128)(2,1)S(1)}, bf16[144,512]{1,0:T(8,128)(2,1)S(1)}, u32[]{:S(2)}, u32[]{:S(2)}) %collective-permute-start.14) | collective-permute-done | bytes 147488 | tf_op jit(solution)/shard_map/ppermute | solution.py:552
  163.7 2.3 %collective-permute-start.25 = (bf16[176,512]{1,0:T(8,128)(2,1)S(1)}, bf16[176,512]{1,0:T(8,128)(2,1)S(1)}, u32[]{:S(2)}, u32[]{:S(2)}) collective-permute-start(bf16[176,512]{1,0:T(8,128)(2,1)S(1)} %add_convert_fusion.8.p0), channel_id=1, source_target_pairs={{0,4},{4,0},{8,12},{12,8},{16,20},{20,16},{24,28},{28,24},{1,5},{5... | collective-permute-start | bytes 540680 | tf_op jit(solution)/shard_map/ppermute | solution.py:552
  173.1 3.0 %collective-permute-done.26.p3 = bf16[176,512]{1,0:T(8,128)(2,1)S(1)} collective-permute-done((bf16[176,512]{1,0:T(8,128)(2,1)S(1)}, bf16[176,512]{1,0:T(8,128)(2,1)S(1)}, u32[]{:S(2)}, u32[]{:S(2)}) %collective-permute-start.26) | collective-permute-done | bytes 180256 | tf_op jit(solution)/shard_map/ppermute | solution.py:552
  179.2 2.2 %shard_map.479 = (f32[192,512]{1,0:T(8,128)}, f32[128,2048]{1,0:T(8,128)}, f32[512,512]{1,0:T(8,128)}, f32[128,512]{1,0:T(8,128)}) custom-call(s32[2]{0:T(128)S(1)} %pad_add_fusion.at_ref, bf16[288,512]{1,0:T(8,128)(2,1)S(1)} %maximum_select_fusion.1.a0, bf16[288,512]{1,0:T(8,128)(2,1)S(1)} %collective-permute-done.19.a1, ...), custom_call_target="tpu_custom_call" | custom-call | tf_op jit(solution)/shard_map/pallas_call | solution.py:973
  (128 shorter events, 45.8 us)
Async XLA Ops:
  41.2 8.1 %collective-permute-start.1 = (bf16[192,640]{1,0:T(8,128)(2,1)S(1)}, bf16[192,640]{1,0:T(8,128)(2,1)S(1)}, u32[]{:S(2)}, u32[]{:S(2)}) collective-permute-start(bf16[192,640]{1,0:T(8,128)(2,1)S(1)} %add_convert_fusion.5.sum_a), channel_id=1, source_target_pairs={{0,2},{1,3},{2,0},{3,1},{4,6},{5,7},{6,4},{7,5},{8,10},{9,11},{10,... | collective-permute-start | bytes 737288 | tf_op jit(solution)/shard_map/ppermute | solution.py:552
  53.4 12.1 %all-to-all-start.2 = ((bf16[8,32,512]{2,1,0:T(8,128)(2,1)}), bf16[8,32,512]{2,1,0:T(8,128)(2,1)S(1)}, u32[]{:S(2)}, u32[]{:S(2)}) async-start(bf16[8,32,512]{2,1,0:T(8,128)(2,1)} %bitcast.9), calls=%async_computation.2 | async-start | bytes 524288 | tf_op jit(solution)/shard_map/all_to_all | solution.py:647
  80.3 10.9 %all-to-all-start.3 = ((bf16[8,32,192]{2,1,0:T(8,128)(2,1)}), bf16[8,32,192]{2,1,0:T(8,128)(2,1)S(1)}, u32[]{:S(2)}, u32[]{:S(2)}) async-start(bf16[8,32,192]{2,1,0:T(8,128)(2,1)} %bitcast.55), calls=%async_computation.3 | async-start | bytes 262144 | tf_op jit(solution)/shard_map/all_to_all | solution.py:647
  102.6 13.5 %collective-permute-start.4 = (bf16[288,512]{1,0:T(8,128)(2,1)S(1)}, bf16[288,512]{1,0:T(8,128)(2,1)S(1)}, u32[]{:S(2)}, u32[]{:S(2)}) collective-permute-start(bf16[288,512]{1,0:T(8,128)(2,1)S(1)} %get-tuple-element.215), channel_id=1, source_target_pairs={{0,4},{4,0},{8,12},{12,8},{16,20},{20,16},{24,28},{28,24},{1,5},{5... | collective-permute-start | bytes 884744 | tf_op jit(solution)/shard_map/ppermute | solution.py:552
  102.9 13.2 %collective-permute-start.5 = (bf16[288,512]{1,0:T(8,128)(2,1)S(1)}, bf16[288,512]{1,0:T(8,128)(2,1)S(1)}, u32[]{:S(2)}, u32[]{:S(2)}) collective-permute-start(bf16[288,512]{1,0:T(8,128)(2,1)S(1)} %get-tuple-element.214), channel_id=1, source_target_pairs={{0,8},{4,12},{8,0},{12,4},{16,24},{20,28},{24,16},{28,20},{1,9},{5... | collective-permute-start | bytes 884744 | tf_op jit(solution)/shard_map/ppermute | solution.py:552
  104.0 15.7 %collective-permute-start.11 = (bf16[416,512]{1,0:T(8,128)(2,1)S(1)}, bf16[416,512]{1,0:T(8,128)(2,1)S(1)}, u32[]{:S(2)}, u32[]{:S(2)}) collective-permute-start(bf16[416,512]{1,0:T(8,128)(2,1)S(1)} %constant_dynamic-slice_fusion.4), channel_id=1, source_target_pairs={{0,1},{1,0},{2,3},{3,2},{4,5},{5,4},{6,7},{7,6},{8,9},{9,8},{10,11... | collective-permute-start | bytes 1277960 | tf_op jit(solution)/shard_map/ppermute | solution.py:552
  116.1 7.5 %collective-permute-start.8 = (bf16[2,448,512]{2,1,0:T(8,128)(2,1)S(1)}, bf16[2,448,512]{2,1,0:T(8,128)(2,1)S(1)}, u32[]{:S(2)}, u32[]{:S(2)}) collective-permute-start(bf16[2,448,512]{2,1,0:T(8,128)(2,1)S(1)} %get-tuple-element.179), channel_id=1, source_target_pairs={{0,1},{1,0},{2,3},{3,2},{4,5},{5,4},{6,7},{7,6},{8,9},{9,8},{10,11... | collective-permute-start | bytes 2752520 | tf_op jit(solution)/shard_map/ppermute | solution.py:552
  119.9 7.7 %collective-permute-start.12 = (bf16[208,512]{1,0:T(8,128)(2,1)S(1)}, bf16[208,512]{1,0:T(8,128)(2,1)S(1)}, u32[]{:S(2)}, u32[]{:S(2)}) collective-permute-start(bf16[208,512]{1,0:T(8,128)(2,1)S(1)} %constant_dynamic-slice_fusion.3), channel_id=1, source_target_pairs={{0,2},{1,3},{2,0},{3,1},{4,6},{5,7},{6,4},{7,5},{8,10},{9,11},{10,... | collective-permute-start | bytes 638984 | tf_op jit(solution)/shard_map/ppermute | solution.py:552
  123.9 12.5 %collective-permute-start.10 = (bf16[448,512]{1,0:T(8,128)(2,1)S(1)}, bf16[448,512]{1,0:T(8,128)(2,1)S(1)}, u32[]{:S(2)}, u32[]{:S(2)}) collective-permute-start(bf16[448,512]{1,0:T(8,128)(2,1)S(1)} %constant_dynamic-slice_fusion.5), channel_id=1, source_target_pairs={{0,2},{1,3},{2,0},{3,1},{4,6},{5,7},{6,4},{7,5},{8,10},{9,11},{10,... | collective-permute-start | bytes 1376264 | tf_op jit(solution)/shard_map/ppermute | solution.py:552
  125.4 8.6 %collective-permute-start.9 = (bf16[2,72,512]{2,1,0:T(8,128)(2,1)S(1)}, bf16[2,72,512]{2,1,0:T(8,128)(2,1)S(1)}, u32[]{:S(2)}, u32[]{:S(2)}) collective-permute-start(bf16[2,72,512]{2,1,0:T(8,128)(2,1)S(1)} %constant_dynamic-slice_fusion.6), channel_id=1, source_target_pairs={{0,16},{4,20},{8,24},{12,28},{16,0},{20,4},{24,8},{28,12},{1,17},{... | collective-permute-start | bytes 442376 | tf_op jit(solution)/shard_map/ppermute | solution.py:552
  136.8 8.8 %collective-permute-start.13 = (bf16[2,72,512]{2,1,0:T(8,128)(2,1)S(1)}, bf16[2,72,512]{2,1,0:T(8,128)(2,1)S(1)}, u32[]{:S(2)}, u32[]{:S(2)}) collective-permute-start(bf16[2,72,512]{2,1,0:T(8,128)(2,1)S(1)} %add_convert_fusion.10), channel_id=1, source_target_pairs={{0,16},{4,20},{8,24},{12,28},{16,0},{20,4},{24,8},{28,12},{1,17},{... | collective-permute-start | bytes 442376 | tf_op jit(solution)/shard_map/ppermute | solution.py:552
  138.0 11.3 %collective-permute-start.15 = (bf16[176,512]{1,0:T(8,128)(2,1)}, bf16[176,512]{1,0:T(8,128)(2,1)}, u32[]{:S(2)}, u32[]{:S(2)}) collective-permute-start(bf16[176,512]{1,0:T(8,128)(2,1)} %get-tuple-element.216), channel_id=1, source_target_pairs={{0,8},{4,12},{8,0},{12,4},{16,24},{20,28},{24,16},{28,20},{1,9},{5... | collective-permute-start | bytes 540680 | tf_op jit(solution)/shard_map/ppermute | solution.py:552
  138.8 10.5 %collective-permute-start.16 = (bf16[176,512]{1,0:T(8,128)(2,1)}, bf16[176,512]{1,0:T(8,128)(2,1)}, u32[]{:S(2)}, u32[]{:S(2)}) collective-permute-start(bf16[176,512]{1,0:T(8,128)(2,1)} %get-tuple-element.218), channel_id=1, source_target_pairs={{0,4},{4,0},{8,12},{12,8},{16,20},{20,16},{24,28},{28,24},{1,5},{5... | collective-permute-start | bytes 540680 | tf_op jit(solution)/shard_map/ppermute | solution.py:552
  139.8 13.3 %collective-permute-start.17 = (bf16[176,512]{1,0:T(8,128)(2,1)S(1)}, bf16[176,512]{1,0:T(8,128)(2,1)}, u32[]{:S(2)}, u32[]{:S(2)}) collective-permute-start(bf16[176,512]{1,0:T(8,128)(2,1)S(1)} %get-tuple-element.217), channel_id=1, source_target_pairs={{0,12},{4,8},{8,4},{12,0},{16,28},{20,24},{24,20},{28,16},{1,13},{... | collective-permute-start | bytes 540680 | tf_op jit(solution)/shard_map/ppermute | solution.py:552
  141.5 19.2 %all-to-all-start.4 = ((bf16[8,32,512]{2,1,0:T(8,128)(2,1)}), bf16[8,32,512]{2,1,0:T(8,128)(2,1)S(1)}, u32[]{:S(2)}, u32[]{:S(2)}) async-start(bf16[8,32,512]{2,1,0:T(8,128)(2,1)} %bitcast.24), calls=%async_computation.4 | async-start | bytes 524288 | tf_op jit(solution)/shard_map/all_to_all | solution.py:647
  145.7 8.8 %collective-permute-start.20 = (bf16[144,512]{1,0:T(8,128)(2,1)S(1)}, bf16[144,512]{1,0:T(8,128)(2,1)S(1)}, u32[]{:S(2)}, u32[]{:S(2)}) collective-permute-start(bf16[144,512]{1,0:T(8,128)(2,1)S(1)} %get-tuple-element.219), channel_id=1, source_target_pairs={{0,4},{4,0},{8,12},{12,8},{16,20},{20,16},{24,28},{28,24},{1,5},{5... | collective-permute-start | bytes 442376 | tf_op jit(solution)/shard_map/ppermute | solution.py:552
  147.8 12.8 %collective-permute-start.14 = (bf16[144,512]{1,0:T(8,128)(2,1)S(1)}, bf16[144,512]{1,0:T(8,128)(2,1)S(1)}, u32[]{:S(2)}, u32[]{:S(2)}) collective-permute-start(bf16[144,512]{1,0:T(8,128)(2,1)S(1)} %get-tuple-element.220), channel_id=1, source_target_pairs={{0,8},{4,12},{8,0},{12,4},{16,24},{20,28},{24,16},{28,20},{1,9},{5... | collective-permute-start | bytes 442376 | tf_op jit(solution)/shard_map/ppermute | solution.py:552
  154.5 9.1 %collective-permute-start.18 = (bf16[176,512]{1,0:T(8,128)(2,1)S(1)}, bf16[176,512]{1,0:T(8,128)(2,1)S(1)}, u32[]{:S(2)}, u32[]{:S(2)}) collective-permute-start(bf16[176,512]{1,0:T(8,128)(2,1)S(1)} %add_convert_fusion.9), channel_id=1, source_target_pairs={{0,16},{4,20},{8,24},{12,28},{16,0},{20,4},{24,8},{28,12},{1,17},{... | collective-permute-start | bytes 540680 | tf_op jit(solution)/shard_map/ppermute | solution.py:552
  163.6 7.6 %collective-permute-start.24 = (bf16[176,512]{1,0:T(8,128)(2,1)S(1)}, bf16[176,512]{1,0:T(8,128)(2,1)S(1)}, u32[]{:S(2)}, u32[]{:S(2)}) collective-permute-start(bf16[176,512]{1,0:T(8,128)(2,1)S(1)} %add_convert_fusion.8.p0), channel_id=1, source_target_pairs={{0,8},{4,12},{8,0},{12,4},{16,24},{20,28},{24,16},{28,20},{1,9},{5... | collective-permute-start | bytes 540680 | tf_op jit(solution)/shard_map/ppermute | solution.py:552
  163.7 9.4 %collective-permute-start.25 = (bf16[176,512]{1,0:T(8,128)(2,1)S(1)}, bf16[176,512]{1,0:T(8,128)(2,1)S(1)}, u32[]{:S(2)}, u32[]{:S(2)}) collective-permute-start(bf16[176,512]{1,0:T(8,128)(2,1)S(1)} %add_convert_fusion.8.p0), channel_id=1, source_target_pairs={{0,4},{4,0},{8,12},{12,8},{16,20},{20,16},{24,28},{28,24},{1,5},{5... | collective-permute-start | bytes 540680 | tf_op jit(solution)/shard_map/ppermute | solution.py:552
  166.0 10.1 %collective-permute-start.26 = (bf16[176,512]{1,0:T(8,128)(2,1)S(1)}, bf16[176,512]{1,0:T(8,128)(2,1)S(1)}, u32[]{:S(2)}, u32[]{:S(2)}) collective-permute-start(bf16[176,512]{1,0:T(8,128)(2,1)S(1)} %add_convert_fusion.8.p0), channel_id=1, source_target_pairs={{0,12},{4,8},{8,4},{12,0},{16,28},{20,24},{24,20},{28,16},{1,13},{... | collective-permute-start | bytes 540680 | tf_op jit(solution)/shard_map/ppermute | solution.py:552
  167.3 11.4 %collective-permute-start.21 = (bf16[288,512]{1,0:T(8,128)(2,1)S(1)}, bf16[288,512]{1,0:T(8,128)(2,1)S(1)}, u32[]{:S(2)}, u32[]{:S(2)}) collective-permute-start(bf16[288,512]{1,0:T(8,128)(2,1)S(1)} %maximum_select_fusion.2.b0), channel_id=1, source_target_pairs={{0,8},{4,12},{8,0},{12,4},{16,24},{20,28},{24,16},{28,20},{1,9},{5... | collective-permute-start | bytes 884744 | tf_op jit(solution)/shard_map/ppermute | solution.py:552
  167.9 11.2 %collective-permute-start.19 = (bf16[288,512]{1,0:T(8,128)(2,1)S(1)}, bf16[288,512]{1,0:T(8,128)(2,1)S(1)}, u32[]{:S(2)}, u32[]{:S(2)}) collective-permute-start(bf16[288,512]{1,0:T(8,128)(2,1)S(1)} %maximum_select_fusion.1.a0), channel_id=1, source_target_pairs={{0,4},{4,0},{8,12},{12,8},{16,20},{20,16},{24,28},{28,24},{1,5},{5... | collective-permute-start | bytes 884744 | tf_op jit(solution)/shard_map/ppermute | solution.py:552
  171.1 8.0 %collective-permute-start.23 = (bf16[192,512]{1,0:T(8,128)(2,1)S(1)}, bf16[192,512]{1,0:T(8,128)(2,1)S(1)}, u32[]{:S(2)}, u32[]{:S(2)}) collective-permute-start(bf16[192,512]{1,0:T(8,128)(2,1)S(1)} %add_convert_fusion.7.back_a), channel_id=1, source_target_pairs={{0,2},{1,3},{2,0},{3,1},{4,6},{5,7},{6,4},{7,5},{8,10},{9,11},{10,... | collective-permute-start | bytes 589832 | tf_op jit(solution)/shard_map/ppermute | solution.py:552
  (27 other events, 218.5 us)

commit v7 on v6

--- a/solution.py
+++ b/solution.py
@@ -288,7 +288,7 @@
     low1 = (slope1 * mm_nt(low2, w2_ref[...])).astype(bf16)
     w1_acc[...] += mm_tn(edge, low1)
     slot_sums(row_ref, step * kt, kt, width, low1, sums)
-    base_ref[...] = grad + mm(low1, edge_weight)
+    base_ref[...] = (grad + mm(low1, edge_weight)).astype(bf16)
     own_sum = gathered(low1.astype(f32), rows)
     own_acc[...] += own_sum
     row = iota((16, 1), 0)
@@ -452,7 +452,7 @@
     low1 = grad1.astype(bf16)
     w1_acc[...] += mm_tn(edge, low1)
     slot_sums(row_ref, step * kt, kt, width, low1, sums)
-    grad = base_ref[...] + mm_nt(low1, w1_ref[2 * D :, :])
+    grad = base_ref[...].astype(f32) + mm_nt(low1, w1_ref[2 * D :, :])
     out_ref[...] = grad.reshape(kt, rows, E)
     own_sum = gathered(grad1, rows)
     own_acc[...] += own_sum
@@ -814,7 +814,7 @@
         edge_kernel,
         (
             shape((kn, rows, E), bf16),
-            stored((total, E), f32),
+            stored((total, E), bf16),
             stored((rows, E), bf16),
             stored((n_far, E), bf16),
             stored((rows, E), bf16),

time: 182 us -> 182 us (level)
  no operation moved by 1% of the time
where the time goes in v7:
time: 182 us; the launch traced here: 181 us
  Pallas kernels  70.4 us (39%)
  waiting for transfers between devices  41.9 us (23%)
  starting transfers between devices  37.4 us (21%)
  blocking collectives  24.6 us (14%)
  other arithmetic  3.05 us (2%)
    ppermute x27, waiting for transfers between devices, swap(): lax.ppermute(values, axis, [(i, i ^ bit) for i in range(lax.axis_size(axi...  34.5 us
    ppermute x27, starting transfers between devices, swap(): lax.ppermute(values, axis, [(i, i ^ bit) for i in range(lax.axis_size(axi...  26.2 us
    all_to_all x2, blocking collectives, exchange(): return lax.all_to_all(shaped, 'res', 0, 0, tiled=True).reshape(values.shape)  24.6 us
    pallas_call x1, Pallas kernels, on_device(): call(edge_kernel, (shape((kn, rows, E), bf16), stored((total, E), bf16),...  14.5 us
    pallas_call x1, Pallas kernels, on_device(): call(functools.partial(message_backward_kernel, parts), (shape((kn, rows,...  11.7 us
    pallas_call x2, Pallas kernels, slope_of(): call(slope_kernel, stored((total, D), bf16), grid=grid, in_specs=[flat],...  11.7 us
    all_to_all x3, starting transfers between devices, exchange(): return lax.all_to_all(shaped, 'res', 0, 0, tiled=True).reshape(values.shape)  11.2 us
    pallas_call x1, Pallas kernels, on_device(): call(message_forward_kernel, (stored((total, D), bf16),) * 3 + (shape((ro...  10.3 us
  transfers between devices with their start and end apart: 30, of which 19 were waited for; matrix products, arithmetic and copies ran while one was open for 2% of the time, Pallas kernels for 18%

profile of v7, /device:TPU:0, one launch (start us, length us, event | category | flops | bytes accessed | tf_op | source)
XLA Modules:
  0.0 180.8 jit_solution(12293297889860664948)
XLA Ops:
  0.7 2.7 %shard_map.467 = (s32[16,192]{1,0:T(8,128)S(1)}, f32[192,16]{1,0:T(8,128)S(1)}, bf16[256,128]{1,0:T(8,128)(2,1)S(1)}) custom-call(s32[1]{0:T(128)} %bitcast.me_ref, s32[15,192]{1,0:T(8,128)} %bitcast.56, s32[1,192]{1,0:T(1,128)} %bitcast.45), custom_call_target="tpu_custom_call" | custom-call | tf_op jit(solution)/shard_map/pallas_call | solution.py:739
  3.4 14.0 %all_to_all.25 = bf16[8,32,128]{2,1,0:T(8,128)(2,1)S(1)} all-to-all(bf16[8,32,128]{2,1,0:T(8,128)(2,1)S(1)} %bitcast.44), channel_id=1, replica_groups=mesh['res'=8,'nbr'=4] {'res'}, dimensions={0} | all-to-all | bytes 131072 | tf_op jit(solution)/shard_map/all_to_all | solution.py:647
  18.7 10.6 %all_to_all.26 = bf16[8,32,512]{2,1,0:T(8,128)(2,1)S(1)} all-to-all(bf16[8,32,512]{2,1,0:T(8,128)(2,1)S(1)} %bitcast.50), channel_id=1, replica_groups=mesh['res'=8,'nbr'=4] {'res'}, dimensions={0} | all-to-all | bytes 524288 | tf_op jit(solution)/shard_map/all_to_all | solution.py:647
  29.3 10.3 %shard_map.468 = (bf16[2880,512]{1,0:T(8,128)(2,1)}, bf16[2880,512]{1,0:T(8,128)(2,1)}, bf16[2880,512]{1,0:T(8,128)(2,1)}, bf16[192,640]{1,0:T(8,128)(2,1)S(1)}) custom-call(f32[192,16]{1,0:T(8,128)} %copy-done.17, bf16[15,192,192]{2,1,0:T(8,128)(2,1)} %bitcast.58, bf16[192,512]{1,0:T(8,128)(2,1)} %refs_14_.1, bf16[256,512]{1,0:T(8,128)(2,1)S(1)} %bitcast.38, ...), custom_call_target="tpu_custom_call" | custom-call | flops 12079595520 | bytes 11796480 | tf_op jit(solution)/shard_map/pallas_call | solution.py:758
  42.9 5.9 %shard_map.469.d1_ref = bf16[2880,512]{1,0:T(8,128)(2,1)} custom-call(bf16[2880,512]{1,0:T(8,128)(2,1)} %get-tuple-element.123.pre_ref), custom_call_target="tpu_custom_call" | custom-call | flops 14745600 | bytes 5898240 | tf_op jit(solution)/shard_map/pallas_call | solution.py:778
  49.4 4.0 %shard_map.470 = (bf16[192,512]{1,0:T(8,128)(2,1)}, bf16[192,512]{1,0:T(8,128)(2,1)}, f32[192,512]{1,0:T(8,128)}, f32[192,1]{1,0:T(8,128)}, bf16[192,2048]{1,0:T...) custom-call(bf16[192,640]{1,0:T(8,128)(2,1)S(1)} %add_convert_fusion, ...), custom_call_target="tpu_custom_call" | custom-call | tf_op jit(solution)/shard_map/pallas_call | solution.py:791
  53.4 3.6 %all-to-all-start.2 = ((bf16[8,32,512]{2,1,0:T(8,128)(2,1)}), bf16[8,32,512]{2,1,0:T(8,128)(2,1)S(1)}, u32[]{:S(2)}, u32[]{:S(2)}) async-start(bf16[8,32,512]{2,1,0:T(8,128)(2,1)} %bitcast.9), calls=%async_computation.2 | async-start | bytes 524288 | tf_op jit(solution)/shard_map/all_to_all | solution.py:647
  57.0 5.8 %shard_map.471.d2_ref = bf16[2880,512]{1,0:T(8,128)(2,1)} custom-call(bf16[2880,512]{1,0:T(8,128)(2,1)} %get-tuple-element.129.pre_ref), custom_call_target="tpu_custom_call" | custom-call | flops 14745600 | bytes 5898240 | tf_op jit(solution)/shard_map/pallas_call | solution.py:778
  62.8 2.7 %all-to-all-done.2 = bf16[8,32,512]{2,1,0:T(8,128)(2,1)S(1)} async-done(((bf16[8,32,512]{2,1,0:T(8,128)(2,1)}), bf16[8,32,512]{2,1,0:T(8,128)(2,1)S(1)}, u32[]{:S(2)}, u32[]{:S(2)}) %all-to-all-start.2) | async-done | bytes 262176 | tf_op jit(solution)/shard_map/all_to_all | solution.py:647
  65.5 14.5 %shard_map.472 = (bf16[15,192,192]{2,1,0:T(8,128)(2,1)}, bf16[2880,192]{1,0:T(8,128)(2,1)}, bf16[192,192]{1,0:T(8,128)(2,1)}, bf16[256,192]{1,0:T(8,128)(2,1)}, ...) custom-call(s32[16,192]{1,0:T(8,128)} %copy-done.18, ...), custom_call_target="tpu_custom_call" | custom-call | flops 12079595520 | bytes 6635520 | tf_op jit(solution)/shard_map/pallas_call | solution.py:813
  80.0 3.6 %all-to-all-start.3 = ((bf16[8,32,192]{2,1,0:T(8,128)(2,1)}), bf16[8,32,192]{2,1,0:T(8,128)(2,1)S(1)}, u32[]{:S(2)}, u32[]{:S(2)}) async-start(bf16[8,32,192]{2,1,0:T(8,128)(2,1)} %bitcast.55), calls=%async_computation.3 | async-start | bytes 262144 | tf_op jit(solution)/shard_map/all_to_all | solution.py:647
  83.6 2.7 %shard_map.473 = bf16[4,208,512]{2,1,0:T(8,128)(2,1)} custom-call(bf16[192,512]{1,0:T(8,128)(2,1)} %get-tuple-element.94.sent_ref, bf16[256,512]{1,0:T(8,128)(2,1)} %bitcast.43, bf16[192,192]{1,0:T(8,128)(2,1)} %get-tuple-element.133.own_ref, bf16[256,192]{1,0:T(8,128)(2,1)} %get-tuple-element.135.far_grad_ref, ...), custom_call_target="tpu_custom_call" | custom-call | flops 1000000000 | bytes 1000000 | tf_op jit(solution)/shard_map/pallas_call | solution.py:860
  86.3 4.6 %all-to-all-done.3 = bf16[8,32,192]{2,1,0:T(8,128)(2,1)S(1)} async-done(((bf16[8,32,192]{2,1,0:T(8,128)(2,1)}), bf16[8,32,192]{2,1,0:T(8,128)(2,1)S(1)}, u32[]{:S(2)}, u32[]{:S(2)}) %all-to-all-start.3) | async-done | bytes 98336 | tf_op jit(solution)/shard_map/all_to_all | solution.py:647
  95.3 4.2 %shard_map.475 = (f32[192,128]{1,0:T(8,128)S(1)}, bf16[192,512]{1,0:T(8,128)(2,1)S(1)}, f32[192,512]{1,0:T(8,128)S(1)}, bf16[192,1216]{1,0:T(8,128)(2,1)S(1)}, b...) custom-call(f32[192,128]{1,0:T(8,128)} %get-tuple-element.141.refs_0, ...), custom_call_target="tpu_custom_call" | custom-call | bytes 20922368 | tf_op jit(solution)/shard_map/pallas_call | solution.py:370
  99.7 2.6 %shard_map.476 = (f32[192,512]{1,0:T(8,128)S(1)}, f32[192,512]{1,0:T(8,128)S(1)}, f32[16,512]{1,0:T(8,128)S(1)}, bf16[1152,512]{1,0:T(8,128)(2,1)S(1)}) custom-call(s32[1]{0:T(128)} %bitcast.15.place_ref, bf16[192,384]{1,0:T(8,128)(2,1)S(1)} %add_convert_fusion.13.back_a, bf16[192,384]{1,0:T(8,128)(2,1)S(1)} %collective-permute-done.3.back_b, ...), custom_call_target="tpu_custom_call" | custom-call | tf_op jit(solution)/shard_map/pallas_call | solution.py:878
  103.9 11.7 %shard_map.477 = (f32[15,192,192]{2,1,0:T(8,128)}, bf16[192,512]{1,0:T(8,128)(2,1)S(1)}, bf16[256,512]{1,0:T(8,128)(2,1)}, bf16[192,512]{1,0:T(8,128)(2,1)S(1)},...) custom-call(s32[1]{0:T(128)S(6)} %and.66.core_ref, s32[16,192]{1,0:T(8,128)} %copy-done.18, ...), custom_call_target="tpu_custom_call" | custom-call | flops 12079595520 | bytes 14745600 | tf_op jit(solution)/shard_map/pallas_call | solution.py:900
  127.2 6.3 %collective-permute-done.9 = bf16[2,72,512]{2,1,0:T(8,128)(2,1)S(1)} collective-permute-done((bf16[2,72,512]{2,1,0:T(8,128)(2,1)S(1)}, bf16[2,72,512]{2,1,0:T(8,128)(2,1)S(1)}, u32[]{:S(2)}, u32[]{:S(2)}) %collective-permute-start.9) | collective-permute-done | bytes 147488 | tf_op jit(solution)/shard_map/ppermute | solution.py:552
  133.6 2.4 %collective-permute-done.10 = bf16[448,512]{1,0:T(8,128)(2,1)S(1)} collective-permute-done((bf16[448,512]{1,0:T(8,128)(2,1)S(1)}, bf16[448,512]{1,0:T(8,128)(2,1)S(1)}, u32[]{:S(2)}, u32[]{:S(2)}) %collective-permute-start.10) | collective-permute-done | bytes 458784 | tf_op jit(solution)/shard_map/ppermute | solution.py:552
  141.0 4.0 %all-to-all-start.4 = ((bf16[8,32,512]{2,1,0:T(8,128)(2,1)}), bf16[8,32,512]{2,1,0:T(8,128)(2,1)S(1)}, u32[]{:S(2)}, u32[]{:S(2)}) async-start(bf16[8,32,512]{2,1,0:T(8,128)(2,1)} %bitcast.24), calls=%async_computation.4 | async-start | bytes 524288 | tf_op jit(solution)/shard_map/all_to_all | solution.py:647
  148.6 4.0 %collective-permute-done.17 = bf16[176,512]{1,0:T(8,128)(2,1)} collective-permute-done((bf16[176,512]{1,0:T(8,128)(2,1)S(1)}, bf16[176,512]{1,0:T(8,128)(2,1)}, u32[]{:S(2)}, u32[]{:S(2)}) %collective-permute-start.17) | collective-permute-done | bytes 180256 | tf_op jit(solution)/shard_map/ppermute | solution.py:552
  154.1 5.9 %collective-permute-done.14 = bf16[144,512]{1,0:T(8,128)(2,1)S(1)} collective-permute-done((bf16[144,512]{1,0:T(8,128)(2,1)S(1)}, bf16[144,512]{1,0:T(8,128)(2,1)S(1)}, u32[]{:S(2)}, u32[]{:S(2)}) %collective-permute-start.14) | collective-permute-done | bytes 147488 | tf_op jit(solution)/shard_map/ppermute | solution.py:552
  160.8 2.2 %collective-permute-done.18 = bf16[176,512]{1,0:T(8,128)(2,1)S(1)} collective-permute-done((bf16[176,512]{1,0:T(8,128)(2,1)S(1)}, bf16[176,512]{1,0:T(8,128)(2,1)S(1)}, u32[]{:S(2)}, u32[]{:S(2)}) %collective-permute-start.18) | collective-permute-done | bytes 180256 | tf_op jit(solution)/shard_map/ppermute | solution.py:552
  163.2 2.2 %collective-permute-start.25 = (bf16[176,512]{1,0:T(8,128)(2,1)S(1)}, bf16[176,512]{1,0:T(8,128)(2,1)S(1)}, u32[]{:S(2)}, u32[]{:S(2)}) collective-permute-start(bf16[176,512]{1,0:T(8,128)(2,1)S(1)} %add_convert_fusion.8.p0), channel_id=1, source_target_pairs={{0,4},{4,0},{8,12},{12,8},{16,20},{20,16},{24,28},{28,24},{1,5},{5... | collective-permute-start | bytes 540680 | tf_op jit(solution)/shard_map/ppermute | solution.py:552
  172.3 3.3 %collective-permute-done.26.p3 = bf16[176,512]{1,0:T(8,128)(2,1)S(1)} collective-permute-done((bf16[176,512]{1,0:T(8,128)(2,1)S(1)}, bf16[176,512]{1,0:T(8,128)(2,1)S(1)}, u32[]{:S(2)}, u32[]{:S(2)}) %collective-permute-start.26) | collective-permute-done | bytes 180256 | tf_op jit(solution)/shard_map/ppermute | solution.py:552
  (128 shorter events, 45.7 us)
Async XLA Ops:
  41.2 8.1 %collective-permute-start.1 = (bf16[192,640]{1,0:T(8,128)(2,1)S(1)}, bf16[192,640]{1,0:T(8,128)(2,1)S(1)}, u32[]{:S(2)}, u32[]{:S(2)}) collective-permute-start(bf16[192,640]{1,0:T(8,128)(2,1)S(1)} %add_convert_fusion.5.sum_a), channel_id=1, source_target_pairs={{0,2},{1,3},{2,0},{3,1},{4,6},{5,7},{6,4},{7,5},{8,10},{9,11},{10,... | collective-permute-start | bytes 737288 | tf_op jit(solution)/shard_map/ppermute | solution.py:552
  53.4 12.1 %all-to-all-start.2 = ((bf16[8,32,512]{2,1,0:T(8,128)(2,1)}), bf16[8,32,512]{2,1,0:T(8,128)(2,1)S(1)}, u32[]{:S(2)}, u32[]{:S(2)}) async-start(bf16[8,32,512]{2,1,0:T(8,128)(2,1)} %bitcast.9), calls=%async_computation.2 | async-start | bytes 524288 | tf_op jit(solution)/shard_map/all_to_all | solution.py:647
  80.0 10.9 %all-to-all-start.3 = ((bf16[8,32,192]{2,1,0:T(8,128)(2,1)}), bf16[8,32,192]{2,1,0:T(8,128)(2,1)S(1)}, u32[]{:S(2)}, u32[]{:S(2)}) async-start(bf16[8,32,192]{2,1,0:T(8,128)(2,1)} %bitcast.55), calls=%async_computation.3 | async-start | bytes 262144 | tf_op jit(solution)/shard_map/all_to_all | solution.py:647
  102.4 13.2 %collective-permute-start.4 = (bf16[288,512]{1,0:T(8,128)(2,1)S(1)}, bf16[288,512]{1,0:T(8,128)(2,1)S(1)}, u32[]{:S(2)}, u32[]{:S(2)}) collective-permute-start(bf16[288,512]{1,0:T(8,128)(2,1)S(1)} %get-tuple-element.215), channel_id=1, source_target_pairs={{0,4},{4,0},{8,12},{12,8},{16,20},{20,16},{24,28},{28,24},{1,5},{5... | collective-permute-start | bytes 884744 | tf_op jit(solution)/shard_map/ppermute | solution.py:552
  102.7 13.0 %collective-permute-start.5 = (bf16[288,512]{1,0:T(8,128)(2,1)S(1)}, bf16[288,512]{1,0:T(8,128)(2,1)S(1)}, u32[]{:S(2)}, u32[]{:S(2)}) collective-permute-start(bf16[288,512]{1,0:T(8,128)(2,1)S(1)} %get-tuple-element.214), channel_id=1, source_target_pairs={{0,8},{4,12},{8,0},{12,4},{16,24},{20,28},{24,16},{28,20},{1,9},{5... | collective-permute-start | bytes 884744 | tf_op jit(solution)/shard_map/ppermute | solution.py:552
  103.8 15.5 %collective-permute-start.11 = (bf16[416,512]{1,0:T(8,128)(2,1)S(1)}, bf16[416,512]{1,0:T(8,128)(2,1)S(1)}, u32[]{:S(2)}, u32[]{:S(2)}) collective-permute-start(bf16[416,512]{1,0:T(8,128)(2,1)S(1)} %constant_dynamic-slice_fusion.4), channel_id=1, source_target_pairs={{0,1},{1,0},{2,3},{3,2},{4,5},{5,4},{6,7},{7,6},{8,9},{9,8},{10,11... | collective-permute-start | bytes 1277960 | tf_op jit(solution)/shard_map/ppermute | solution.py:552
  115.6 7.5 %collective-permute-start.8 = (bf16[2,448,512]{2,1,0:T(8,128)(2,1)S(1)}, bf16[2,448,512]{2,1,0:T(8,128)(2,1)S(1)}, u32[]{:S(2)}, u32[]{:S(2)}) collective-permute-start(bf16[2,448,512]{2,1,0:T(8,128)(2,1)S(1)} %get-tuple-element.179), channel_id=1, source_target_pairs={{0,1},{1,0},{2,3},{3,2},{4,5},{5,4},{6,7},{7,6},{8,9},{9,8},{10,11... | collective-permute-start | bytes 2752520 | tf_op jit(solution)/shard_map/ppermute | solution.py:552
  119.4 7.7 %collective-permute-start.12 = (bf16[208,512]{1,0:T(8,128)(2,1)S(1)}, bf16[208,512]{1,0:T(8,128)(2,1)S(1)}, u32[]{:S(2)}, u32[]{:S(2)}) collective-permute-start(bf16[208,512]{1,0:T(8,128)(2,1)S(1)} %constant_dynamic-slice_fusion.3), channel_id=1, source_target_pairs={{0,2},{1,3},{2,0},{3,1},{4,6},{5,7},{6,4},{7,5},{8,10},{9,11},{10,... | collective-permute-start | bytes 638984 | tf_op jit(solution)/shard_map/ppermute | solution.py:552
  123.5 12.5 %collective-permute-start.10 = (bf16[448,512]{1,0:T(8,128)(2,1)S(1)}, bf16[448,512]{1,0:T(8,128)(2,1)S(1)}, u32[]{:S(2)}, u32[]{:S(2)}) collective-permute-start(bf16[448,512]{1,0:T(8,128)(2,1)S(1)} %constant_dynamic-slice_fusion.5), channel_id=1, source_target_pairs={{0,2},{1,3},{2,0},{3,1},{4,6},{5,7},{6,4},{7,5},{8,10},{9,11},{10,... | collective-permute-start | bytes 1376264 | tf_op jit(solution)/shard_map/ppermute | solution.py:552
  125.0 8.6 %collective-permute-start.9 = (bf16[2,72,512]{2,1,0:T(8,128)(2,1)S(1)}, bf16[2,72,512]{2,1,0:T(8,128)(2,1)S(1)}, u32[]{:S(2)}, u32[]{:S(2)}) collective-permute-start(bf16[2,72,512]{2,1,0:T(8,128)(2,1)S(1)} %constant_dynamic-slice_fusion.6), channel_id=1, source_target_pairs={{0,16},{4,20},{8,24},{12,28},{16,0},{20,4},{24,8},{28,12},{1,17},{... | collective-permute-start | bytes 442376 | tf_op jit(solution)/shard_map/ppermute | solution.py:552
  136.3 8.6 %collective-permute-start.13 = (bf16[2,72,512]{2,1,0:T(8,128)(2,1)S(1)}, bf16[2,72,512]{2,1,0:T(8,128)(2,1)S(1)}, u32[]{:S(2)}, u32[]{:S(2)}) collective-permute-start(bf16[2,72,512]{2,1,0:T(8,128)(2,1)S(1)} %add_convert_fusion.10), channel_id=1, source_target_pairs={{0,16},{4,20},{8,24},{12,28},{16,0},{20,4},{24,8},{28,12},{1,17},{... | collective-permute-start | bytes 442376 | tf_op jit(solution)/shard_map/ppermute | solution.py:552
  137.5 11.2 %collective-permute-start.15 = (bf16[176,512]{1,0:T(8,128)(2,1)}, bf16[176,512]{1,0:T(8,128)(2,1)}, u32[]{:S(2)}, u32[]{:S(2)}) collective-permute-start(bf16[176,512]{1,0:T(8,128)(2,1)} %get-tuple-element.216), channel_id=1, source_target_pairs={{0,8},{4,12},{8,0},{12,4},{16,24},{20,28},{24,16},{28,20},{1,9},{5... | collective-permute-start | bytes 540680 | tf_op jit(solution)/shard_map/ppermute | solution.py:552
  138.2 10.4 %collective-permute-start.16 = (bf16[176,512]{1,0:T(8,128)(2,1)S(1)}, bf16[176,512]{1,0:T(8,128)(2,1)}, u32[]{:S(2)}, u32[]{:S(2)}) collective-permute-start(bf16[176,512]{1,0:T(8,128)(2,1)S(1)} %get-tuple-element.218), channel_id=1, source_target_pairs={{0,4},{4,0},{8,12},{12,8},{16,20},{20,16},{24,28},{28,24},{1,5},{5... | collective-permute-start | bytes 540680 | tf_op jit(solution)/shard_map/ppermute | solution.py:552
  139.3 13.3 %collective-permute-start.17 = (bf16[176,512]{1,0:T(8,128)(2,1)S(1)}, bf16[176,512]{1,0:T(8,128)(2,1)}, u32[]{:S(2)}, u32[]{:S(2)}) collective-permute-start(bf16[176,512]{1,0:T(8,128)(2,1)S(1)} %get-tuple-element.217), channel_id=1, source_target_pairs={{0,12},{4,8},{8,4},{12,0},{16,28},{20,24},{24,20},{28,16},{1,13},{... | collective-permute-start | bytes 540680 | tf_op jit(solution)/shard_map/ppermute | solution.py:552
  141.0 19.1 %all-to-all-start.4 = ((bf16[8,32,512]{2,1,0:T(8,128)(2,1)}), bf16[8,32,512]{2,1,0:T(8,128)(2,1)S(1)}, u32[]{:S(2)}, u32[]{:S(2)}) async-start(bf16[8,32,512]{2,1,0:T(8,128)(2,1)} %bitcast.24), calls=%async_computation.4 | async-start | bytes 524288 | tf_op jit(solution)/shard_map/all_to_all | solution.py:647
  145.1 8.9 %collective-permute-start.20 = (bf16[144,512]{1,0:T(8,128)(2,1)S(1)}, bf16[144,512]{1,0:T(8,128)(2,1)S(1)}, u32[]{:S(2)}, u32[]{:S(2)}) collective-permute-start(bf16[144,512]{1,0:T(8,128)(2,1)S(1)} %get-tuple-element.219), channel_id=1, source_target_pairs={{0,4},{4,0},{8,12},{12,8},{16,20},{20,16},{24,28},{28,24},{1,5},{5... | collective-permute-start | bytes 442376 | tf_op jit(solution)/shard_map/ppermute | solution.py:552
  147.2 12.8 %collective-permute-start.14 = (bf16[144,512]{1,0:T(8,128)(2,1)S(1)}, bf16[144,512]{1,0:T(8,128)(2,1)S(1)}, u32[]{:S(2)}, u32[]{:S(2)}) collective-permute-start(bf16[144,512]{1,0:T(8,128)(2,1)S(1)} %get-tuple-element.220), channel_id=1, source_target_pairs={{0,8},{4,12},{8,0},{12,4},{16,24},{20,28},{24,16},{28,20},{1,9},{5... | collective-permute-start | bytes 442376 | tf_op jit(solution)/shard_map/ppermute | solution.py:552
  153.9 9.1 %collective-permute-start.18 = (bf16[176,512]{1,0:T(8,128)(2,1)S(1)}, bf16[176,512]{1,0:T(8,128)(2,1)S(1)}, u32[]{:S(2)}, u32[]{:S(2)}) collective-permute-start(bf16[176,512]{1,0:T(8,128)(2,1)S(1)} %add_convert_fusion.9), channel_id=1, source_target_pairs={{0,16},{4,20},{8,24},{12,28},{16,0},{20,4},{24,8},{28,12},{1,17},{... | collective-permute-start | bytes 540680 | tf_op jit(solution)/shard_map/ppermute | solution.py:552
  163.1 7.6 %collective-permute-start.24 = (bf16[176,512]{1,0:T(8,128)(2,1)S(1)}, bf16[176,512]{1,0:T(8,128)(2,1)S(1)}, u32[]{:S(2)}, u32[]{:S(2)}) collective-permute-start(bf16[176,512]{1,0:T(8,128)(2,1)S(1)} %add_convert_fusion.8.p0), channel_id=1, source_target_pairs={{0,8},{4,12},{8,0},{12,4},{16,24},{20,28},{24,16},{28,20},{1,9},{5... | collective-permute-start | bytes 540680 | tf_op jit(solution)/shard_map/ppermute | solution.py:552
  163.2 9.1 %collective-permute-start.25 = (bf16[176,512]{1,0:T(8,128)(2,1)S(1)}, bf16[176,512]{1,0:T(8,128)(2,1)S(1)}, u32[]{:S(2)}, u32[]{:S(2)}) collective-permute-start(bf16[176,512]{1,0:T(8,128)(2,1)S(1)} %add_convert_fusion.8.p0), channel_id=1, source_target_pairs={{0,4},{4,0},{8,12},{12,8},{16,20},{20,16},{24,28},{28,24},{1,5},{5... | collective-permute-start | bytes 540680 | tf_op jit(solution)/shard_map/ppermute | solution.py:552
  165.4 10.2 %collective-permute-start.26 = (bf16[176,512]{1,0:T(8,128)(2,1)S(1)}, bf16[176,512]{1,0:T(8,128)(2,1)S(1)}, u32[]{:S(2)}, u32[]{:S(2)}) collective-permute-start(bf16[176,512]{1,0:T(8,128)(2,1)S(1)} %add_convert_fusion.8.p0), channel_id=1, source_target_pairs={{0,12},{4,8},{8,4},{12,0},{16,28},{20,24},{24,20},{28,16},{1,13},{... | collective-permute-start | bytes 540680 | tf_op jit(solution)/shard_map/ppermute | solution.py:552
  166.8 11.3 %collective-permute-start.21 = (bf16[288,512]{1,0:T(8,128)(2,1)S(1)}, bf16[288,512]{1,0:T(8,128)(2,1)S(1)}, u32[]{:S(2)}, u32[]{:S(2)}) collective-permute-start(bf16[288,512]{1,0:T(8,128)(2,1)S(1)} %maximum_select_fusion.2.b0), channel_id=1, source_target_pairs={{0,8},{4,12},{8,0},{12,4},{16,24},{20,28},{24,16},{28,20},{1,9},{5... | collective-permute-start | bytes 884744 | tf_op jit(solution)/shard_map/ppermute | solution.py:552
  167.4 11.2 %collective-permute-start.19 = (bf16[288,512]{1,0:T(8,128)(2,1)S(1)}, bf16[288,512]{1,0:T(8,128)(2,1)S(1)}, u32[]{:S(2)}, u32[]{:S(2)}) collective-permute-start(bf16[288,512]{1,0:T(8,128)(2,1)S(1)} %maximum_select_fusion.1.a0), channel_id=1, source_target_pairs={{0,4},{4,0},{8,12},{12,8},{16,20},{20,16},{24,28},{28,24},{1,5},{5... | collective-permute-start | bytes 884744 | tf_op jit(solution)/shard_map/ppermute | solution.py:552
  170.7 7.9 %collective-permute-start.23 = (bf16[192,512]{1,0:T(8,128)(2,1)S(1)}, bf16[192,512]{1,0:T(8,128)(2,1)S(1)}, u32[]{:S(2)}, u32[]{:S(2)}) collective-permute-start(bf16[192,512]{1,0:T(8,128)(2,1)S(1)} %add_convert_fusion.7.back_a), channel_id=1, source_target_pairs={{0,2},{1,3},{2,0},{3,1},{4,6},{5,7},{6,4},{7,5},{8,10},{9,11},{10,... | collective-permute-start | bytes 589832 | tf_op jit(solution)/shard_map/ppermute | solution.py:552
  (27 other events, 211.5 us)
